TPU v7x, 256 devices: a whole 4x4x8 slice. The times are simulated.
256 devices in a mesh: dp: 4 (over x_lo, core), mp: 64 (over y, z, x_hi).
Axes of the slice: x: 4 (x_hi: 2, x_lo: 2; x = x_hi * 2 + x_lo), y: 4, z: 8, core: 2. Of those that a mesh axis runs over, the one named last changes fastest.
Arguments:
- tokens: bfloat16 [65536, 4608], P('mp', 'dp'), may hold values from -6 to 6
- kv_weight: bfloat16 [2, 4608, 1024], P(None, 'dp', 'mp'), may hold values from -0.25 to 0.25
- d_kv: bfloat16 [65536, 2, 1024], P('mp', None, 'dp'), may hold values from -16 to 16
Outputs:
- kv_out: bfloat16 [65536, 2, 1024], P('mp', None, 'dp')
- d_tokens: bfloat16 [65536, 4608], P('mp', 'dp')
- grad_kv: float32 [2, 4608, 1024], P(None, 'dp', 'mp')
All inputs are finite; a program needn't handle non-finite values.
Results may differ from a plain program's by a relative error of at most 0.001.
Values may be sent and summed in bfloat16 or wider, within the bound.
No kernel may reach another device: no remote copies, remote signals or barrier semaphores. Data moves between devices by JAX's collectives and lax.ppermute only.
A program may use at most 128 MiB of HBM per device.

v0:
```python
import jax
import jax.numpy as jnp
from jax import lax
from jax.sharding import PartitionSpec as P


def per_device(tokens, kv_weight, d_kv):
    panels = lax.all_gather(kv_weight, "mp", axis=2, tiled=True)
    partial_value = jnp.einsum("td,kdc->tkc", tokens, panels, preferred_element_type=jnp.float32)
    kv_out = lax.psum_scatter(partial_value, "dp", scatter_dimension=2, tiled=True).astype(
        jnp.bfloat16
    )
    cotangent = lax.all_gather(d_kv, "dp", axis=2, tiled=True)
    d_tokens = jnp.einsum(
        "tkc,kdc->td", cotangent, panels, preferred_element_type=jnp.float32
    ).astype(jnp.bfloat16)
    partial_grad = jnp.einsum("td,tkc->ckd", tokens, cotangent, preferred_element_type=jnp.float32)
    owned_share = lax.psum_scatter(partial_grad, "mp", scatter_dimension=0, tiled=True)
    grad_kv = jnp.transpose(owned_share, (1, 2, 0))
    return (kv_out, d_tokens, grad_kv)


def solution(mesh):
    placed = (P("mp", "dp"), P(None, "dp", "mp"), P("mp", None, "dp"))
    return jax.shard_map(
        per_device,
        mesh=mesh,
        in_specs=placed,
        out_specs=(P("mp", None, "dp"), P("mp", "dp"), P(None, "dp", "mp")),
        check_vma=False,
    )
```

profile of v0, /device:TPU:1, one launch (start us, length us, event | category | flops | bytes accessed | tf_op | source)
XLA Modules:
  0.0 1118.4 jit_solution(502643453600094065)
XLA Ops:
  7.2 0.0 copy-start
  7.2 0.0 all-gather.3.cloned.1.call-start
  7.2 0.7 all-gather.3.cloned.1.call-update
  7.9 0.0 all-gather.5.cloned.1.call-start
  8.0 2.3 copy.6
  10.3 0.0 all-gather.5.cloned.1.call-update
  10.3 0.0 reduce-scatter.3.cloned.1.call-start
  10.4 132.5 %all-gather.3.cloned.1.call-done = bf16[2,1152,1024]{1,2,0:T(8,128)(2,1)} async-done(((bf16[2,1152,16]{1,2,0:T(8,128)(2,1)}), bf16[2,1152,1024]{1,2,0:T(8,128)(2,1)}) %all-gather.3.cloned.1.call-update) | async-done | bytes 4718608 | tf_op jit(solution)/shard_map/all_gather | solution.py:8
  142.8 0.0 copy-done
  142.8 10.2 fusion.1
  153.0 0.0 reduce-scatter.3.cloned.1.call-update
  153.0 0.0 reduce-scatter.5.cloned.1.call-start
  153.1 41.4 %all-gather.5.cloned.1.call-done = bf16[1024,2,1024]{2,0,1:T(8,128)(2,1)} async-done(((bf16[1024,2,256]{2,0,1:T(8,128)(2,1)}), bf16[1024,2,1024]{2,0,1:T(8,128)(2,1)}) %all-gather.5.cloned.1.call-update) | async-done | bytes 4194320 | tf_op jit(solution)/shard_map/all_gather | solution.py:13
  194.5 9.6 convolution_bitcast_fusion
  204.2 0.0 reduce-scatter.5.cloned.1.call-update
  204.2 9.8 bitcast_convert_fusion
  214.0 65.6 %reduce-scatter.3.cloned.1.call-done = f32[1024,2,256]{2,0,1:T(8,128)} async-done(((f32[1024,2,1024]{2,0,1:T(8,128)}), f32[1024,2,256]{2,0,1:T(8,128)}) %reduce-scatter.3.cloned.1.call-update) | async-done | bytes 2097168 | tf_op jit(solution)/shard_map/reduce_scatter | solution.py:10
  279.5 1.7 convert_element_type.6
  281.2 2.0 copy.8
  283.3 828.6 %reduce-scatter.5.cloned.1.call-done = f32[16,2,1152]{2,0,1:T(8,128)} async-done(((f32[1024,2,1152]{2,0,1:T(8,128)}), f32[16,2,1152]{2,0,1:T(8,128)}) %reduce-scatter.5.cloned.1.call-update) | async-done | bytes 147472 | tf_op jit(solution)/shard_map/reduce_scatter | solution.py:18
Async XLA Ops:
  7.2 135.7 %copy-start = (bf16[1024,1152]{1,0:T(8,128)(2,1)S(1)}, bf16[1024,1152]{1,0:T(8,128)(2,1)}, u32[]{:S(2)}) copy-start(bf16[1024,1152]{1,0:T(8,128)(2,1)} %param.3) | copy-start | bytes 7077892
  7.2 135.7 %all-gather.3.cloned.1.call-start = ((), (), s32[]{:S(2)}) async-start(), calls=%async_computation.2 | async-start | bytes 4792320 | tf_op jit(solution)/shard_map/all_gather | solution.py:8
  7.9 186.6 %all-gather.5.cloned.1.call-start = ((), (), s32[]{:S(2)}) async-start(), calls=%async_computation.4 | async-start | bytes 5242880 | tf_op jit(solution)/shard_map/all_gather | solution.py:13
  10.3 269.2 %reduce-scatter.3.cloned.1.call-start = ((), (), s32[]{:S(2)}) async-start(), calls=%async_computation.3 | async-start | bytes 10485760 | tf_op jit(solution)/shard_map/reduce_scatter | solution.py:10
  153.0 958.8 %reduce-scatter.5.cloned.1.call-start = ((), (), s32[]{:S(2)}) async-start(), calls=%async_computation.5 | async-start | bytes 9584640 | tf_op jit(solution)/shard_map/reduce_scatter | solution.py:18
Sparse Core Ops, SparseCore 0:
  11.6 131.1 all-gather.2
  145.2 49.2 all-gather.4
  197.1 82.3 reduce-scatter.2
  285.8 826.0 reduce-scatter.4
where the time goes:
time: 1120 us
  waiting for transfers between devices  1070 us (96%)
  matrix products  29.6 us (3%)
  between operations  13.8 us (1%)
    reduce_scatter x1, waiting for transfers between devices, per_device(): lax.psum_scatter(partial_grad, 'mp', scatter_dimension=0, tiled=True)  829 us
    all_gather x1, waiting for transfers between devices, per_device(): panels = lax.all_gather(kv_weight, 'mp', axis=2, tiled=True)  132 us
    reduce_scatter x1, waiting for transfers between devices, per_device(): lax.psum_scatter(partial_value, 'dp', scatter_dimension=2, tiled=True)  65.6 us
    all_gather x1, waiting for transfers between devices, per_device(): cotangent = lax.all_gather(d_kv, 'dp', axis=2, tiled=True)  41.4 us
  transfers between devices with their start and end apart: 4, of which 4 were waited for; matrix products, arithmetic and copies ran while one was open for 3% of the time, Pallas kernels for 0%

commit v1 on v0

v1 whole, which is shorter than its diff:
```python
import jax
import jax.numpy as jnp
from jax import lax
from jax.sharding import Mesh, PartitionSpec as P

MP = ("y", "z", "xh")
DP = ("xl", "core")


def per_device(tokens, kv_weight, d_kv):
    panels = kv_weight
    for axis in ("xh", "z", "y"):
        panels = lax.all_gather(panels, axis, axis=2, tiled=True)
    partial_value = jnp.einsum("td,kdc->tkc", tokens, panels, preferred_element_type=jnp.float32)
    kv_out = lax.psum_scatter(partial_value, DP, scatter_dimension=2, tiled=True).astype(
        jnp.bfloat16
    )
    cotangent = lax.all_gather(d_kv, DP, axis=2, tiled=True)
    d_tokens = jnp.einsum(
        "tkc,kdc->td", cotangent, panels, preferred_element_type=jnp.float32
    ).astype(jnp.bfloat16)
    share = jnp.einsum("td,tkc->ckd", tokens, cotangent, preferred_element_type=jnp.float32)
    share = share.reshape(4, 8, 2, 16, 2, 1152)
    share = lax.psum_scatter(share, "z", scatter_dimension=1, tiled=True)
    share = lax.psum_scatter(share, "y", scatter_dimension=0, tiled=True)
    share = lax.psum_scatter(share, "xh", scatter_dimension=2, tiled=True)
    grad_kv = jnp.transpose(share.reshape(16, 2, 1152), (1, 2, 0))
    return (kv_out, d_tokens, grad_kv)


def solution(mesh):
    fine = Mesh(mesh.devices.reshape(2, 2, 4, 8, 2), DP + MP)
    return jax.shard_map(
        per_device,
        mesh=fine,
        in_specs=(P(MP, DP), P(None, DP, MP), P(MP, None, DP)),
        out_specs=(P(MP, None, DP), P(MP, DP), P(None, DP, MP)),
        check_vma=False,
    )
```

time: 1120 us -> 517 us (0.46)
  waiting for transfers between devices: 1070 us -> 449 us
  local copies, waits for them, and re-layouts: 4.39 us -> 18.3 us
    reduce_scatter x2 -> x3, waiting for transfers between devices: 894 us -> 114 us  [the longest x1 75.3 us: per_device(): lax.psum_scatter(partial_value, DP, scatter_dimension=2, tiled=True)]
    unnamed x4 -> x8, waiting for transfers between devices: 0.73 us -> 208 us
    all_gather x2 -> x3, waiting for transfers between devices: 174 us -> 128 us  [the longest x2 80.8 us: per_device(): panels = lax.all_gather(panels, axis, axis=2, tiled=True)]
  transfers between devices with their start and end apart: 4 -> 7, of which waited for: 4 -> 7; matrix products, arithmetic and copies ran while one was open for 3% -> 9% of each run, Pallas kernels for 0% -> 0%
where the time goes in v1:
time: 517 us
  waiting for transfers between devices  449 us (87%)
  matrix products  27.4 us (5%)
  local copies, waits for them, and re-layouts  18.3 us (4%)
  between operations  14.2 us (3%)
  blocking collectives  6.07 us (1%)
    unnamed x8, waiting for transfers between devices  208 us
    all_gather x2, waiting for transfers between devices, per_device(): panels = lax.all_gather(panels, axis, axis=2, tiled=True)  80.8 us
    reduce_scatter x1, waiting for transfers between devices, per_device(): lax.psum_scatter(partial_value, DP, scatter_dimension=2, tiled=True)  75.3 us
    all_gather x1, waiting for transfers between devices, per_device(): cotangent = lax.all_gather(d_kv, DP, axis=2, tiled=True)  46.7 us
    reduce_scatter x1, waiting for transfers between devices, per_device(): share = lax.psum_scatter(share, 'y', scatter_dimension=0, tiled=True)  19.5 us
    reduce_scatter x1, waiting for transfers between devices, per_device(): share = lax.psum_scatter(share, 'xh', scatter_dimension=2, tiled=True)  18.7 us
  transfers between devices with their start and end apart: 7, of which 7 were waited for; matrix products, arithmetic and copies ran while one was open for 9% of the time, Pallas kernels for 0%

profile of v1, /device:TPU:1, one launch (start us, length us, event | category | flops | bytes accessed | tf_op | source)
XLA Modules:
  0.0 516.9 jit_solution(587155650411539414)
XLA Ops:
  7.2 0.0 copy-start
  7.2 0.0 all-gather.8.cloned.1.call-start
  7.2 2.5 copy.13
  9.7 0.0 all-gather.8.cloned.1.call-update
  9.7 0.0 all-gather.4.cloned.1.call-start
  9.8 0.9 copy.11
  10.7 6.1 %all_gather.12 = bf16[2,1152,32]{1,0,2:T(2,128)(2,1)} all-gather(bf16[2,1152,16]{1,0,2:T(2,128)(2,1)S(1)} %copy.11), channel_id=1, replica_groups=mesh['xl'=2,'core'=2,'y'=4,'z'=8,'xh'=2] {'xh'}, dimensions={2}, use_global_device_ids=true | all-gather | bytes 221184 | tf_op jit(solution)/shard_map/all_gather | solution.py:13
  16.8 0.0 all-gather.4.cloned.1.call-update
  16.8 0.0 all-reduce.3.cloned.1.call-start
  16.9 46.7 %all-gather.8.cloned.1.call-done = bf16[1024,2,1024]{2,0,1:T(8,128)(2,1)} async-done(((bf16[1024,2,256]{2,0,1:T(8,128)(2,1)}), bf16[1024,2,1024]{2,0,1:T(8,128)(2,1)}) %all-gather.8.cloned.1.call-update) | async-done | bytes 4194320 | tf_op jit(solution)/shard_map/all_gather | solution.py:18
  63.6 0.0 copy-done
  63.6 7.5 %fusion = f32[2,1024,1152]{2,1,0:T(8,128)S(1)} fusion(bf16[1024,2,1024]{2,0,1:T(8,128)(2,1)} %all-gather.8.cloned.1.call-done, bf16[1024,1152]{1,0:T(8,128)(2,1)S(1)} %copy-done), kind=kOutput, calls=%fused_computation.1 | convolution fusion | flops 4831838208 | bytes 15990784 | tf_op jit(solution)/shard_map/td,tkc->ckd/dot_general | solution.py:22
  71.1 5.0 copy.15
  76.1 0.0 copy-start.1
  76.1 0.0 all-reduce.3.cloned.1.call-update
  76.1 0.0 all-gather.6.cloned.1.call-start
  76.2 24.8 %all-gather.4.cloned.1.call-done = bf16[2,1152,256]{1,0,2:T(2,128)(2,1)} async-done(((bf16[2,1152,32]{1,0,2:T(2,128)(2,1)}), bf16[2,1152,256]{1,0,2:T(2,128)(2,1)}) %all-gather.4.cloned.1.call-update) | async-done | bytes 1179664 | tf_op jit(solution)/shard_map/all_gather | solution.py:13
  101.0 4.2 copy.12
  105.1 0.0 all-gather.6.cloned.1.call-update
  105.2 0.0 reduce-scatter.9.cloned.1.call-start
  105.2 0.0 copy-done.1
  105.2 0.6 dynamic-slice
  105.8 207.8 %all-reduce.3.cloned.1.call-done = f32[4,8,2,16,2,1152]{5,3,4,2,1,0:T(8,128)} async-done(((f32[4,8,2,16,2,1152]{5,3,4,2,1,0:T(8,128)}), f32[4,8,2,16,2,1152]{5,3,4,2,1,0:T(8,128)}) %all-reduce.3.cloned.1.call-update) | async-done | bytes 9437200
  313.6 3.0 constant_dynamic-slice_fusion
  316.6 0.0 reduce-scatter.9.cloned.1.call-update
  316.6 0.0 reduce-scatter.7.cloned.1.call-start
  316.7 56.1 %all-gather.6.cloned.1.call-done = bf16[2,1152,1024]{2,1,0:T(8,128)(2,1)} async-done(((bf16[2,1152,256]{2,1,0:T(8,128)(2,1)}), bf16[2,1152,1024]{2,1,0:T(8,128)(2,1)}) %all-gather.6.cloned.1.call-update) | async-done | bytes 4718608 | tf_op jit(solution)/shard_map/all_gather | solution.py:13
  372.7 10.1 %fusion.2 = f32[1024,2,1024]{2,0,1:T(8,128)} fusion(bf16[2,1152,1024]{2,1,0:T(8,128)(2,1)} %all-gather.6.cloned.1.call-done, bf16[1024,1152]{1,0:T(8,128)(2,1)S(1)} %copy-done), kind=kOutput, calls=%fused_computation.3 | convolution fusion | flops 4831838208 | bytes 15466496 | tf_op jit(solution)/shard_map/td,kdc->tkc/dot_general | solution.py:14
  382.8 0.0 reduce-scatter.7.cloned.1.call-update
  382.8 0.0 reduce-scatter.11.cloned.1.call-start
  382.9 19.5 %reduce-scatter.9.cloned.1.call-done = f32[1,1,2,16,2,1152]{5,3,4,2,1,0:T(8,128)} async-done(((f32[4,1,2,16,2,1152]{5,3,4,2,1,0:T(8,128)}), f32[1,1,2,16,2,1152]{5,3,4,2,1,0:T(8,128)}) %reduce-scatter.9.cloned.1.call-update) | async-done | bytes 294928 | tf_op jit(solution)/shard_map/reduce_scatter | solution.py:25
  402.4 0.0 reduce-scatter.11.cloned.1.call-update
  402.4 9.9 %bitcast_convert_fusion = bf16[1024,1152]{1,0:T(8,128)(2,1)} fusion(bf16[1024,2,1024]{2,0,1:T(8,128)(2,1)} %all-gather.8.cloned.1.call-done, bf16[2,1152,1024]{2,1,0:T(8,128)(2,1)} %all-gather.6.cloned.1.call-done), kind=kOutput, calls=%fused_computation | convolution fusion | flops 4833017856 | bytes 11272192 | tf_op jit(solution)/shard_map/tkc,kdc->td/dot_general | solution.py:19
  412.3 75.3 %reduce-scatter.7.cloned.1.call-done = f32[1024,2,256]{2,0,1:T(8,128)} async-done(((f32[1024,2,1024]{2,0,1:T(8,128)}), f32[1024,2,256]{2,0,1:T(8,128)}) %reduce-scatter.7.cloned.1.call-update) | async-done | bytes 2097168 | tf_op jit(solution)/shard_map/reduce_scatter | solution.py:15
  487.6 1.7 convert_element_type.6
  489.3 2.0 copy.16
  491.4 18.7 %reduce-scatter.11.cloned.1.call-done = f32[1,1,1,16,2,1152]{5,3,4,2,1,0:T(8,128)} async-done(((f32[1,1,2,16,2,1152]{5,3,4,2,1,0:T(8,128)}), f32[1,1,1,16,2,1152]{5,3,4,2,1,0:T(8,128)}) %reduce-scatter.11.cloned.1.call-update) | async-done | bytes 147472 | tf_op jit(solution)/shard_map/reduce_scatter | solution.py:26
Async XLA Ops:
  7.2 56.5 %copy-start = (bf16[1024,1152]{1,0:T(8,128)(2,1)S(1)}, bf16[1024,1152]{1,0:T(8,128)(2,1)}, u32[]{:S(2)}) copy-start(bf16[1024,1152]{1,0:T(8,128)(2,1)} %param.3) | copy-start | bytes 7077892
  7.2 56.4 %all-gather.8.cloned.1.call-start = ((), (), s32[]{:S(2)}) async-start(), calls=%async_computation.6 | async-start | bytes 5242880 | tf_op jit(solution)/shard_map/all_gather | solution.py:18
  9.7 91.2 %all-gather.4.cloned.1.call-start = ((), (), s32[]{:S(2)}) async-start(), calls=%async_computation.3 | async-start | bytes 1327104 | tf_op jit(solution)/shard_map/all_gather | solution.py:13
  16.8 296.7 %all-reduce.3.cloned.1.call-start = ((), (), s32[]{:S(2)}) async-start(), calls=%async_computation.9 | async-start | bytes 18874368
  76.1 29.1 %copy-start.1 = (u32[256]{0:T(256)S(1)}, u32[256]{0:T(256)}, u32[]{:S(2)}) copy-start(u32[256]{0:T(256)} %constant.3) | copy-start | bytes 3076
  76.1 296.6 %all-gather.6.cloned.1.call-start = ((), (), s32[]{:S(2)}) async-start(), calls=%async_computation.4 | async-start | bytes 5898240 | tf_op jit(solution)/shard_map/all_gather | solution.py:13
  105.2 297.2 %reduce-scatter.9.cloned.1.call-start = ((), (), s32[]{:S(2)}) async-start(), calls=%async_computation.7 | async-start | bytes 1474560 | tf_op jit(solution)/shard_map/reduce_scatter | solution.py:25
  316.6 171.0 %reduce-scatter.7.cloned.1.call-start = ((), (), s32[]{:S(2)}) async-start(), calls=%async_computation.5 | async-start | bytes 10485760 | tf_op jit(solution)/shard_map/reduce_scatter | solution.py:15
  382.8 127.2 %reduce-scatter.11.cloned.1.call-start = ((), (), s32[]{:S(2)}) async-start(), calls=%async_computation.8 | async-start | bytes 442368 | tf_op jit(solution)/shard_map/reduce_scatter | solution.py:26
Sparse Core Ops, SparseCore 0:
  10.4 53.1 all-gather.7
  65.4 35.5 all-gather.3
  103.3 210.1 all-reduce.2
  315.8 56.9 all-gather.5
  375.2 27.1 reduce-scatter.8
  404.9 82.7 reduce-scatter.6
  490.7 19.3 reduce-scatter.10

commit v2 on v1

v2 whole, which is shorter than its diff:
```python
import functools

import jax
import jax.numpy as jnp
from jax import lax
from jax.experimental import pallas as pl
from jax.experimental.pallas import tpu as pltpu
from jax.sharding import Mesh, PartitionSpec as P

MP = ("y", "z", "xh")
DP = ("xl", "core")
F32 = jnp.float32
BF16 = jnp.bfloat16
SMEM = pl.BlockSpec(memory_space=pltpu.SMEM)
COST = pl.CostEstimate(flops=1, bytes_accessed=1, transcendentals=0)
VMEM = pl.BlockSpec(memory_space=pltpu.VMEM)


def flip(x, axis, bits):
    n = lax.axis_size(axis)
    return lax.ppermute(x, axis, [(i, i ^ bits) for i in range(n)])


def put(x, piece, i):
    return lax.dynamic_update_index_in_dim(x, piece, i, 0)


def hold(*xs):
    return lax.optimization_barrier(xs)


def room(mib):
    return pltpu.CompilerParams(vmem_limit_bytes=mib * 2**20)


def shape(dims, dtype):
    return jax.ShapeDtypeStruct(dims, dtype)


def exponent(largest):
    return jnp.floor(jnp.log(jnp.maximum(largest, 1e-30)) * 1.4426950408889634)


def encode(x, e):
    u = x * jnp.exp2(13.0 - e)
    u2 = u * u
    return (u * jnp.abs(u) * u2 * (u2 * u2)).astype(BF16)


def decode(w, e):
    w = w.astype(F32)
    fourth = lax.rsqrt(lax.rsqrt(jnp.maximum(jnp.abs(w), 1e-37)))
    u = fourth * lax.rsqrt(fourth)
    return jnp.where(w > 0, u, jnp.where(w < 0, -u, 0.0)) * jnp.exp2(e - 13.0)


def largest_of(ref):
    return jnp.max(ref[...], axis=(0, 1), keepdims=True)


def grad_kernel(u_ref, p0, p1, p2, p3, tok, own, s1, s2, s3, acc, top):
    u = u_ref[0]
    top[...] = jnp.zeros_like(top)
    for r, p in enumerate((p0, p1, p2, p3)):
        g = lax.dot_general(p[...], tok[...], (((0,), (0,)), ((), ())), preferred_element_type=F32)
        acc[r ^ u] = g
        top[...] = jnp.maximum(top[...], jnp.max(jnp.abs(g).reshape(32, 8, 1152), axis=0))
    e = exponent(largest_of(top))
    own[...] = acc[0]
    for i, s in ((1, s1), (2, s2), (3, s3)):

        @pl.loop(0, 16)
        def _(j):
            rows = pl.ds(pl.multiple_of(j * 16, 16), 16)
            s[rows, :] = encode(acc[i, rows, :], e)

        s[256:272, :] = jnp.broadcast_to(e, (16, 1152)).astype(BF16)


def grad(u, pieces, tokens):
    return pl.pallas_call(
        grad_kernel,
        out_shape=[shape((256, 1152), F32)] + [shape((272, 1152), BF16)] * 3,
        in_specs=[SMEM] + [VMEM] * 5,
        out_specs=[VMEM] * 4,
        scratch_shapes=[pltpu.VMEM((4, 256, 1152), F32), pltpu.VMEM((8, 1152), F32)],
        compiler_params=room(16),
        cost_estimate=COST,
        name="grad",
    )(u, *pieces, tokens)


def sum_kernel(own, r1, r2, r3, out, acc, top):
    top[...] = jnp.zeros_like(top)
    es = [r[256:257, 0:1].astype(F32) for r in (r1, r2, r3)]

    @pl.loop(0, 16)
    def _(j):
        rows = pl.ds(pl.multiple_of(j * 16, 16), 16)
        x = own[rows, :]
        for r, e in zip((r1, r2, r3), es):
            x = x + decode(r[rows, :], e)
        acc[rows, :] = x
        top[...] = jnp.maximum(top[...], jnp.abs(x))

    e = exponent(largest_of(top))

    @pl.loop(0, 16)
    def _(j):
        rows = pl.ds(pl.multiple_of(j * 16, 16), 16)
        out[rows, :1152] = encode(acc[rows, :], e)
        out[rows, 1152:] = jnp.broadcast_to(e, (16, 128)).astype(BF16)


def sum_over_y(own, received):
    return pl.pallas_call(
        sum_kernel,
        out_shape=shape((256, 1280), BF16),
        in_specs=[VMEM] * 4,
        out_specs=VMEM,
        scratch_shapes=[pltpu.VMEM((256, 1152), F32), pltpu.VMEM((16, 1152), F32)],
        compiler_params=room(6),
        cost_estimate=COST,
        name="sum_over_y",
    )(own, *received)


def final_kernel(x, out):
    out[...] = jnp.zeros_like(out)

    @pl.loop(0, 16)
    def _(j):
        rows = pl.ds(pl.multiple_of(j * 16, 16), 16)
        out[...] += decode(x[rows, :1152], x[rows, 1152:1153].astype(F32))


def spread(x):
    return lax.all_to_all(x.reshape(16, 16, 1280), ("z", "xh"), 0, 0, tiled=True)


def sum_over_z(x):
    return pl.pallas_call(
        final_kernel,
        out_shape=shape((16, 1152), F32),
        in_specs=[VMEM],
        out_specs=VMEM,
        compiler_params=room(4),
        cost_estimate=COST,
        name="sum_over_z",
    )(x.reshape(256, 1280))


def encode12(x):
    e = exponent(jnp.max(jnp.abs(x), axis=(0, 1), keepdims=True))
    a = jnp.maximum(jnp.abs(x) * jnp.exp2(-e), 1e-30)
    w = jnp.exp2(12.0 * (jnp.log(a) * 1.4426950408889634) + 100.0)
    return jnp.where(x < 0, -w, w).astype(BF16), jnp.broadcast_to(e, (16, 256)).astype(BF16)


def decode12(w, e):
    w = w.astype(F32)
    a = jnp.maximum(jnp.abs(w), 1e-37)
    x = jnp.exp2((jnp.log(a) * 1.4426950408889634 - 100.0) * (1.0 / 12.0) + e)
    return jnp.where(w > 0, x, jnp.where(w < 0, -x, 0.0))


def project_kernel(quarters, adds, tok, w, *refs):
    n = len(quarters)
    added, outs = refs[: n * adds], refs[n * adds :]

    @pl.loop(0, 4)
    def _(j):
        rows = pl.ds(pl.multiple_of(j * 256, 256), 256)
        taller = pl.ds(pl.multiple_of(j * 272, 16), 272)
        for i, r in enumerate(quarters):
            x = lax.dot_general(
                tok[rows, :],
                w[:, r].reshape(256, 1152),
                (((1,), (1,)), ((), ())),
                preferred_element_type=F32,
            )
            for a in added[i * adds : (i + 1) * adds]:
                if a.shape[0] == 1088:
                    coded = a[taller, :]
                    x = x + decode12(coded[:256], coded[256:257, 0:1].astype(F32))
                else:
                    x = x + a[rows, :]
            if outs[i].shape[0] == 1088:
                outs[i][taller, :] = jnp.concatenate(encode12(x), axis=0)
            else:
                outs[i][rows, :] = x.astype(outs[i].dtype)


def project(tokens, w, quarters, added=(), dtype=F32, coded=False):
    n, adds = len(quarters), len(added) // len(quarters)
    return pl.pallas_call(
        functools.partial(project_kernel, quarters, adds),
        out_shape=[shape((1088 if coded else 1024, 256), dtype)] * n,
        in_specs=[VMEM] * (2 + len(added)),
        out_specs=[VMEM] * n,
        compiler_params=room(8),
        cost_estimate=COST,
        name="project",
    )(tokens, w, *added)


def back_kernel(p0, p1, p2, p3, w, *refs):
    out = refs[-1]
    flat = jnp.concatenate([w[:, r].reshape(256, 1152) for r in range(4)], axis=0)

    @pl.loop(0, 4)
    def _(j):
        rows = pl.ds(pl.multiple_of(j * 256, 256), 256)
        x = jnp.concatenate([p[rows, :] for p in (p0, p1, p2, p3)], axis=1)
        x = jnp.dot(x, flat, preferred_element_type=F32)
        for added in refs[:-1]:
            x = x + added[rows, :]
        out[rows, :] = x.astype(out.dtype)


def back(pieces, w, added=(), dtype=F32):
    return pl.pallas_call(
        back_kernel,
        out_shape=shape((1024, 1152), dtype),
        in_specs=[VMEM] * (5 + len(added)),
        out_specs=VMEM,
        compiler_params=room(12),
        cost_estimate=COST,
        name="back",
    )(*pieces, w, *added)


def per_device(tokens, kv_weight, d_kv):
    xl, core, y, xh = (lax.axis_index(a) for a in ("xl", "core", "y", "xh"))
    dp = 2 * xl + core
    u = (dp ^ y).reshape(1)

    own_k, own_v = d_kv[:, 0], d_kv[:, 1]
    wt = jnp.transpose(kv_weight, (0, 2, 1))

    both = put(put(jnp.zeros((2, *wt.shape), BF16), wt, xh), flip(wt, "xh", 1), xh ^ 1)
    both = jnp.transpose(both, (1, 0, 2, 3)).reshape(2, 32, 1152)
    beside_k, beside_v = flip(own_k, "core", 1), flip(own_v, "core", 1)
    both, own_k, own_v = hold(both, own_k, own_v)

    across_k = flip(own_k, "xl", 1)
    wy = put(jnp.zeros((4, 2, 32, 1152), BF16), both, y ^ dp)
    for bits in (1, 3, 2):
        wy = put(wy, flip(both, "y", bits), y ^ bits ^ dp)
    wk = lax.all_gather(wy[:, 0].reshape(128, 1152), "z", axis=0, tiled=True).reshape(8, 4, 32, 1152)
    wv = lax.all_gather(wy[:, 1].reshape(128, 1152), "z", axis=0, tiled=True).reshape(8, 4, 32, 1152)
    across_k, wy, own_v = hold(across_k, wy, own_v)

    across_v = flip(own_v, "xl", 1)
    corner_k = flip(across_k, "core", 1)
    gk, *send_k = grad(u, (own_k, beside_k, across_k, corner_k), tokens)
    got_k = [flip(s, "y", bits) for s, bits in zip(send_k, (1, 2, 3))]
    across_v, gk = hold(across_v, gk)
    corner_v = flip(across_v, "core", 1)
    gv, *send_v = grad(u, (own_v, beside_v, across_v, corner_v), tokens)
    got_v = [flip(s, "y", bits) for s, bits in zip(send_v, (1, 2, 3))]

    gv, gk, wk, *got_k = hold(gv, gk, wk, *got_k)
    to_far, to_near = project(tokens, wk, (3, 1))
    (far,) = project(tokens, wk, (2,), (flip(to_far, "core", 1),))
    near_k = flip(to_near, "core", 1)
    across = flip(far, "xl", 1)
    gk, far = hold(gk, far)
    total_k = spread(sum_over_y(gk, got_k))
    d_tokens = back((own_k, beside_k, across_k, corner_k), wk)
    total_k, across, d_tokens, gv, wv, near_k, *got_v = hold(
        total_k, across, d_tokens, gv, wv, near_k, *got_v
    )

    to_far, to_near = project(tokens, wv, (3, 1))
    (far,) = project(tokens, wv, (2,), (flip(to_far, "core", 1),), BF16, True)
    near_v = flip(to_near, "core", 1)
    across_out = flip(far, "xl", 1)
    gv, far, total_k, across = hold(gv, far, total_k, across)
    total_v = spread(sum_over_y(gv, got_v))
    grad_k = sum_over_z(total_k)
    (out_k,) = project(tokens, wk, (0,), (near_k, across), BF16)
    total_v, across_out, out_k, grad_k, wv = hold(total_v, across_out, out_k, grad_k, wv)
    grad_v = sum_over_z(total_v)
    (out_v,) = project(tokens, wv, (0,), (near_v, across_out), BF16)
    d_tokens = back((own_v, beside_v, across_v, corner_v), wv, (d_tokens,), BF16)
    kv_out = jnp.stack([out_k, out_v], axis=1)
    grad_kv = jnp.transpose(jnp.stack([grad_k, grad_v]), (0, 2, 1))
    return (kv_out, d_tokens, grad_kv)


def solution(mesh):
    fine = Mesh(mesh.devices.reshape(2, 2, 4, 8, 2), DP + MP)
    return jax.shard_map(
        per_device,
        mesh=fine,
        in_specs=(P(MP, DP), P(None, DP, MP), P(MP, None, DP)),
        out_specs=(P(MP, None, DP), P(MP, DP), P(None, DP, MP)),
        check_vma=False,
    )
```

time: 517 us -> 211 us (0.41)
  waiting for transfers between devices: 449 us -> 65.4 us
  starting transfers between devices: 0.29 us -> 47.6 us
  Pallas kernels: 0 us -> 41.1 us
  matrix products: 27.4 us -> 0 us
  local copies, waits for them, and re-layouts: 18.3 us -> 40.9 us
  blocking collectives: 6.07 us -> 0 us
    unnamed x8 -> x2, waiting for transfers between devices: 208 us -> 0.71 us
    all_gather x3 -> x2, waiting for transfers between devices: 128 us -> 0.01 us  [the longest x1 0.01 us: per_device(): lax.all_gather(wy[:, 0].reshape(128, 1152), 'z', axis=0, tiled=True)]
    reduce_scatter x3 -> x0, waiting for transfers between devices: 114 us -> none  [the longest x1 75.3 us: per_device(): lax.psum_scatter(partial_value, DP, scatter_dimension=2, tiled=True)]
    ppermute x0 -> x22, waiting for transfers between devices: none -> 64.7 us  [flip(): return lax.ppermute(x, axis, [(i, i ^ bits) for i in range(n)])]
    pallas_call x0 -> x14, Pallas kernels: none -> 41.1 us  [the longest x6 14.2 us: project(): pl.pallas_call(functools.partial(project_kernel, quarters, adds), out_sha...]
    ppermute x0 -> x22, starting transfers between devices: none -> 29.1 us  [flip(): return lax.ppermute(x, axis, [(i, i ^ bits) for i in range(n)])]
    dot_general x3 -> x0, matrix products: 27.4 us -> none  [the longest x1 10.1 us: per_device(): jnp.einsum('td,kdc->tkc', tokens, panels, preferred_element_type=jnp.floa...]
    unnamed x9 -> x107, local copies, waits for them, and re-layouts: 9.12 us -> 35.6 us
  transfers between devices with their start and end apart: 7 -> 26, of which waited for: 7 -> 13; matrix products, arithmetic and copies ran while one was open for 9% -> 2% of each run, Pallas kernels for 0% -> 12%
where the time goes in v2:
time: 211 us; the launch traced here: 210 us
  waiting for transfers between devices  65.4 us (31%)
  starting transfers between devices  47.6 us (23%)
  Pallas kernels  41.1 us (19%)
  local copies, waits for them, and re-layouts  40.9 us (19%)
  between operations  14.6 us (7%)
    ppermute x22, waiting for transfers between devices, flip(): return lax.ppermute(x, axis, [(i, i ^ bits) for i in range(n)])  64.7 us
    unnamed x107, local copies, waits for them, and re-layouts  35.6 us
    ppermute x22, starting transfers between devices, flip(): return lax.ppermute(x, axis, [(i, i ^ bits) for i in range(n)])  29.1 us
    all_to_all x2, starting transfers between devices, spread(): lax.all_to_all(x.reshape(16, 16, 1280), ('z', 'xh'), 0, 0, tiled=True)  18.4 us
    pallas_call x6, Pallas kernels, project(): pl.pallas_call(functools.partial(project_kernel, quarters, adds), out_sha...  14.2 us
    pallas_call x2, Pallas kernels, grad(): pl.pallas_call(grad_kernel, out_shape=[shape((256, 1152), F32)] + [shape(...  8.64 us
    pallas_call x2, Pallas kernels, back(): pl.pallas_call(back_kernel, out_shape=shape((1024, 1152), dtype), in_spec...  8.62 us
    pallas_call x2, Pallas kernels, sum_over_y(): pl.pallas_call(sum_kernel, out_shape=shape((256, 1280), BF16), in_specs=[...  5.86 us
  transfers between devices with their start and end apart: 26, of which 13 were waited for; matrix products, arithmetic and copies ran while one was open for 2% of the time, Pallas kernels for 12%

profile of v2, /device:TPU:1, one launch (start us, length us, event | category | flops | bytes accessed | tf_op | source)
XLA Modules:
  0.0 210.4 jit_solution(10506453666762768287)
XLA Ops:
  7.2 3.7 %collective-permute-start = (bf16[2,16,1152]{2,1,0:T(8,128)(2,1)}, bf16[2,16,1152]{2,1,0:T(8,128)(2,1)S(1)}, u32[]{:S(2)}, u32[]{:S(2)}) collective-permute-start(bf16[2,16,1152]{2,1,0:T(8,128)(2,1)} %bitcast.71), channel_id=1, source_target_pairs={{0,1},{1,0},{2,3},{3,2},{4,5},{5,4},{6,7},{7,6},{8,9},{9,8},{10,11... | collective-permute-start | bytes 221192 | tf_op jit(solution)/shard_map/ppermute | solution.py:21
  10.9 0.9 bitcast_dynamic-update-slice_fusion.4
  11.8 3.3 %fusion = (bf16[1024,1,256]{2,1,0:T(2,128)(2,1)S(1)}, bf16[1024,1,256]{2,1,0:T(2,128)(2,1)S(1)}) fusion(bf16[1024,2,256]{2,1,0:T(2,128)(2,1)} %param.5), kind=kLoop, calls=%fused_computation.10 | loop fusion | bytes 2097152 | tf_op jit(solution)/shard_map/slice | solution.py:238
  15.4 3.0 %collective-permute-start.4 = (bf16[2,32,1152]{2,1,0:T(8,128)(2,1)S(1)}, bf16[2,32,1152]{2,1,0:T(8,128)(2,1)S(1)}, u32[]{:S(2)}, u32[]{:S(2)}) collective-permute-start(bf16[2,32,1152]{2,1,0:T(8,128)(2,1)S(1)} %bitcast.67), channel_id=1, source_target_pairs={{0,32},{16,48},{32,0},{48,16},{1,33},{17,49},{33,1},{49,17},{2,34}... | collective-permute-start | bytes 442376 | tf_op jit(solution)/shard_map/ppermute | solution.py:21
  19.3 5.8 %collective-permute-done.2 = bf16[2,32,1152]{2,1,0:T(8,128)(2,1)S(1)} collective-permute-done((bf16[2,32,1152]{2,1,0:T(8,128)(2,1)S(1)}, bf16[2,32,1152]{2,1,0:T(8,128)(2,1)S(1)}, u32[]{:S(2)}, u32[]{:S(2)}) %collective-permute-start.2) | collective-permute-done | bytes 147488 | tf_op jit(solution)/shard_map/ppermute | solution.py:21
  25.2 0.9 fusion.1
  27.3 2.0 collective-permute-start.7
  29.3 9.4 %collective-permute-done.1.p2 = bf16[1024,256]{1,0:T(8,128)(2,1)S(1)} collective-permute-done((bf16[1024,256]{1,0:T(8,128)(2,1)S(1)}, bf16[1024,256]{1,0:T(8,128)(2,1)S(1)}, u32[]{:S(2)}, u32[]{:S(2)}) %collective-permute-start.1) | collective-permute-done | bytes 524320 | tf_op jit(solution)/shard_map/ppermute | solution.py:21
  38.7 2.6 %collective-permute-start.8 = (bf16[1024,256]{1,0:T(8,128)(2,1)S(1)}, bf16[1024,256]{1,0:T(8,128)(2,1)S(1)}, u32[]{:S(2)}, u32[]{:S(2)}) collective-permute-start(bf16[1024,256]{1,0:T(8,128)(2,1)S(1)} %collective-permute-done.1.p2), channel_id=1, source_target_pairs={{0,64},{64,0},{1,65},{65,1},{2,66},{66,2},{3,67},{67,3},{4,68},{68... | collective-permute-start | bytes 1572872 | tf_op jit(solution)/shard_map/ppermute | solution.py:21
  41.6 1.2 collective-permute-done.8.p3
  42.8 4.3 %grad.2 = (f32[256,1152]{1,0:T(8,128)S(1)}, bf16[272,1152]{1,0:T(8,128)(2,1)S(1)}, bf16[272,1152]{1,0:T(8,128)(2,1)S(1)}, bf16[272,1152]{1,0:T(8,128)(2,1)S(1)}) custom-call(s32[1]{0:T(128)} %bitcast.u_ref, bf16[1024,256]{1,0:T(8,128)(2,1)S(1)} %bitcast.56, bf16[1024,256]{1,0:T(8,128)(2,1)S(1)} %collective-permute-done.7.p1, ...), custom_call_target="tpu_custom_call" | custom-call | flops 1 | bytes 1 | tf_op jit(solution)/shard_map/grad/pallas_call | solution.py:81
  47.2 1.0 copy-done.27
  48.2 2.1 collective-permute-start.10
  50.3 2.5 %collective-permute-start.11 = (bf16[272,1152]{1,0:T(8,128)(2,1)S(1)}, bf16[272,1152]{1,0:T(8,128)(2,1)S(1)}, u32[]{:S(2)}, u32[]{:S(2)}) collective-permute-start(bf16[272,1152]{1,0:T(8,128)(2,1)S(1)} %get-tuple-element.56), channel_id=1, source_target_pairs={{0,32},{16,48},{32,0},{48,16},{1,33},{17,49},{33,1},{49,17},{2,34}... | collective-permute-start | bytes 1880072 | tf_op jit(solution)/shard_map/ppermute | solution.py:21
  52.8 0.9 collective-permute-start.5
  53.7 1.1 collective-permute-done.6.p2
  55.6 1.5 collective-permute-done.9.p3
  57.2 4.3 %grad.3 = (f32[256,1152]{1,0:T(8,128)S(1)}, bf16[272,1152]{1,0:T(8,128)(2,1)S(1)}, bf16[272,1152]{1,0:T(8,128)(2,1)S(1)}, bf16[272,1152]{1,0:T(8,128)(2,1)S(1)}) custom-call(s32[1]{0:T(128)} %bitcast.u_ref, bf16[1024,256]{1,0:T(8,128)(2,1)S(1)} %bitcast.52, bf16[1024,256]{1,0:T(8,128)(2,1)S(1)} %collective-permute-done.5.p1, ...), custom_call_target="tpu_custom_call" | custom-call | flops 1 | bytes 1 | tf_op jit(solution)/shard_map/grad/pallas_call | solution.py:81
  62.4 1.0 copy-done.25
  63.4 0.8 copy-done.49
  66.8 13.4 %collective-permute-done.11.r2 = bf16[272,1152]{1,0:T(8,128)(2,1)S(1)} collective-permute-done((bf16[272,1152]{1,0:T(8,128)(2,1)S(1)}, bf16[272,1152]{1,0:T(8,128)(2,1)S(1)}, u32[]{:S(2)}, u32[]{:S(2)}) %collective-permute-start.11) | collective-permute-done | bytes 626720 | tf_op jit(solution)/shard_map/ppermute | solution.py:21
  80.9 1.2 collective-permute-done.12.r3
  82.9 1.7 copy-done.1
  84.6 2.1 %project.6 = (f32[1024,256]{1,0:T(8,128)S(1)}, f32[1024,256]{1,0:T(8,128)S(1)}) custom-call(bf16[1024,1152]{1,0:T(8,128)(2,1)S(1)} %copy-done, bf16[8,4,32,1152]{3,2,1,0:T(8,128)(2,1)S(1)} %bitcast.42), custom_call_target="tpu_custom_call" | custom-call | flops 1 | bytes 1 | tf_op jit(solution)/shard_map/project/pallas_call | solution.py:196
  86.8 1.0 copy-done.47
  87.7 1.9 collective-permute-start.13
  89.7 2.3 %collective-permute-done.13.refs_0_ = f32[1024,256]{1,0:T(8,128)S(1)} collective-permute-done((f32[1024,256]{1,0:T(8,128)S(1)}, f32[1024,256]{1,0:T(8,128)S(1)}, u32[]{:S(2)}, u32[]{:S(2)}) %collective-permute-start.13) | collective-permute-done | bytes 1048608 | tf_op jit(solution)/shard_map/ppermute | solution.py:21
  92.0 1.5 project.7
  93.5 2.9 %sum_over_y.2 = bf16[256,1280]{1,0:T(8,128)(2,1)S(1)} custom-call(f32[256,1152]{1,0:T(8,128)S(1)} %copy-done.28, bf16[272,1152]{1,0:T(8,128)(2,1)S(1)} %copy-done.31, bf16[272,1152]{1,0:T(8,128)(2,1)S(1)} %copy-done.33, bf16[272,1152]{1,0:T(8,128)(2,1)S(1)} %copy-done.37), custom_call_target="tpu_custom_call" | custom-call | flops 1 | bytes 1 | tf_op jit(solution)/shard_map/sum_over_y/pallas_call | solution.py:116
  96.5 0.8 copy-done.9
  97.3 8.6 %all-to-all-start = ((bf16[16,16,1280]{2,1,0:T(8,128)(2,1)}), bf16[16,16,1280]{2,1,0:T(8,128)(2,1)}, u32[]{:S(2)}, u32[]{:S(2)}) async-start(bf16[16,16,1280]{2,1,0:T(8,128)(2,1)} %bitcast.59), calls=%async_computation | async-start | bytes 1310720 | tf_op jit(solution)/shard_map/all_to_all | solution.py:138
  106.7 0.9 collective-permute-start.14
  107.5 1.2 collective-permute-start.17
  108.7 2.7 %collective-permute-start.18 = (bf16[272,1152]{1,0:T(8,128)(2,1)}, bf16[272,1152]{1,0:T(8,128)(2,1)S(1)}, u32[]{:S(2)}, u32[]{:S(2)}) collective-permute-start(bf16[272,1152]{1,0:T(8,128)(2,1)} %copy-done.49), channel_id=1, source_target_pairs={{0,48},{16,32},{32,16},{48,0},{1,49},{17,33},{33,17},{49,1},{2,50}... | collective-permute-start | bytes 1880072 | tf_op jit(solution)/shard_map/ppermute | solution.py:21
  111.4 1.7 copy-done.2
  113.0 1.0 copy-done.20
  114.1 1.0 copy-done.22
  115.1 1.0 copy-done.24
  116.2 3.5 %back.2.refs_0_ = f32[1024,1152]{1,0:T(8,128)S(1)} custom-call(bf16[1024,256]{1,0:T(8,128)(2,1)S(1)} %bitcast.57, bf16[1024,256]{1,0:T(8,128)(2,1)S(1)} %copy-done.22, bf16[1024,256]{1,0:T(8,128)(2,1)S(1)} %copy-done.20, bf16[1024,256]{1,0:T(8,128)(2,1)S(1)} %copy-done.24, bf16[8,4,32,1152]{3,2,1,0:T(8,128)(2,1)S(1)} %bitcast.44), custom_call_target="tpu_custom_call" | custom-call | flops 1 | bytes 1 | tf_op jit(solution)/shard_map/back/pallas_call | solution.py:222
  119.7 2.2 %copy-done.7 = f32[1024,1152]{1,0:T(8,128)} copy-done((f32[1024,1152]{1,0:T(8,128)}, f32[1024,1152]{1,0:T(8,128)S(1)}, u32[]{:S(2)}) %copy-start.7) | copy-done | bytes 4718616
  121.9 1.3 collective-permute-done.16.r1
  123.2 0.8 copy-done.34
  124.0 12.2 %collective-permute-done.17.r2 = bf16[272,1152]{1,0:T(8,128)(2,1)S(1)} collective-permute-done((bf16[272,1152]{1,0:T(8,128)(2,1)}, bf16[272,1152]{1,0:T(8,128)(2,1)S(1)}, u32[]{:S(2)}, u32[]{:S(2)}) %collective-permute-start.17) | collective-permute-done | bytes 626720 | tf_op jit(solution)/shard_map/ppermute | solution.py:21
  137.1 1.2 collective-permute-done.18.r3
  138.3 0.8 copy-done.40
  139.2 1.7 copy-done.4
  140.8 2.1 %project.8 = (f32[1024,256]{1,0:T(8,128)S(1)}, f32[1024,256]{1,0:T(8,128)S(1)}) custom-call(bf16[1024,1152]{1,0:T(8,128)(2,1)S(1)} %copy-done, bf16[8,4,32,1152]{3,2,1,0:T(8,128)(2,1)S(1)} %bitcast.46), custom_call_target="tpu_custom_call" | custom-call | flops 1 | bytes 1 | tf_op jit(solution)/shard_map/project/pallas_call | solution.py:196
  143.0 1.0 copy-done.48
  144.0 1.9 collective-permute-start.19
  145.9 2.3 %collective-permute-done.19.refs_0_ = f32[1024,256]{1,0:T(8,128)S(1)} collective-permute-done((f32[1024,256]{1,0:T(8,128)S(1)}, f32[1024,256]{1,0:T(8,128)S(1)}, u32[]{:S(2)}, u32[]{:S(2)}) %collective-permute-start.19) | collective-permute-done | bytes 1048608 | tf_op jit(solution)/shard_map/ppermute | solution.py:21
  148.1 2.5 %project.9 = bf16[1088,256]{1,0:T(8,128)(2,1)S(1)} custom-call(bf16[1024,1152]{1,0:T(8,128)(2,1)S(1)} %copy-done, bf16[8,4,32,1152]{3,2,1,0:T(8,128)(2,1)S(1)} %bitcast.47, f32[1024,256]{1,0:T(8,128)S(1)} %collective-permute-done.19.refs_0_), custom_call_target="tpu_custom_call" | custom-call | flops 1 | bytes 1 | tf_op jit(solution)/shard_map/project/pallas_call | solution.py:196
  150.7 2.9 %sum_over_y.3 = bf16[256,1280]{1,0:T(8,128)(2,1)S(1)} custom-call(f32[256,1152]{1,0:T(8,128)S(1)} %copy-done.26, bf16[272,1152]{1,0:T(8,128)(2,1)S(1)} %copy-done.35, bf16[272,1152]{1,0:T(8,128)(2,1)S(1)} %copy-done.39, bf16[272,1152]{1,0:T(8,128)(2,1)S(1)} %copy-done.41), custom_call_target="tpu_custom_call" | custom-call | flops 1 | bytes 1 | tf_op jit(solution)/shard_map/sum_over_y/pallas_call | solution.py:116
  154.5 9.8 %all-to-all-start.1 = ((bf16[16,16,1280]{2,1,0:T(8,128)(2,1)}), bf16[16,16,1280]{2,1,0:T(8,128)(2,1)S(1)}, u32[]{:S(2)}, u32[]{:S(2)}) async-start(bf16[16,16,1280]{2,1,0:T(8,128)(2,1)} %bitcast.60), calls=%async_computation.1 | async-start | bytes 1310720 | tf_op jit(solution)/shard_map/all_to_all | solution.py:138
  165.0 2.4 %sum_over_z.2 = f32[16,1152]{1,0:T(8,128)S(1)} custom-call(bf16[256,1280]{1,0:T(8,128)(2,1)} %bitcast.20.x), custom_call_target="tpu_custom_call" | custom-call | flops 1 | bytes 1 | tf_op jit(solution)/shard_map/sum_over_z/pallas_call | solution.py:142
  168.1 1.7 copy-done.3
  169.8 3.0 %project.10 = bf16[1024,256]{1,0:T(8,128)(2,1)S(1)} custom-call(bf16[1024,1152]{1,0:T(8,128)(2,1)S(1)} %copy-done, bf16[8,4,32,1152]{3,2,1,0:T(8,128)(2,1)S(1)} %bitcast.45, f32[1024,256]{1,0:T(8,128)} %collective-permute-done.15.refs_0_, f32[1024,256]{1,0:T(8,128)} %collective-permute-done.14.refs_1_), custom_call_target="tpu_custom_call" | custom-call | flops 1 | bytes 1 | tf_op jit(solution)/shard_map/project/pallas_call | solution.py:196
  173.6 11.8 %collective-permute-done.20.refs_1_ = bf16[1088,256]{1,0:T(8,128)(2,1)S(1)} collective-permute-done((bf16[1088,256]{1,0:T(8,128)(2,1)}, bf16[1088,256]{1,0:T(8,128)(2,1)S(1)}, u32[]{:S(2)}, u32[]{:S(2)}) %collective-permute-start.20) | collective-permute-done | bytes 557088 | tf_op jit(solution)/shard_map/ppermute | solution.py:21
  186.3 1.4 sum_over_z.3
  187.6 1.7 copy-done.5
  189.3 1.1 copy-done.44
  190.3 2.9 %project.11 = bf16[1024,256]{1,0:T(8,128)(2,1)S(1)} custom-call(bf16[1024,1152]{1,0:T(8,128)(2,1)S(1)} %copy-done, bf16[8,4,32,1152]{3,2,1,0:T(8,128)(2,1)S(1)} %bitcast.48, f32[1024,256]{1,0:T(8,128)} %collective-permute-done.21.refs_0_, bf16[1088,256]{1,0:T(8,128)(2,1)S(1)} %copy-done.44), custom_call_target="tpu_custom_call" | custom-call | flops 1 | bytes 1 | tf_op jit(solution)/shard_map/project/pallas_call | solution.py:196
  193.5 2.0 copy.17
  196.2 2.3 %copy-done.8 = f32[1024,1152]{1,0:T(8,128)S(1)} copy-done((f32[1024,1152]{1,0:T(8,128)S(1)}, f32[1024,1152]{1,0:T(8,128)}, u32[]{:S(2)}) %copy-start.8) | copy-done | bytes 4718616
  198.5 5.1 %back.3 = bf16[1024,1152]{1,0:T(8,128)(2,1)} custom-call(bf16[1024,256]{1,0:T(8,128)(2,1)S(1)} %bitcast.53, bf16[1024,256]{1,0:T(8,128)(2,1)S(1)} %copy-done.16, bf16[1024,256]{1,0:T(8,128)(2,1)S(1)} %copy-done.14, bf16[1024,256]{1,0:T(8,128)(2,1)S(1)} %copy-done.18, bf16[8,4,32,1152]{3,2,1,0:T(8,128)(2,1)S(1)} %bitcast.49, f32[1024,1152]{1,0:T(8,128)S(1)} %copy-done.8), custom_call_target="tpu_custom_call" | custom-call | flops 1 | bytes 1 | tf_op jit(solution)/shard_map/back/pallas_call | solution.py:222
  (124 shorter events, 14.8 us)
Async XLA Ops:
  7.2 75.8 %all-gather.3.cloned.1.call-start = ((), (), s32[]{:S(2)}) async-start(), calls=%async_computation.2 | async-start | bytes 2654208 | tf_op jit(solution)/shard_map/all_gather | solution.py:250
  7.2 8.2 %collective-permute-start = (bf16[2,16,1152]{2,1,0:T(8,128)(2,1)}, bf16[2,16,1152]{2,1,0:T(8,128)(2,1)S(1)}, u32[]{:S(2)}, u32[]{:S(2)}) collective-permute-start(bf16[2,16,1152]{2,1,0:T(8,128)(2,1)} %bitcast.71), channel_id=1, source_target_pairs={{0,1},{1,0},{2,3},{3,2},{4,5},{5,4},{6,7},{7,6},{8,9},{9,8},{10,11... | collective-permute-start | bytes 221192 | tf_op jit(solution)/shard_map/ppermute | solution.py:21
  15.4 27.4 %copy-start = (bf16[1024,1152]{1,0:T(8,128)(2,1)S(1)}, bf16[1024,1152]{1,0:T(8,128)(2,1)}, u32[]{:S(2)}) copy-start(bf16[1024,1152]{1,0:T(8,128)(2,1)} %tok.15) | copy-start | bytes 7077892
  15.4 9.8 %collective-permute-start.4 = (bf16[2,32,1152]{2,1,0:T(8,128)(2,1)S(1)}, bf16[2,32,1152]{2,1,0:T(8,128)(2,1)S(1)}, u32[]{:S(2)}, u32[]{:S(2)}) collective-permute-start(bf16[2,32,1152]{2,1,0:T(8,128)(2,1)S(1)} %bitcast.67), channel_id=1, source_target_pairs={{0,32},{16,48},{32,0},{48,16},{1,33},{17,49},{33,1},{49,17},{2,34}... | collective-permute-start | bytes 442376 | tf_op jit(solution)/shard_map/ppermute | solution.py:21
  18.4 6.7 %collective-permute-start.3 = (bf16[2,32,1152]{2,1,0:T(8,128)(2,1)S(1)}, bf16[2,32,1152]{2,1,0:T(8,128)(2,1)S(1)}, u32[]{:S(2)}, u32[]{:S(2)}) collective-permute-start(bf16[2,32,1152]{2,1,0:T(8,128)(2,1)S(1)} %bitcast.68), channel_id=1, source_target_pairs={{0,48},{16,32},{32,16},{48,0},{1,49},{17,33},{33,17},{49,1},{2,50}... | collective-permute-start | bytes 442376 | tf_op jit(solution)/shard_map/ppermute | solution.py:21
  19.2 5.9 %collective-permute-start.2 = (bf16[2,32,1152]{2,1,0:T(8,128)(2,1)S(1)}, bf16[2,32,1152]{2,1,0:T(8,128)(2,1)S(1)}, u32[]{:S(2)}, u32[]{:S(2)}) collective-permute-start(bf16[2,32,1152]{2,1,0:T(8,128)(2,1)S(1)} %bitcast.69), channel_id=1, source_target_pairs={{0,16},{16,0},{32,48},{48,32},{1,17},{17,1},{33,49},{49,33},{2,18}... | collective-permute-start | bytes 442376 | tf_op jit(solution)/shard_map/ppermute | solution.py:21
  26.1 113.0 %all-gather.5.cloned.1.call-start = ((), (), s32[]{:S(2)}) async-start(), calls=%async_computation.3 | async-start | bytes 2654208 | tf_op jit(solution)/shard_map/all_gather | solution.py:251
  26.9 11.8 %collective-permute-start.1 = (bf16[1024,256]{1,0:T(8,128)(2,1)S(1)}, bf16[1024,256]{1,0:T(8,128)(2,1)S(1)}, u32[]{:S(2)}, u32[]{:S(2)}) collective-permute-start(bf16[1024,256]{1,0:T(8,128)(2,1)S(1)} %bitcast.54), channel_id=1, source_target_pairs={{0,128},{128,0},{1,129},{129,1},{2,130},{130,2},{3,131},{131,3},{4... | collective-permute-start | bytes 1572872 | tf_op jit(solution)/shard_map/ppermute | solution.py:21
  27.3 14.3 %collective-permute-start.7 = (bf16[1024,256]{1,0:T(8,128)(2,1)S(1)}, bf16[1024,256]{1,0:T(8,128)(2,1)S(1)}, u32[]{:S(2)}, u32[]{:S(2)}) collective-permute-start(bf16[1024,256]{1,0:T(8,128)(2,1)S(1)} %bitcast.55), channel_id=1, source_target_pairs={{0,64},{64,0},{1,65},{65,1},{2,66},{66,2},{3,67},{67,3},{4,68},{68... | collective-permute-start | bytes 1572872 | tf_op jit(solution)/shard_map/ppermute | solution.py:21
  38.7 22.9 %copy-start.19 = (bf16[1024,256]{1,0:T(8,128)(2,1)}, bf16[1024,256]{1,0:T(8,128)(2,1)S(1)}, u32[]{:S(2)}) copy-start(bf16[1024,256]{1,0:T(8,128)(2,1)S(1)} %collective-permute-done.1.p2) | copy-start | bytes 1572868
  38.7 4.2 %collective-permute-start.8 = (bf16[1024,256]{1,0:T(8,128)(2,1)S(1)}, bf16[1024,256]{1,0:T(8,128)(2,1)S(1)}, u32[]{:S(2)}, u32[]{:S(2)}) collective-permute-start(bf16[1024,256]{1,0:T(8,128)(2,1)S(1)} %collective-permute-done.1.p2), channel_id=1, source_target_pairs={{0,64},{64,0},{1,65},{65,1},{2,66},{66,2},{3,67},{67,3},{4,68},{68... | collective-permute-start | bytes 1572872 | tf_op jit(solution)/shard_map/ppermute | solution.py:21
  41.3 13.6 %collective-permute-start.6 = (bf16[1024,256]{1,0:T(8,128)(2,1)S(1)}, bf16[1024,256]{1,0:T(8,128)(2,1)S(1)}, u32[]{:S(2)}, u32[]{:S(2)}) collective-permute-start(bf16[1024,256]{1,0:T(8,128)(2,1)S(1)} %bitcast.50), channel_id=1, source_target_pairs={{0,128},{128,0},{1,129},{129,1},{2,130},{130,2},{3,131},{131,3},{4... | collective-permute-start | bytes 1572872 | tf_op jit(solution)/shard_map/ppermute | solution.py:21
  41.6 11.2 %copy-start.21 = (bf16[1024,256]{1,0:T(8,128)(2,1)}, bf16[1024,256]{1,0:T(8,128)(2,1)S(1)}, u32[]{:S(2)}) copy-start(bf16[1024,256]{1,0:T(8,128)(2,1)S(1)} %collective-permute-done.7.p1) | copy-start | bytes 1572868
  42.8 12.0 %copy-start.23 = (bf16[1024,256]{1,0:T(8,128)(2,1)}, bf16[1024,256]{1,0:T(8,128)(2,1)S(1)}, u32[]{:S(2)}) copy-start(bf16[1024,256]{1,0:T(8,128)(2,1)S(1)} %collective-permute-done.8.p3) | copy-start | bytes 1572868
  47.2 1.0 copy-start.27
  48.2 17.7 %collective-permute-start.10 = (bf16[272,1152]{1,0:T(8,128)(2,1)S(1)}, bf16[272,1152]{1,0:T(8,128)(2,1)S(1)}, u32[]{:S(2)}, u32[]{:S(2)}) collective-permute-start(bf16[272,1152]{1,0:T(8,128)(2,1)S(1)} %get-tuple-element.55), channel_id=1, source_target_pairs={{0,16},{16,0},{32,48},{48,32},{1,17},{17,1},{33,49},{49,33},{2,18}... | collective-permute-start | bytes 1880072 | tf_op jit(solution)/shard_map/ppermute | solution.py:21
  50.3 29.9 %collective-permute-start.11 = (bf16[272,1152]{1,0:T(8,128)(2,1)S(1)}, bf16[272,1152]{1,0:T(8,128)(2,1)S(1)}, u32[]{:S(2)}, u32[]{:S(2)}) collective-permute-start(bf16[272,1152]{1,0:T(8,128)(2,1)S(1)} %get-tuple-element.56), channel_id=1, source_target_pairs={{0,32},{16,48},{32,0},{48,16},{1,33},{17,49},{33,1},{49,17},{2,34}... | collective-permute-start | bytes 1880072 | tf_op jit(solution)/shard_map/ppermute | solution.py:21
  52.8 29.3 %collective-permute-start.12 = (bf16[272,1152]{1,0:T(8,128)(2,1)S(1)}, bf16[272,1152]{1,0:T(8,128)(2,1)S(1)}, u32[]{:S(2)}, u32[]{:S(2)}) collective-permute-start(bf16[272,1152]{1,0:T(8,128)(2,1)S(1)} %get-tuple-element.57), channel_id=1, source_target_pairs={{0,48},{16,32},{32,16},{48,0},{1,49},{17,33},{33,17},{49,1},{2,50}... | collective-permute-start | bytes 1880072 | tf_op jit(solution)/shard_map/ppermute | solution.py:21
  52.8 2.9 %collective-permute-start.5 = (bf16[1024,256]{1,0:T(8,128)(2,1)S(1)}, bf16[1024,256]{1,0:T(8,128)(2,1)S(1)}, u32[]{:S(2)}, u32[]{:S(2)}) collective-permute-start(bf16[1024,256]{1,0:T(8,128)(2,1)S(1)} %bitcast.51), channel_id=1, source_target_pairs={{0,64},{64,0},{1,65},{65,1},{2,66},{66,2},{3,67},{67,3},{4,68},{68... | collective-permute-start | bytes 1572872 | tf_op jit(solution)/shard_map/ppermute | solution.py:21
  54.9 2.3 %collective-permute-start.9 = (bf16[1024,256]{1,0:T(8,128)(2,1)S(1)}, bf16[1024,256]{1,0:T(8,128)(2,1)S(1)}, u32[]{:S(2)}, u32[]{:S(2)}) collective-permute-start(bf16[1024,256]{1,0:T(8,128)(2,1)S(1)} %collective-permute-done.6.p2), channel_id=1, source_target_pairs={{0,64},{64,0},{1,65},{65,1},{2,66},{66,2},{3,67},{67,3},{4,68},{68... | collective-permute-start | bytes 1572872 | tf_op jit(solution)/shard_map/ppermute | solution.py:21
  55.6 5.9 %copy-start.15 = (bf16[1024,256]{1,0:T(8,128)(2,1)}, bf16[1024,256]{1,0:T(8,128)(2,1)S(1)}, u32[]{:S(2)}) copy-start(bf16[1024,256]{1,0:T(8,128)(2,1)S(1)} %collective-permute-done.5.p1) | copy-start | bytes 1572868
  57.2 8.7 %copy-start.17 = (bf16[1024,256]{1,0:T(8,128)(2,1)}, bf16[1024,256]{1,0:T(8,128)(2,1)S(1)}, u32[]{:S(2)}) copy-start(bf16[1024,256]{1,0:T(8,128)(2,1)S(1)} %collective-permute-done.9.p3) | copy-start | bytes 1572868
  62.4 1.0 copy-start.25
  82.9 1.7 copy-start.1
  86.7 1.0 copy-start.47
  87.7 5.7 %copy-start.28 = (f32[256,1152]{1,0:T(8,128)S(1)}, f32[256,1152]{1,0:T(8,128)}, u32[]{:S(2)}) copy-start(f32[256,1152]{1,0:T(8,128)} %copy-done.27) | copy-start | bytes 3538948
  87.7 5.7 %copy-start.31 = (bf16[272,1152]{1,0:T(8,128)(2,1)S(1)}, bf16[272,1152]{1,0:T(8,128)(2,1)}, u32[]{:S(2)}) copy-start(bf16[272,1152]{1,0:T(8,128)(2,1)} %copy-done.30) | copy-start | bytes 1880068
  87.7 5.7 %copy-start.33 = (bf16[272,1152]{1,0:T(8,128)(2,1)S(1)}, bf16[272,1152]{1,0:T(8,128)(2,1)}, u32[]{:S(2)}) copy-start(bf16[272,1152]{1,0:T(8,128)(2,1)} %copy-done.32) | copy-start | bytes 1880068
  87.7 5.8 %copy-start.37 = (bf16[272,1152]{1,0:T(8,128)(2,1)S(1)}, bf16[272,1152]{1,0:T(8,128)(2,1)}, u32[]{:S(2)}) copy-start(bf16[272,1152]{1,0:T(8,128)(2,1)} %copy-done.36) | copy-start | bytes 1880068
  87.7 4.2 %collective-permute-start.13 = (f32[1024,256]{1,0:T(8,128)S(1)}, f32[1024,256]{1,0:T(8,128)S(1)}, u32[]{:S(2)}, u32[]{:S(2)}) collective-permute-start(f32[1024,256]{1,0:T(8,128)S(1)} %get-tuple-element.60), channel_id=1, source_target_pairs={{0,64},{64,0},{1,65},{65,1},{2,66},{66,2},{3,67},{67,3},{4,68},{68... | collective-permute-start | bytes 3145736 | tf_op jit(solution)/shard_map/ppermute | solution.py:21
  93.5 3.0 %copy-start.29 = (f32[1024,256]{1,0:T(8,128)}, f32[1024,256]{1,0:T(8,128)S(1)}, u32[]{:S(2)}) copy-start(f32[1024,256]{1,0:T(8,128)S(1)} %project.7) | copy-start | bytes 3145732
  96.4 0.9 copy-start.9
  97.3 41.9 %all-to-all-start = ((bf16[16,16,1280]{2,1,0:T(8,128)(2,1)}), bf16[16,16,1280]{2,1,0:T(8,128)(2,1)}, u32[]{:S(2)}, u32[]{:S(2)}) async-start(bf16[16,16,1280]{2,1,0:T(8,128)(2,1)} %bitcast.59), calls=%async_computation | async-start | bytes 1310720 | tf_op jit(solution)/shard_map/all_to_all | solution.py:138
  105.9 33.2 %collective-permute-start.15 = (f32[1024,256]{1,0:T(8,128)}, f32[1024,256]{1,0:T(8,128)}, u32[]{:S(2)}, u32[]{:S(2)}) collective-permute-start(f32[1024,256]{1,0:T(8,128)} %copy-done.47), channel_id=1, source_target_pairs={{0,64},{64,0},{1,65},{65,1},{2,66},{66,2},{3,67},{67,3},{4,68},{68... | collective-permute-start | bytes 3145736 | tf_op jit(solution)/shard_map/ppermute | solution.py:21
  106.7 32.5 %collective-permute-start.14 = (f32[1024,256]{1,0:T(8,128)}, f32[1024,256]{1,0:T(8,128)}, u32[]{:S(2)}, u32[]{:S(2)}) collective-permute-start(f32[1024,256]{1,0:T(8,128)} %copy-done.29), channel_id=1, source_target_pairs={{0,128},{128,0},{1,129},{129,1},{2,130},{130,2},{3,131},{131,3},{4... | collective-permute-start | bytes 3145736 | tf_op jit(solution)/shard_map/ppermute | solution.py:21
  107.5 15.7 %collective-permute-start.16 = (bf16[272,1152]{1,0:T(8,128)(2,1)}, bf16[272,1152]{1,0:T(8,128)(2,1)S(1)}, u32[]{:S(2)}, u32[]{:S(2)}) collective-permute-start(bf16[272,1152]{1,0:T(8,128)(2,1)} %copy-done.51), channel_id=1, source_target_pairs={{0,16},{16,0},{32,48},{48,32},{1,17},{17,1},{33,49},{49,33},{2,18}... | collective-permute-start | bytes 1880072 | tf_op jit(solution)/shard_map/ppermute | solution.py:21
  107.5 28.7 %collective-permute-start.17 = (bf16[272,1152]{1,0:T(8,128)(2,1)}, bf16[272,1152]{1,0:T(8,128)(2,1)S(1)}, u32[]{:S(2)}, u32[]{:S(2)}) collective-permute-start(bf16[272,1152]{1,0:T(8,128)(2,1)} %copy-done.50), channel_id=1, source_target_pairs={{0,32},{16,48},{32,0},{48,16},{1,33},{17,49},{33,1},{49,17},{2,34}... | collective-permute-start | bytes 1880072 | tf_op jit(solution)/shard_map/ppermute | solution.py:21
  108.7 29.6 %collective-permute-start.18 = (bf16[272,1152]{1,0:T(8,128)(2,1)}, bf16[272,1152]{1,0:T(8,128)(2,1)S(1)}, u32[]{:S(2)}, u32[]{:S(2)}) collective-permute-start(bf16[272,1152]{1,0:T(8,128)(2,1)} %copy-done.49), channel_id=1, source_target_pairs={{0,48},{16,32},{32,16},{48,0},{1,49},{17,33},{33,17},{49,1},{2,50}... | collective-permute-start | bytes 1880072 | tf_op jit(solution)/shard_map/ppermute | solution.py:21
  111.4 1.7 copy-start.2
  113.0 1.0 copy-start.20
  114.1 1.0 copy-start.22
  115.1 1.0 copy-start.24
  119.7 2.2 %copy-start.7 = (f32[1024,1152]{1,0:T(8,128)}, f32[1024,1152]{1,0:T(8,128)S(1)}, u32[]{:S(2)}) copy-start(f32[1024,1152]{1,0:T(8,128)S(1)} %back.2.refs_0_) | copy-start | bytes 14155780
  139.2 1.7 copy-start.4
  143.0 1.0 copy-start.48
  144.0 6.7 %copy-start.26 = (f32[256,1152]{1,0:T(8,128)S(1)}, f32[256,1152]{1,0:T(8,128)}, u32[]{:S(2)}) copy-start(f32[256,1152]{1,0:T(8,128)} %copy-done.25) | copy-start | bytes 3538948
  144.0 6.7 %copy-start.35 = (bf16[272,1152]{1,0:T(8,128)(2,1)S(1)}, bf16[272,1152]{1,0:T(8,128)(2,1)}, u32[]{:S(2)}) copy-start(bf16[272,1152]{1,0:T(8,128)(2,1)} %copy-done.34) | copy-start | bytes 1880068
  144.0 6.7 %copy-start.39 = (bf16[272,1152]{1,0:T(8,128)(2,1)S(1)}, bf16[272,1152]{1,0:T(8,128)(2,1)}, u32[]{:S(2)}) copy-start(bf16[272,1152]{1,0:T(8,128)(2,1)} %copy-done.38) | copy-start | bytes 1880068
  144.0 6.7 %copy-start.41 = (bf16[272,1152]{1,0:T(8,128)(2,1)S(1)}, bf16[272,1152]{1,0:T(8,128)(2,1)}, u32[]{:S(2)}) copy-start(bf16[272,1152]{1,0:T(8,128)(2,1)} %copy-done.40) | copy-start | bytes 1880068
  144.0 4.2 %collective-permute-start.19 = (f32[1024,256]{1,0:T(8,128)S(1)}, f32[1024,256]{1,0:T(8,128)S(1)}, u32[]{:S(2)}, u32[]{:S(2)}) collective-permute-start(f32[1024,256]{1,0:T(8,128)S(1)} %get-tuple-element.72), channel_id=1, source_target_pairs={{0,64},{64,0},{1,65},{65,1},{2,66},{66,2},{3,67},{67,3},{4,68},{68... | collective-permute-start | bytes 3145736 | tf_op jit(solution)/shard_map/ppermute | solution.py:21
  150.7 3.0 %copy-start.42 = (bf16[1088,256]{1,0:T(8,128)(2,1)}, bf16[1088,256]{1,0:T(8,128)(2,1)S(1)}, u32[]{:S(2)}) copy-start(bf16[1088,256]{1,0:T(8,128)(2,1)S(1)} %project.9) | copy-start | bytes 1671172
  154.5 31.8 %all-to-all-start.1 = ((bf16[16,16,1280]{2,1,0:T(8,128)(2,1)}), bf16[16,16,1280]{2,1,0:T(8,128)(2,1)S(1)}, u32[]{:S(2)}, u32[]{:S(2)}) async-start(bf16[16,16,1280]{2,1,0:T(8,128)(2,1)} %bitcast.60), calls=%async_computation.1 | async-start | bytes 1310720 | tf_op jit(solution)/shard_map/all_to_all | solution.py:138
  164.3 23.3 %collective-permute-start.21 = (f32[1024,256]{1,0:T(8,128)}, f32[1024,256]{1,0:T(8,128)}, u32[]{:S(2)}, u32[]{:S(2)}) collective-permute-start(f32[1024,256]{1,0:T(8,128)} %copy-done.48), channel_id=1, source_target_pairs={{0,64},{64,0},{1,65},{65,1},{2,66},{66,2},{3,67},{67,3},{4,68},{68... | collective-permute-start | bytes 3145736 | tf_op jit(solution)/shard_map/ppermute | solution.py:21
  165.0 20.4 %collective-permute-start.20 = (bf16[1088,256]{1,0:T(8,128)(2,1)}, bf16[1088,256]{1,0:T(8,128)(2,1)S(1)}, u32[]{:S(2)}, u32[]{:S(2)}) collective-permute-start(bf16[1088,256]{1,0:T(8,128)(2,1)} %copy-done.42), channel_id=1, source_target_pairs={{0,128},{128,0},{1,129},{129,1},{2,130},{130,2},{3,131},{131,3},{4... | collective-permute-start | bytes 1671176 | tf_op jit(solution)/shard_map/ppermute | solution.py:21
  168.1 1.7 copy-start.3
  187.6 1.7 copy-start.5
  189.3 1.1 copy-start.44
  190.3 3.0 %copy-start.12 = (bf16[1024,256]{1,0:T(8,128)(2,1)S(1)}, bf16[1024,256]{1,0:T(8,128)(2,1)}, u32[]{:S(2)}) copy-start(bf16[1024,256]{1,0:T(8,128)(2,1)} %copy-done.11) | copy-start | bytes 1572868
  193.3 2.2 %copy-start.46 = (f32[16,1152]{1,0:T(8,128)S(1)}, f32[16,1152]{1,0:T(8,128)}, u32[]{:S(2)}) copy-start(f32[16,1152]{1,0:T(8,128)} %copy-done.45) | copy-start | bytes 221188
  193.3 2.9 %copy-start.6 = (bf16[1024,1152]{1,0:T(8,128)(2,1)S(1)}, bf16[1024,1152]{1,0:T(8,128)(2,1)}, u32[]{:S(2)}) copy-start(bf16[1024,1152]{1,0:T(8,128)(2,1)} %all-gather.5.cloned.1.call-done) | copy-start | bytes 7077892
  193.3 2.9 %copy-start.14 = (bf16[1024,256]{1,0:T(8,128)(2,1)S(1)}, bf16[1024,256]{1,0:T(8,128)(2,1)}, u32[]{:S(2)}) copy-start(bf16[1024,256]{1,0:T(8,128)(2,1)} %copy-done.13) | copy-start | bytes 1572868
  193.3 2.9 %copy-start.16 = (bf16[1024,256]{1,0:T(8,128)(2,1)S(1)}, bf16[1024,256]{1,0:T(8,128)(2,1)}, u32[]{:S(2)}) copy-start(bf16[1024,256]{1,0:T(8,128)(2,1)} %copy-done.15) | copy-start | bytes 1572868
  193.3 2.9 %copy-start.18 = (bf16[1024,256]{1,0:T(8,128)(2,1)S(1)}, bf16[1024,256]{1,0:T(8,128)(2,1)}, u32[]{:S(2)}) copy-start(bf16[1024,256]{1,0:T(8,128)(2,1)} %copy-done.17) | copy-start | bytes 1572868
  196.2 2.3 %copy-start.8 = (f32[1024,1152]{1,0:T(8,128)S(1)}, f32[1024,1152]{1,0:T(8,128)}, u32[]{:S(2)}) copy-start(f32[1024,1152]{1,0:T(8,128)} %copy-done.7) | copy-start | bytes 14155780
  (14 other events, 11.5 us)
Sparse Core Ops, SparseCore 0:
  26.2 40.1 all-gather.2
  68.2 40.4 all-gather.4

commit v3 on v2

v3 whole, which is shorter than its diff:
```python
import functools

import jax
import jax.numpy as jnp
from jax import lax
from jax.experimental import pallas as pl
from jax.experimental.pallas import tpu as pltpu
from jax.sharding import Mesh, PartitionSpec as P

MP = ("y", "z", "xh")
DP = ("xl", "core")
F32 = jnp.float32
BF16 = jnp.bfloat16
SMEM = pl.BlockSpec(memory_space=pltpu.SMEM)
COST = pl.CostEstimate(flops=1, bytes_accessed=1, transcendentals=0)
VMEM = pl.BlockSpec(memory_space=pltpu.VMEM)


def flip(x, axis, bits):
    n = lax.axis_size(axis)
    return lax.ppermute(x, axis, [(i, i ^ bits) for i in range(n)])


def put(x, piece, i):
    return lax.dynamic_update_index_in_dim(x, piece, i, 0)


def hold(*xs):
    return lax.optimization_barrier(xs)


def room(mib):
    return pltpu.CompilerParams(vmem_limit_bytes=mib * 2**20)


def shape(dims, dtype):
    return jax.ShapeDtypeStruct(dims, dtype)


def exponent(largest):
    return jnp.floor(jnp.log(jnp.maximum(largest, 1e-30)) * 1.4426950408889634)


def encode(x, e):
    u = x * jnp.exp2(13.0 - e)
    u2 = u * u
    return (u * jnp.abs(u) * u2 * (u2 * u2)).astype(BF16)


def decode(w, e):
    w = w.astype(F32)
    fourth = lax.rsqrt(lax.rsqrt(jnp.maximum(jnp.abs(w), 1e-37)))
    u = fourth * lax.rsqrt(fourth)
    return jnp.where(w > 0, u, jnp.where(w < 0, -u, 0.0)) * jnp.exp2(e - 13.0)


def largest_of(ref):
    return jnp.max(ref[...], axis=(0, 1), keepdims=True)


def grad_kernel(u_ref, p0, p1, p2, p3, tok, own, s1, s2, s3, acc, top):
    u = u_ref[0]
    top[...] = jnp.zeros_like(top)
    for r, p in enumerate((p0, p1, p2, p3)):
        g = lax.dot_general(p[...], tok[...], (((0,), (0,)), ((), ())), preferred_element_type=F32)
        acc[r ^ u] = g
        top[...] = jnp.maximum(top[...], jnp.max(jnp.abs(g).reshape(32, 8, 1152), axis=0))
    e = exponent(largest_of(top))
    own[...] = acc[0]
    for i, s in ((1, s1), (2, s2), (3, s3)):

        @pl.loop(0, 16)
        def _(j):
            rows = pl.ds(pl.multiple_of(j * 16, 16), 16)
            s[rows, :] = encode(acc[i, rows, :], e)

        s[256:272, :] = jnp.broadcast_to(e, (16, 1152)).astype(BF16)


def grad(u, pieces, tokens):
    return pl.pallas_call(
        grad_kernel,
        out_shape=[shape((256, 1152), F32)] + [shape((272, 1152), BF16)] * 3,
        in_specs=[SMEM] + [VMEM] * 5,
        out_specs=[VMEM] * 4,
        scratch_shapes=[pltpu.VMEM((4, 256, 1152), F32), pltpu.VMEM((8, 1152), F32)],
        compiler_params=room(16),
        cost_estimate=COST,
        name="grad",
    )(u, *pieces, tokens)


def sum_kernel(*refs):
    groups, out, acc, top = (refs[:4], refs[4:8]), refs[8], refs[9], refs[10]
    for k, (own, *received) in enumerate(groups):
        top[...] = jnp.zeros_like(top)
        es = [r[256:257, 0:1].astype(F32) for r in received]

        @pl.loop(0, 16)
        def _(j):
            rows = pl.ds(pl.multiple_of(j * 16, 16), 16)
            x = own[rows, :]
            for r, e in zip(received, es):
                x = x + decode(r[rows, :], e)
            acc[rows, :] = x
            top[...] = jnp.maximum(top[...], jnp.abs(x))

        e = exponent(largest_of(top))

        @pl.loop(0, 16)
        def _(j):
            rows = pl.ds(pl.multiple_of(j * 16, 16), 16)
            to = pl.ds(pl.multiple_of(j * 32 + k * 16, 16), 16)
            out[to, :1152] = encode(acc[rows, :], e)
            out[to, 1152:] = jnp.broadcast_to(e, (16, 128)).astype(BF16)


def sum_over_y(*groups):
    return pl.pallas_call(
        sum_kernel,
        out_shape=shape((512, 1280), BF16),
        in_specs=[VMEM] * 8,
        out_specs=VMEM,
        scratch_shapes=[pltpu.VMEM((256, 1152), F32), pltpu.VMEM((16, 1152), F32)],
        compiler_params=room(6),
        cost_estimate=COST,
        name="sum_over_y",
    )(*groups)


def final_kernel(x, out):
    out[...] = jnp.zeros_like(out)

    @pl.loop(0, 16)
    def _(j):
        rows = pl.ds(pl.multiple_of(j * 32, 32), 32)
        out[...] += decode(x[rows, :1152], x[rows, 1152:1153].astype(F32))


def spread(x):
    return lax.all_to_all(x.reshape(16, 32, 1280), ("z", "xh"), 0, 0, tiled=True)


def sum_over_z(x):
    return pl.pallas_call(
        final_kernel,
        out_shape=shape((32, 1152), F32),
        in_specs=[VMEM],
        out_specs=VMEM,
        compiler_params=room(4),
        cost_estimate=COST,
        name="sum_over_z",
    )(x.reshape(512, 1280))


def encode12(x):
    e = exponent(jnp.max(jnp.abs(x), axis=(0, 1), keepdims=True))
    a = jnp.maximum(jnp.abs(x) * jnp.exp2(-e), 1e-30)
    w = jnp.exp2(12.0 * (jnp.log(a) * 1.4426950408889634) + 100.0)
    return jnp.where(x < 0, -w, w).astype(BF16), jnp.broadcast_to(e, (16, 256)).astype(BF16)


def decode12(w, e):
    w = w.astype(F32)
    a = jnp.maximum(jnp.abs(w), 1e-37)
    x = jnp.exp2((jnp.log(a) * 1.4426950408889634 - 100.0) * (1.0 / 12.0) + e)
    return jnp.where(w > 0, x, jnp.where(w < 0, -x, 0.0))


def product(tok, w, rows, r, k):
    columns = w[:, r, k].reshape(256, 1152)
    return lax.dot_general(
        tok[rows, :], columns, (((1,), (1,)), ((), ())), preferred_element_type=F32
    )


def each_block(body):
    for k in range(2):

        @pl.loop(0, 4)
        def _(j):
            i = j + 4 * k
            body(
                k,
                pl.ds(pl.multiple_of(j * 256, 256), 256),
                pl.ds(pl.multiple_of(i * 256, 256), 256),
                pl.ds(pl.multiple_of(i * 272, 16), 272),
            )


def beside_kernel(tok, w, to_far, to_near):
    def body(k, tokens, rows, coded):
        to_far[rows, :] = product(tok, w, tokens, 3, k)
        to_near[rows, :] = product(tok, w, tokens, 1, k)

    each_block(body)


def far_kernel(tok, w, got, out):
    def body(k, tokens, rows, coded):
        x = product(tok, w, tokens, 2, k) + got[rows, :]
        out[coded, :] = jnp.concatenate(encode12(x), axis=0)

    each_block(body)


def near_kernel(tok, w, got, across, out_k, out_v):
    def body(k, tokens, rows, coded):
        c = across[coded, :]
        x = product(tok, w, tokens, 0, k) + got[rows, :]
        x = x + decode12(c[:256], c[256:257, 0:1].astype(F32))
        (out_k, out_v)[k][tokens, :] = x.astype(BF16)

    each_block(body)


def project(kernel, outs, *args):
    return pl.pallas_call(
        kernel,
        out_shape=outs,
        in_specs=[VMEM] * len(args),
        out_specs=[VMEM] * len(outs),
        compiler_params=room(8),
        cost_estimate=COST,
        name=kernel.__name__,
    )(*args)


def back_kernel(*refs):
    pieces, w, out = refs[:8], refs[8], refs[9]
    flat = jnp.concatenate(
        [w[:, r, k].reshape(256, 1152) for k in range(2) for r in range(4)], axis=0
    )

    @pl.loop(0, 4)
    def _(j):
        rows = pl.ds(pl.multiple_of(j * 256, 256), 256)
        x = jnp.concatenate([p[rows, :] for p in pieces], axis=1)
        out[rows, :] = jnp.dot(x, flat, preferred_element_type=F32).astype(BF16)


def back(pieces, w):
    return pl.pallas_call(
        back_kernel,
        out_shape=shape((1024, 1152), BF16),
        in_specs=[VMEM] * 9,
        out_specs=VMEM,
        compiler_params=room(16),
        cost_estimate=COST,
        name="back",
    )(*pieces, w)


def per_device(tokens, kv_weight, d_kv):
    xl, core, y, xh = (lax.axis_index(a) for a in ("xl", "core", "y", "xh"))
    dp = 2 * xl + core
    u = (dp ^ y).reshape(1)

    own_k, own_v = d_kv[:, 0], d_kv[:, 1]
    wt = jnp.transpose(kv_weight, (0, 2, 1))

    both = put(put(jnp.zeros((2, *wt.shape), BF16), wt, xh), flip(wt, "xh", 1), xh ^ 1)
    both = jnp.transpose(both, (1, 0, 2, 3)).reshape(2, 32, 1152)
    beside_k, beside_v = flip(own_k, "core", 1), flip(own_v, "core", 1)
    both, own_k, own_v = hold(both, own_k, own_v)

    first = flip(own_k[:512], "xl", 1)
    got_w = [flip(both, "y", bits) for bits in (1, 2, 3)]
    first, second, both, *got_w = hold(first, own_k[512:], both, *got_w)
    second = flip(second, "xl", 1)
    w = put(jnp.zeros((4, 2, 32, 1152), BF16), both, y ^ dp)
    for bits, piece in zip((1, 2, 3), got_w):
        w = put(w, piece, y ^ bits ^ dp)
    w = lax.all_gather(w.reshape(256, 1152), "z", axis=0, tiled=True).reshape(8, 4, 2, 32, 1152)
    second, own_v = hold(second, own_v)

    across_v = flip(own_v, "xl", 1)
    across_k = jnp.concatenate([first, second])
    corner_k = flip(across_k, "core", 1)
    gk, *send_k = grad(u, (own_k, beside_k, across_k, corner_k), tokens)
    got_k = [flip(s, "y", bits) for s, bits in zip(send_k, (1, 2, 3))]
    across_v, gk = hold(across_v, gk)
    corner_v = flip(across_v, "core", 1)
    gv, *send_v = grad(u, (own_v, beside_v, across_v, corner_v), tokens)
    got_v = [flip(s, "y", bits) for s, bits in zip(send_v, (1, 2, 3))]
    gk, gv, w, got_v[1], *got_k = hold(gk, gv, w, got_v[1], *got_k)

    both_cores = shape((2048, 256), F32)
    to_far, to_near = project(beside_kernel, [both_cores] * 2, tokens, w)
    got_far, got_near = flip(to_far, "core", 1), flip(to_near, "core", 1)
    got_far, got_near, gk, gv, *got = hold(got_far, got_near, gk, gv, *got_k, *got_v)
    total = spread(sum_over_y(gk, *got[:3], gv, *got[3:]))
    (far,) = project(far_kernel, [shape((2176, 256), BF16)], tokens, w, got_far)
    across = flip(far, "xl", 1)
    d_tokens = back(
        (own_k, beside_k, across_k, corner_k, own_v, beside_v, across_v, corner_v), w
    )
    total, across, d_tokens, got_near = hold(total, across, d_tokens, got_near)
    out_k, out_v = project(
        near_kernel, [shape((1024, 256), BF16)] * 2, tokens, w, got_near, across
    )
    grads = sum_over_z(total).reshape(2, 16, 1152)
    kv_out = jnp.stack([out_k, out_v], axis=1)
    grad_kv = jnp.transpose(grads, (0, 2, 1))
    return (kv_out, d_tokens, grad_kv)


def solution(mesh):
    fine = Mesh(mesh.devices.reshape(2, 2, 4, 8, 2), DP + MP)
    return jax.shard_map(
        per_device,
        mesh=fine,
        in_specs=(P(MP, DP), P(None, DP, MP), P(MP, None, DP)),
        out_specs=(P(MP, None, DP), P(MP, DP), P(None, DP, MP)),
        check_vma=False,
    )
```

time: 211 us -> 217 us (1.028)
  waiting for transfers between devices: 65.4 us -> 90.6 us
  starting transfers between devices: 47.6 us -> 35.5 us
  local copies, waits for them, and re-layouts: 40.9 us -> 37 us
  Pallas kernels: 41.1 us -> 38.4 us
    ppermute x22 -> x20, waiting for transfers between devices: 64.7 us -> 90.6 us  [flip(): return lax.ppermute(x, axis, [(i, i ^ bits) for i in range(n)])]
    unnamed x107 -> x86, local copies, waits for them, and re-layouts: 35.6 us -> 25.7 us
    all_to_all x2 -> x1, starting transfers between devices: 18.4 us -> 9.92 us  [spread(): lax.all_to_all(x.reshape(16, 32, 1280), ('z', 'xh'), 0, 0, tiled=True)]
    dynamic_update_slice x7 -> x6, local copies, waits for them, and re-layouts: 1.07 us -> 6.33 us  [put(): return lax.dynamic_update_index_in_dim(x, piece, i, 0)]
    ppermute x22 -> x20, starting transfers between devices: 29.1 us -> 25.5 us  [flip(): return lax.ppermute(x, axis, [(i, i ^ bits) for i in range(n)])]
    pallas_call x12 -> x6, Pallas kernels: 32.5 us -> 29.7 us  [the longest x3 12.6 us: project(): pl.pallas_call(kernel, out_shape=outs, in_specs=[VMEM] * len(args), out_s...]
  transfers between devices with their start and end apart: 26 -> 22, of which waited for: 13 -> 8; matrix products, arithmetic and copies ran while one was open for 2% -> 2% of each run, Pallas kernels for 12% -> 10%
where the time goes in v3:
time: 217 us; the launch traced here: 216 us
  waiting for transfers between devices  90.6 us (42%)
  Pallas kernels  38.4 us (18%)
  local copies, waits for them, and re-layouts  37 us (17%)
  starting transfers between devices  35.5 us (16%)
  between operations  14.5 us (7%)
    ppermute x20, waiting for transfers between devices, flip(): return lax.ppermute(x, axis, [(i, i ^ bits) for i in range(n)])  90.6 us
    unnamed x86, local copies, waits for them, and re-layouts  25.7 us
    ppermute x20, starting transfers between devices, flip(): return lax.ppermute(x, axis, [(i, i ^ bits) for i in range(n)])  25.5 us
    pallas_call x3, Pallas kernels, project(): pl.pallas_call(kernel, out_shape=outs, in_specs=[VMEM] * len(args), out_s...  12.6 us
    all_to_all x1, starting transfers between devices, spread(): lax.all_to_all(x.reshape(16, 32, 1280), ('z', 'xh'), 0, 0, tiled=True)  9.92 us
    pallas_call x2, Pallas kernels, grad(): pl.pallas_call(grad_kernel, out_shape=[shape((256, 1152), F32)] + [shape(...  8.68 us
    pallas_call x1, Pallas kernels, back(): pl.pallas_call(back_kernel, out_shape=shape((1024, 1152), BF16), in_specs...  7.8 us
    dynamic_update_slice x6, local copies, waits for them, and re-layouts, put(): return lax.dynamic_update_index_in_dim(x, piece, i, 0)  6.33 us
  transfers between devices with their start and end apart: 22, of which 8 were waited for; matrix products, arithmetic and copies ran while one was open for 2% of the time, Pallas kernels for 10%

profile of v3, /device:TPU:1, one launch (start us, length us, event | category | flops | bytes accessed | tf_op | source)
XLA Modules:
  0.0 216.1 jit_solution(4778576966262183682)
XLA Ops:
  7.2 3.7 %collective-permute-start = (bf16[2,16,1152]{2,1,0:T(8,128)(2,1)}, bf16[2,16,1152]{2,1,0:T(8,128)(2,1)S(1)}, u32[]{:S(2)}, u32[]{:S(2)}) collective-permute-start(bf16[2,16,1152]{2,1,0:T(8,128)(2,1)} %bitcast.57), channel_id=1, source_target_pairs={{0,1},{1,0},{2,3},{3,2},{4,5},{5,4},{6,7},{7,6},{8,9},{9,8},{10,11... | collective-permute-start | bytes 221192 | tf_op jit(solution)/shard_map/ppermute | solution.py:21
  10.9 0.9 bitcast_dynamic-update-slice_fusion.4
  11.8 3.3 %fusion = (bf16[1024,1,256]{2,1,0:T(2,128)(2,1)S(1)}, bf16[1024,1,256]{2,1,0:T(2,128)(2,1)S(1)}) fusion(bf16[1024,2,256]{2,1,0:T(2,128)(2,1)} %param.5), kind=kLoop, calls=%fused_computation.11 | loop fusion | bytes 2097152 | tf_op jit(solution)/shard_map/slice | solution.py:259
  15.1 0.1 copy.17
  15.4 0.8 fusion.1
  16.2 0.3 collective-permute-start.1
  16.5 2.7 %collective-permute-start.4 = (bf16[2,32,1152]{2,1,0:T(8,128)(2,1)S(1)}, bf16[2,32,1152]{2,1,0:T(8,128)(2,1)}, u32[]{:S(2)}, u32[]{:S(2)}) collective-permute-start(bf16[2,32,1152]{2,1,0:T(8,128)(2,1)S(1)} %bitcast.52), channel_id=1, source_target_pairs={{0,48},{16,32},{32,16},{48,0},{1,49},{17,33},{33,17},{49,1},{2,50}... | collective-permute-start | bytes 442376 | tf_op jit(solution)/shard_map/ppermute | solution.py:21
  19.2 0.3 collective-permute-start.3
  19.6 0.2 collective-permute-start.2
  19.8 5.6 %collective-permute-done.4 = bf16[2,32,1152]{2,1,0:T(8,128)(2,1)} collective-permute-done((bf16[2,32,1152]{2,1,0:T(8,128)(2,1)S(1)}, bf16[2,32,1152]{2,1,0:T(8,128)(2,1)}, u32[]{:S(2)}, u32[]{:S(2)}) %collective-permute-start.4) | collective-permute-done | bytes 147488 | tf_op jit(solution)/shard_map/ppermute | solution.py:21
  25.5 0.9 broadcast_in_dim.29
  26.3 0.7 bitcast_dynamic-update-slice_fusion.3
  27.0 1.6 bitcast_dynamic-update-slice_fusion.2
  28.6 1.6 bitcast_dynamic-update-slice_fusion.1
  30.1 1.6 bitcast_dynamic-update-slice_fusion
  31.7 1.2 collective-permute-start.5
  33.0 3.6 %collective-permute-start.7 = (bf16[1024,256]{1,0:T(8,128)(2,1)S(1)}, bf16[1024,256]{1,0:T(8,128)(2,1)S(1)}, u32[]{:S(2)}, u32[]{:S(2)}) collective-permute-start(bf16[1024,256]{1,0:T(8,128)(2,1)S(1)} %bitcast.42), channel_id=1, source_target_pairs={{0,64},{64,0},{1,65},{65,1},{2,66},{66,2},{3,67},{67,3},{4,68},{68... | collective-permute-start | bytes 1572872 | tf_op jit(solution)/shard_map/ppermute | solution.py:21
  36.5 1.0 constant_dynamic-update-slice_fusion.1
  37.6 4.3 %collective-permute-start.8 = (bf16[1024,256]{1,0:T(8,128)(2,1)S(1)}, bf16[1024,256]{1,0:T(8,128)(2,1)S(1)}, u32[]{:S(2)}, u32[]{:S(2)}) collective-permute-start(bf16[1024,256]{1,0:T(8,128)(2,1)S(1)} %constant_dynamic-update-slice_fusion.p2.refs_2_), channel_id=1, source_target_pairs={{0,64},{64,0},{1,65},{65,1},{2,66},{66,2},{3,67},{67,3},{4,68},{68... | collective-permute-start | bytes 1572872 | tf_op jit(solution)/shard_map/ppermute | solution.py:21
  41.8 1.2 collective-permute-start.6
  43.0 0.4 collective-permute-start.9
  43.4 4.3 %grad.2 = (f32[256,1152]{1,0:T(8,128)S(1)}, bf16[272,1152]{1,0:T(8,128)(2,1)S(1)}, bf16[272,1152]{1,0:T(8,128)(2,1)S(1)}, bf16[272,1152]{1,0:T(8,128)(2,1)S(1)}) custom-call(s32[1]{0:T(128)} %bitcast.8.u_ref, bf16[1024,256]{1,0:T(8,128)(2,1)S(1)} %bitcast.43, bf16[1024,256]{1,0:T(8,128)(2,1)S(1)} %collective-permute-done.7.p1.refs_1_, ...), custom_call_target="tpu_custom_call" | custom-call | flops 1 | bytes 1 | tf_op jit(solution)/shard_map/grad/pallas_call | solution.py:81
  47.8 1.1 copy-done.23
  48.9 6.5 %collective-permute-done.6.p2.refs_6_ = bf16[1024,256]{1,0:T(8,128)(2,1)S(1)} collective-permute-done((bf16[1024,256]{1,0:T(8,128)(2,1)S(1)}, bf16[1024,256]{1,0:T(8,128)(2,1)S(1)}, u32[]{:S(2)}, u32[]{:S(2)}) %collective-permute-start.6) | collective-permute-done | bytes 524320 | tf_op jit(solution)/shard_map/ppermute | solution.py:21
  55.4 0.8 collective-permute-start.10
  56.2 0.4 collective-permute-start.12
  56.6 3.5 %collective-permute-start.13 = (bf16[272,1152]{1,0:T(8,128)(2,1)S(1)}, bf16[272,1152]{1,0:T(8,128)(2,1)S(1)}, u32[]{:S(2)}, u32[]{:S(2)}) collective-permute-start(bf16[272,1152]{1,0:T(8,128)(2,1)S(1)} %get-tuple-element.66), channel_id=1, source_target_pairs={{0,32},{16,48},{32,0},{48,16},{1,33},{17,49},{33,1},{49,17},{2,34}... | collective-permute-start | bytes 1880072 | tf_op jit(solution)/shard_map/ppermute | solution.py:21
  60.1 4.3 %grad.3 = (f32[256,1152]{1,0:T(8,128)S(1)}, bf16[272,1152]{1,0:T(8,128)(2,1)S(1)}, bf16[272,1152]{1,0:T(8,128)(2,1)S(1)}, bf16[272,1152]{1,0:T(8,128)(2,1)S(1)}) custom-call(s32[1]{0:T(128)} %bitcast.8.u_ref, bf16[1024,256]{1,0:T(8,128)(2,1)S(1)} %bitcast.48, bf16[1024,256]{1,0:T(8,128)(2,1)S(1)} %collective-permute-done.9.p1.refs_5_, ...), custom_call_target="tpu_custom_call" | custom-call | flops 1 | bytes 1 | tf_op jit(solution)/shard_map/grad/pallas_call | solution.py:81
  64.5 1.0 copy-done.25
  65.5 0.9 copy-done.35
  66.4 0.8 copy-done.37
  67.2 1.2 collective-permute-start.11
  68.4 3.7 %collective-permute-done.12.refs_1_ = bf16[272,1152]{1,0:T(8,128)(2,1)S(1)} collective-permute-done((bf16[272,1152]{1,0:T(8,128)(2,1)S(1)}, bf16[272,1152]{1,0:T(8,128)(2,1)S(1)}, u32[]{:S(2)}, u32[]{:S(2)}) %collective-permute-start.12) | collective-permute-done | bytes 626720 | tf_op jit(solution)/shard_map/ppermute | solution.py:21
  72.0 0.8 copy-done.29
  72.9 15.0 %collective-permute-done.13.refs_2_ = bf16[272,1152]{1,0:T(8,128)(2,1)S(1)} collective-permute-done((bf16[272,1152]{1,0:T(8,128)(2,1)S(1)}, bf16[272,1152]{1,0:T(8,128)(2,1)S(1)}, u32[]{:S(2)}, u32[]{:S(2)}) %collective-permute-start.13) | collective-permute-done | bytes 626720 | tf_op jit(solution)/shard_map/ppermute | solution.py:21
  87.8 0.9 copy-done.31
  88.7 14.6 %collective-permute-done.14.refs_3_ = bf16[272,1152]{1,0:T(8,128)(2,1)S(1)} collective-permute-done((bf16[272,1152]{1,0:T(8,128)(2,1)S(1)}, bf16[272,1152]{1,0:T(8,128)(2,1)S(1)}, u32[]{:S(2)}, u32[]{:S(2)}) %collective-permute-start.14) | collective-permute-done | bytes 626720 | tf_op jit(solution)/shard_map/ppermute | solution.py:21
  103.3 0.8 copy-done.33
  104.1 2.3 %copy-done = bf16[2048,1152]{1,0:T(8,128)(2,1)S(1)} copy-done((bf16[2048,1152]{1,0:T(8,128)(2,1)S(1)}, bf16[2048,1152]{1,0:T(8,128)(2,1)}, u32[]{:S(2)}) %copy-start) | copy-done | bytes 4718616
  106.5 4.3 %beside_kernel.1 = (f32[2048,256]{1,0:T(8,128)S(1)}, f32[2048,256]{1,0:T(8,128)S(1)}) custom-call(bf16[1024,1152]{1,0:T(8,128)(2,1)S(1)} %copy-done.3, bf16[8,4,2,32,1152]{4,3,2,1,0:T(8,128)(2,1)S(1)} %bitcast.35), custom_call_target="tpu_custom_call" | custom-call | flops 1 | bytes 1 | tf_op jit(solution)/shard_map/beside_kernel/pallas_call | solution.py:218
  110.8 1.5 collective-permute-start.15
  112.3 0.1 collective-permute-start.16
  112.4 0.1 collective-permute-start.18
  112.5 15.2 %collective-permute-done.17.refs_5_ = bf16[272,1152]{1,0:T(8,128)(2,1)S(1)} collective-permute-done((bf16[272,1152]{1,0:T(8,128)(2,1)S(1)}, bf16[272,1152]{1,0:T(8,128)(2,1)S(1)}, u32[]{:S(2)}, u32[]{:S(2)}) %collective-permute-start.17) | collective-permute-done | bytes 626720 | tf_op jit(solution)/shard_map/ppermute | solution.py:21
  127.7 1.3 collective-permute-done.18.refs_7_
  129.0 1.3 copy-done.11
  130.3 1.3 copy-done.9
  131.7 5.8 %sum_over_y.1 = bf16[512,1280]{1,0:T(8,128)(2,1)S(1)} custom-call(f32[256,1152]{1,0:T(8,128)S(1)} %copy-done.24, bf16[272,1152]{1,0:T(8,128)(2,1)S(1)} %copy-done.30, bf16[272,1152]{1,0:T(8,128)(2,1)S(1)} %copy-done.32, bf16[272,1152]{1,0:T(8,128)(2,1)S(1)} %copy-done.34, f32[256,1152]{1,0:T(8,128)S(1)} %copy-done.26, ...), custom_call_target="tpu_custom_call" | custom-call | flops 1 | bytes 1 | tf_op jit(solution)/shard_map/sum_over_y/pallas_call | solution.py:119
  137.5 1.0 copy-done.4
  138.6 9.9 %all-to-all-start = ((bf16[16,32,1280]{2,1,0:T(8,128)(2,1)}), bf16[16,32,1280]{2,1,0:T(8,128)(2,1)}, u32[]{:S(2)}, u32[]{:S(2)}) async-start(bf16[16,32,1280]{2,1,0:T(8,128)(2,1)} %bitcast.45), calls=%async_computation | async-start | bytes 2621440 | tf_op jit(solution)/shard_map/all_to_all | solution.py:141
  148.5 2.3 %copy-done.1 = bf16[2048,1152]{1,0:T(8,128)(2,1)S(1)} copy-done((bf16[2048,1152]{1,0:T(8,128)(2,1)S(1)}, bf16[2048,1152]{1,0:T(8,128)(2,1)}, u32[]{:S(2)}) %copy-start.1) | copy-done | bytes 4718616
  150.8 1.6 copy-done.12
  152.5 5.0 %far_kernel.1 = bf16[2176,256]{1,0:T(8,128)(2,1)S(1)} custom-call(bf16[1024,1152]{1,0:T(8,128)(2,1)S(1)} %copy-done.3, bf16[8,4,2,32,1152]{4,3,2,1,0:T(8,128)(2,1)S(1)} %bitcast.36, f32[2048,256]{1,0:T(8,128)S(1)} %copy-done.12), custom_call_target="tpu_custom_call" | custom-call | flops 1 | bytes 1 | tf_op jit(solution)/shard_map/far_kernel/pallas_call | solution.py:218
  157.5 0.1 collective-permute-start.19
  157.7 7.8 %back.1 = bf16[1024,1152]{1,0:T(8,128)(2,1)} custom-call(bf16[1024,256]{1,0:T(8,128)(2,1)S(1)} %bitcast.44, bf16[1024,256]{1,0:T(8,128)(2,1)S(1)} %copy-done.14, bf16[1024,256]{1,0:T(8,128)(2,1)S(1)} %copy-done.8, bf16[1024,256]{1,0:T(8,128)(2,1)S(1)} %copy-done.16, bf16[1024,256]{1,0:T(8,128)(2,1)S(1)} %bitcast.49, bf16[1024,256]{1,0:T(8,128)(2,1)S(1)} %copy-done.20, ...), custom_call_target="tpu_custom_call" | custom-call | flops 1 | bytes 1 | tf_op jit(solution)/shard_map/back/pallas_call | solution.py:243
  165.5 28.7 %collective-permute-done.19.across = bf16[2176,256]{1,0:T(8,128)(2,1)S(1)} collective-permute-done((bf16[2176,256]{1,0:T(8,128)(2,1)S(1)}, bf16[2176,256]{1,0:T(8,128)(2,1)S(1)}, u32[]{:S(2)}, u32[]{:S(2)}) %collective-permute-start.19) | collective-permute-done | bytes 1114144 | tf_op jit(solution)/shard_map/ppermute | solution.py:21
  194.2 1.0 copy-done.27
  195.2 2.3 %copy-done.2 = bf16[2048,1152]{1,0:T(8,128)(2,1)S(1)} copy-done((bf16[2048,1152]{1,0:T(8,128)(2,1)S(1)}, bf16[2048,1152]{1,0:T(8,128)(2,1)}, u32[]{:S(2)}) %copy-start.2) | copy-done | bytes 4718616
  197.5 1.6 copy-done.10
  199.1 1.2 copy-done.28
  200.3 3.3 %near_kernel.1 = (bf16[1024,256]{1,0:T(8,128)(2,1)S(1)}, bf16[1024,256]{1,0:T(8,128)(2,1)S(1)}) custom-call(bf16[1024,1152]{1,0:T(8,128)(2,1)S(1)} %copy-done.3, bf16[8,4,2,32,1152]{4,3,2,1,0:T(8,128)(2,1)S(1)} %bitcast.40, f32[2048,256]{1,0:T(8,128)S(1)} %copy-done.10, bf16[2176,256]{1,0:T(8,128)(2,1)S(1)} %copy-done.28), custom_call_target="tpu_custom_call" | custom-call | flops 1 | bytes 1 | tf_op jit(solution)/shard_map/near_kernel/pallas_call | solution.py:218
  203.7 0.1 pad_maximum_fusion
  203.8 2.0 copy.12
  205.8 3.5 %sum_over_z.1 = f32[32,1152]{1,0:T(8,128)} custom-call(bf16[512,1280]{1,0:T(8,128)(2,1)} %bitcast.18.x), custom_call_target="tpu_custom_call" | custom-call | flops 1 | bytes 1 | tf_op jit(solution)/shard_map/sum_over_z/pallas_call | solution.py:145
  (88 shorter events, 0.4 us)
Async XLA Ops:
  7.2 97.0 %all-gather.2.cloned.1.call-start = ((), (), s32[]{:S(2)}) async-start(), calls=%async_computation.1 | async-start | bytes 5308416 | tf_op jit(solution)/shard_map/all_gather | solution.py:274
  7.2 8.1 %collective-permute-start = (bf16[2,16,1152]{2,1,0:T(8,128)(2,1)}, bf16[2,16,1152]{2,1,0:T(8,128)(2,1)S(1)}, u32[]{:S(2)}, u32[]{:S(2)}) collective-permute-start(bf16[2,16,1152]{2,1,0:T(8,128)(2,1)} %bitcast.57), channel_id=1, source_target_pairs={{0,1},{1,0},{2,3},{3,2},{4,5},{5,4},{6,7},{7,6},{8,9},{9,8},{10,11... | collective-permute-start | bytes 221192 | tf_op jit(solution)/shard_map/ppermute | solution.py:21
  15.2 44.9 %copy-start.5 = (bf16[1024,1,256]{2,0,1:T(8,128)(2,1)}, bf16[1024,1,256]{2,0,1:T(8,128)(2,1)S(1)}, u32[]{:S(2)}) copy-start(bf16[1024,1,256]{2,0,1:T(8,128)(2,1)S(1)} %copy.17) | copy-start | bytes 1572868
  15.3 28.0 %copy-start.3 = (bf16[1024,1152]{1,0:T(8,128)(2,1)S(1)}, bf16[1024,1152]{1,0:T(8,128)(2,1)}, u32[]{:S(2)}) copy-start(bf16[1024,1152]{1,0:T(8,128)(2,1)} %tok.9) | copy-start | bytes 7077892
  16.2 9.3 %collective-permute-start.1 = (bf16[512,256]{1,0:T(8,128)(2,1)}, bf16[512,256]{1,0:T(8,128)(2,1)}, u32[]{:S(2)}, u32[]{:S(2)}) collective-permute-start(bf16[512,256]{1,0:T(8,128)(2,1)} %get-tuple-element.104), channel_id=1, source_target_pairs={{0,128},{128,0},{1,129},{129,1},{2,130},{130,2},{3,131},{131,3},{4... | collective-permute-start | bytes 786440 | tf_op jit(solution)/shard_map/ppermute | solution.py:21
  16.5 9.0 %collective-permute-start.4 = (bf16[2,32,1152]{2,1,0:T(8,128)(2,1)S(1)}, bf16[2,32,1152]{2,1,0:T(8,128)(2,1)}, u32[]{:S(2)}, u32[]{:S(2)}) collective-permute-start(bf16[2,32,1152]{2,1,0:T(8,128)(2,1)S(1)} %bitcast.52), channel_id=1, source_target_pairs={{0,48},{16,32},{32,16},{48,0},{1,49},{17,33},{33,17},{49,1},{2,50}... | collective-permute-start | bytes 442376 | tf_op jit(solution)/shard_map/ppermute | solution.py:21
  19.2 6.2 %collective-permute-start.3 = (bf16[2,32,1152]{2,1,0:T(8,128)(2,1)S(1)}, bf16[2,32,1152]{2,1,0:T(8,128)(2,1)}, u32[]{:S(2)}, u32[]{:S(2)}) collective-permute-start(bf16[2,32,1152]{2,1,0:T(8,128)(2,1)S(1)} %bitcast.53), channel_id=1, source_target_pairs={{0,32},{16,48},{32,0},{48,16},{1,33},{17,49},{33,1},{49,17},{2,34}... | collective-permute-start | bytes 442376 | tf_op jit(solution)/shard_map/ppermute | solution.py:21
  19.6 5.9 %collective-permute-start.2 = (bf16[2,32,1152]{2,1,0:T(8,128)(2,1)S(1)}, bf16[2,32,1152]{2,1,0:T(8,128)(2,1)}, u32[]{:S(2)}, u32[]{:S(2)}) collective-permute-start(bf16[2,32,1152]{2,1,0:T(8,128)(2,1)S(1)} %bitcast.54), channel_id=1, source_target_pairs={{0,16},{16,0},{32,48},{48,32},{1,17},{17,1},{33,49},{49,33},{2,18}... | collective-permute-start | bytes 442376 | tf_op jit(solution)/shard_map/ppermute | solution.py:21
  31.7 5.8 %collective-permute-start.5 = (bf16[512,256]{1,0:T(8,128)(2,1)}, bf16[512,256]{1,0:T(8,128)(2,1)S(1)}, u32[]{:S(2)}, u32[]{:S(2)}) collective-permute-start(bf16[512,256]{1,0:T(8,128)(2,1)} %get-tuple-element.51), channel_id=1, source_target_pairs={{0,128},{128,0},{1,129},{129,1},{2,130},{130,2},{3,131},{131,3},{4... | collective-permute-start | bytes 786440 | tf_op jit(solution)/shard_map/ppermute | solution.py:21
  33.0 10.4 %collective-permute-start.7 = (bf16[1024,256]{1,0:T(8,128)(2,1)S(1)}, bf16[1024,256]{1,0:T(8,128)(2,1)S(1)}, u32[]{:S(2)}, u32[]{:S(2)}) collective-permute-start(bf16[1024,256]{1,0:T(8,128)(2,1)S(1)} %bitcast.42), channel_id=1, source_target_pairs={{0,64},{64,0},{1,65},{65,1},{2,66},{66,2},{3,67},{67,3},{4,68},{68... | collective-permute-start | bytes 1572872 | tf_op jit(solution)/shard_map/ppermute | solution.py:21
  37.5 10.2 %copy-start.7 = (bf16[1024,256]{1,0:T(8,128)(2,1)}, bf16[1024,256]{1,0:T(8,128)(2,1)S(1)}, u32[]{:S(2)}) copy-start(bf16[1024,256]{1,0:T(8,128)(2,1)S(1)} %constant_dynamic-update-slice_fusion.p2.refs_2_) | copy-start | bytes 1572868
  37.6 5.8 %collective-permute-start.8 = (bf16[1024,256]{1,0:T(8,128)(2,1)S(1)}, bf16[1024,256]{1,0:T(8,128)(2,1)S(1)}, u32[]{:S(2)}, u32[]{:S(2)}) collective-permute-start(bf16[1024,256]{1,0:T(8,128)(2,1)S(1)} %constant_dynamic-update-slice_fusion.p2.refs_2_), channel_id=1, source_target_pairs={{0,64},{64,0},{1,65},{65,1},{2,66},{66,2},{3,67},{67,3},{4,68},{68... | collective-permute-start | bytes 1572872 | tf_op jit(solution)/shard_map/ppermute | solution.py:21
  41.8 13.6 %collective-permute-start.6 = (bf16[1024,256]{1,0:T(8,128)(2,1)S(1)}, bf16[1024,256]{1,0:T(8,128)(2,1)S(1)}, u32[]{:S(2)}, u32[]{:S(2)}) collective-permute-start(bf16[1024,256]{1,0:T(8,128)(2,1)S(1)} %bitcast.46), channel_id=1, source_target_pairs={{0,128},{128,0},{1,129},{129,1},{2,130},{130,2},{3,131},{131,3},{4... | collective-permute-start | bytes 1572872 | tf_op jit(solution)/shard_map/ppermute | solution.py:21
  43.0 17.1 %collective-permute-start.9 = (bf16[1024,256]{1,0:T(8,128)(2,1)S(1)}, bf16[1024,256]{1,0:T(8,128)(2,1)S(1)}, u32[]{:S(2)}, u32[]{:S(2)}) collective-permute-start(bf16[1024,256]{1,0:T(8,128)(2,1)S(1)} %bitcast.47), channel_id=1, source_target_pairs={{0,64},{64,0},{1,65},{65,1},{2,66},{66,2},{3,67},{67,3},{4,68},{68... | collective-permute-start | bytes 1572872 | tf_op jit(solution)/shard_map/ppermute | solution.py:21
  43.3 4.4 %copy-start.13 = (bf16[1024,256]{1,0:T(8,128)(2,1)}, bf16[1024,256]{1,0:T(8,128)(2,1)S(1)}, u32[]{:S(2)}) copy-start(bf16[1024,256]{1,0:T(8,128)(2,1)S(1)} %collective-permute-done.7.p1.refs_1_) | copy-start | bytes 1572868
  43.4 4.4 %copy-start.15 = (bf16[1024,256]{1,0:T(8,128)(2,1)}, bf16[1024,256]{1,0:T(8,128)(2,1)S(1)}, u32[]{:S(2)}) copy-start(bf16[1024,256]{1,0:T(8,128)(2,1)S(1)} %collective-permute-done.8.p3.refs_3_) | copy-start | bytes 1572868
  47.8 1.1 copy-start.23
  55.4 9.1 %copy-start.17 = (bf16[1024,256]{1,0:T(8,128)(2,1)}, bf16[1024,256]{1,0:T(8,128)(2,1)S(1)}, u32[]{:S(2)}) copy-start(bf16[1024,256]{1,0:T(8,128)(2,1)S(1)} %collective-permute-done.6.p2.refs_6_) | copy-start | bytes 1572868
  55.4 4.7 %collective-permute-start.10 = (bf16[1024,256]{1,0:T(8,128)(2,1)S(1)}, bf16[1024,256]{1,0:T(8,128)(2,1)S(1)}, u32[]{:S(2)}, u32[]{:S(2)}) collective-permute-start(bf16[1024,256]{1,0:T(8,128)(2,1)S(1)} %collective-permute-done.6.p2.refs_6_), channel_id=1, source_target_pairs={{0,64},{64,0},{1,65},{65,1},{2,66},{66,2},{3,67},{67,3},{4,68},{68... | collective-permute-start | bytes 1572872 | tf_op jit(solution)/shard_map/ppermute | solution.py:21
  56.2 15.9 %collective-permute-start.12 = (bf16[272,1152]{1,0:T(8,128)(2,1)S(1)}, bf16[272,1152]{1,0:T(8,128)(2,1)S(1)}, u32[]{:S(2)}, u32[]{:S(2)}) collective-permute-start(bf16[272,1152]{1,0:T(8,128)(2,1)S(1)} %get-tuple-element.65), channel_id=1, source_target_pairs={{0,16},{16,0},{32,48},{48,32},{1,17},{17,1},{33,49},{49,33},{2,18}... | collective-permute-start | bytes 1880072 | tf_op jit(solution)/shard_map/ppermute | solution.py:21
  56.6 31.3 %collective-permute-start.13 = (bf16[272,1152]{1,0:T(8,128)(2,1)S(1)}, bf16[272,1152]{1,0:T(8,128)(2,1)S(1)}, u32[]{:S(2)}, u32[]{:S(2)}) collective-permute-start(bf16[272,1152]{1,0:T(8,128)(2,1)S(1)} %get-tuple-element.66), channel_id=1, source_target_pairs={{0,32},{16,48},{32,0},{48,16},{1,33},{17,49},{33,1},{49,17},{2,34}... | collective-permute-start | bytes 1880072 | tf_op jit(solution)/shard_map/ppermute | solution.py:21
  60.1 43.2 %collective-permute-start.14 = (bf16[272,1152]{1,0:T(8,128)(2,1)S(1)}, bf16[272,1152]{1,0:T(8,128)(2,1)S(1)}, u32[]{:S(2)}, u32[]{:S(2)}) collective-permute-start(bf16[272,1152]{1,0:T(8,128)(2,1)S(1)} %get-tuple-element.67), channel_id=1, source_target_pairs={{0,48},{16,32},{32,16},{48,0},{1,49},{17,33},{33,17},{49,1},{2,50}... | collective-permute-start | bytes 1880072 | tf_op jit(solution)/shard_map/ppermute | solution.py:21
  60.1 4.4 %copy-start.19 = (bf16[1024,256]{1,0:T(8,128)(2,1)}, bf16[1024,256]{1,0:T(8,128)(2,1)S(1)}, u32[]{:S(2)}) copy-start(bf16[1024,256]{1,0:T(8,128)(2,1)S(1)} %collective-permute-done.9.p1.refs_5_) | copy-start | bytes 1572868
  60.1 4.4 %copy-start.21 = (bf16[1024,256]{1,0:T(8,128)(2,1)}, bf16[1024,256]{1,0:T(8,128)(2,1)S(1)}, u32[]{:S(2)}) copy-start(bf16[1024,256]{1,0:T(8,128)(2,1)S(1)} %collective-permute-done.10.p3.refs_7_) | copy-start | bytes 1572868
  64.5 1.0 copy-start.25
  65.5 0.9 copy-start.35
  66.4 0.8 copy-start.37
  67.2 36.9 %collective-permute-start.11 = (bf16[272,1152]{1,0:T(8,128)(2,1)S(1)}, bf16[272,1152]{1,0:T(8,128)(2,1)S(1)}, u32[]{:S(2)}, u32[]{:S(2)}) collective-permute-start(bf16[272,1152]{1,0:T(8,128)(2,1)S(1)} %get-tuple-element.64), channel_id=1, source_target_pairs={{0,32},{16,48},{32,0},{48,16},{1,33},{17,49},{33,1},{49,17},{2,34}... | collective-permute-start | bytes 1880072 | tf_op jit(solution)/shard_map/ppermute | solution.py:21
  72.0 0.8 copy-start.29
  87.8 0.9 copy-start.31
  103.3 0.8 copy-start.33
  104.1 2.3 %copy-start = (bf16[2048,1152]{1,0:T(8,128)(2,1)S(1)}, bf16[2048,1152]{1,0:T(8,128)(2,1)}, u32[]{:S(2)}) copy-start(bf16[2048,1152]{1,0:T(8,128)(2,1)} %all-gather.2.cloned.1.call-done) | copy-start | bytes 14155780
  106.5 5.9 %copy-start.38 = (bf16[272,1152]{1,0:T(8,128)(2,1)S(1)}, bf16[272,1152]{1,0:T(8,128)(2,1)}, u32[]{:S(2)}) copy-start(bf16[272,1152]{1,0:T(8,128)(2,1)} %copy-done.37) | copy-start | bytes 1880068
  106.5 6.0 %copy-start.36 = (bf16[272,1152]{1,0:T(8,128)(2,1)S(1)}, bf16[272,1152]{1,0:T(8,128)(2,1)}, u32[]{:S(2)}) copy-start(bf16[272,1152]{1,0:T(8,128)(2,1)} %copy-done.35) | copy-start | bytes 1880068
  106.5 25.2 %copy-start.24 = (f32[256,1152]{1,0:T(8,128)S(1)}, f32[256,1152]{1,0:T(8,128)}, u32[]{:S(2)}) copy-start(f32[256,1152]{1,0:T(8,128)} %copy-done.23) | copy-start | bytes 3538948
  106.5 25.2 %copy-start.26 = (f32[256,1152]{1,0:T(8,128)S(1)}, f32[256,1152]{1,0:T(8,128)}, u32[]{:S(2)}) copy-start(f32[256,1152]{1,0:T(8,128)} %copy-done.25) | copy-start | bytes 3538948
  106.5 25.2 %copy-start.30 = (bf16[272,1152]{1,0:T(8,128)(2,1)S(1)}, bf16[272,1152]{1,0:T(8,128)(2,1)}, u32[]{:S(2)}) copy-start(bf16[272,1152]{1,0:T(8,128)(2,1)} %copy-done.29) | copy-start | bytes 1880068
  106.5 25.2 %copy-start.32 = (bf16[272,1152]{1,0:T(8,128)(2,1)S(1)}, bf16[272,1152]{1,0:T(8,128)(2,1)}, u32[]{:S(2)}) copy-start(bf16[272,1152]{1,0:T(8,128)(2,1)} %copy-done.31) | copy-start | bytes 1880068
  106.5 25.2 %copy-start.34 = (bf16[272,1152]{1,0:T(8,128)(2,1)S(1)}, bf16[272,1152]{1,0:T(8,128)(2,1)}, u32[]{:S(2)}) copy-start(bf16[272,1152]{1,0:T(8,128)(2,1)} %copy-done.33) | copy-start | bytes 1880068
  110.8 18.2 %collective-permute-start.15 = (f32[2048,256]{1,0:T(8,128)S(1)}, f32[2048,256]{1,0:T(8,128)S(1)}, u32[]{:S(2)}, u32[]{:S(2)}) collective-permute-start(f32[2048,256]{1,0:T(8,128)S(1)} %get-tuple-element.69), channel_id=1, source_target_pairs={{0,64},{64,0},{1,65},{65,1},{2,66},{66,2},{3,67},{67,3},{4,68},{68... | collective-permute-start | bytes 6291464 | tf_op jit(solution)/shard_map/ppermute | solution.py:21
  112.3 18.0 %collective-permute-start.16 = (f32[2048,256]{1,0:T(8,128)S(1)}, f32[2048,256]{1,0:T(8,128)S(1)}, u32[]{:S(2)}, u32[]{:S(2)}) collective-permute-start(f32[2048,256]{1,0:T(8,128)S(1)} %get-tuple-element.70), channel_id=1, source_target_pairs={{0,64},{64,0},{1,65},{65,1},{2,66},{66,2},{3,67},{67,3},{4,68},{68... | collective-permute-start | bytes 6291464 | tf_op jit(solution)/shard_map/ppermute | solution.py:21
  112.4 15.3 %collective-permute-start.17 = (bf16[272,1152]{1,0:T(8,128)(2,1)S(1)}, bf16[272,1152]{1,0:T(8,128)(2,1)S(1)}, u32[]{:S(2)}, u32[]{:S(2)}) collective-permute-start(bf16[272,1152]{1,0:T(8,128)(2,1)S(1)} %copy-done.38), channel_id=1, source_target_pairs={{0,16},{16,0},{32,48},{48,32},{1,17},{17,1},{33,49},{49,33},{2,18}... | collective-permute-start | bytes 1880072 | tf_op jit(solution)/shard_map/ppermute | solution.py:21
  112.4 16.6 %collective-permute-start.18 = (bf16[272,1152]{1,0:T(8,128)(2,1)S(1)}, bf16[272,1152]{1,0:T(8,128)(2,1)S(1)}, u32[]{:S(2)}, u32[]{:S(2)}) collective-permute-start(bf16[272,1152]{1,0:T(8,128)(2,1)S(1)} %copy-done.36), channel_id=1, source_target_pairs={{0,48},{16,32},{32,16},{48,0},{1,49},{17,33},{33,17},{49,1},{2,50}... | collective-permute-start | bytes 1880072 | tf_op jit(solution)/shard_map/ppermute | solution.py:21
  129.0 1.3 copy-start.11
  130.3 1.3 copy-start.9
  137.5 1.0 copy-start.4
  138.6 19.0 %slice-start = ((s8[4718592]{0:T(1024)(128)(4,1)}), s8[524288]{0:T(1024)(128)(4,1)S(1)}, s32[]{:S(2)}) async-start(s8[4718592]{0:T(1024)(128)(4,1)} %bitcast.37), calls=%async_computation.2 | async-start | bytes 1048576
  138.6 56.6 %all-to-all-start = ((bf16[16,32,1280]{2,1,0:T(8,128)(2,1)}), bf16[16,32,1280]{2,1,0:T(8,128)(2,1)}, u32[]{:S(2)}, u32[]{:S(2)}) async-start(bf16[16,32,1280]{2,1,0:T(8,128)(2,1)} %bitcast.45), calls=%async_computation | async-start | bytes 2621440 | tf_op jit(solution)/shard_map/all_to_all | solution.py:141
  148.5 2.3 %copy-start.1 = (bf16[2048,1152]{1,0:T(8,128)(2,1)S(1)}, bf16[2048,1152]{1,0:T(8,128)(2,1)}, u32[]{:S(2)}) copy-start(bf16[2048,1152]{1,0:T(8,128)(2,1)} %all-gather.2.cloned.1.call-done) | copy-start | bytes 14155780
  150.8 1.6 copy-start.12
  152.4 5.2 %slice-start.1 = ((s8[4718592]{0:T(1024)(128)(4,1)}), s8[4194304]{0:T(1024)(128)(4,1)S(1)}, s32[]{:S(2)}) async-start(s8[4718592]{0:T(1024)(128)(4,1)} %bitcast.37), calls=%async_computation.3 | async-start | bytes 8388608
  152.4 5.2 %copy-start.6 = (bf16[1024,1,256]{2,0,1:T(8,128)(2,1)S(1)}, bf16[1024,1,256]{2,0,1:T(8,128)(2,1)}, u32[]{:S(2)}) copy-start(bf16[1024,1,256]{2,0,1:T(8,128)(2,1)} %copy-done.5) | copy-start | bytes 1572868
  152.4 5.2 %copy-start.8 = (bf16[1024,256]{1,0:T(8,128)(2,1)S(1)}, bf16[1024,256]{1,0:T(8,128)(2,1)}, u32[]{:S(2)}) copy-start(bf16[1024,256]{1,0:T(8,128)(2,1)} %copy-done.7) | copy-start | bytes 1572868
  152.4 5.2 %copy-start.14 = (bf16[1024,256]{1,0:T(8,128)(2,1)S(1)}, bf16[1024,256]{1,0:T(8,128)(2,1)}, u32[]{:S(2)}) copy-start(bf16[1024,256]{1,0:T(8,128)(2,1)} %copy-done.13) | copy-start | bytes 1572868
  152.4 5.2 %copy-start.16 = (bf16[1024,256]{1,0:T(8,128)(2,1)S(1)}, bf16[1024,256]{1,0:T(8,128)(2,1)}, u32[]{:S(2)}) copy-start(bf16[1024,256]{1,0:T(8,128)(2,1)} %copy-done.15) | copy-start | bytes 1572868
  152.4 5.2 %copy-start.18 = (bf16[1024,256]{1,0:T(8,128)(2,1)S(1)}, bf16[1024,256]{1,0:T(8,128)(2,1)}, u32[]{:S(2)}) copy-start(bf16[1024,256]{1,0:T(8,128)(2,1)} %copy-done.17) | copy-start | bytes 1572868
  152.5 5.2 %copy-start.20 = (bf16[1024,256]{1,0:T(8,128)(2,1)S(1)}, bf16[1024,256]{1,0:T(8,128)(2,1)}, u32[]{:S(2)}) copy-start(bf16[1024,256]{1,0:T(8,128)(2,1)} %copy-done.19) | copy-start | bytes 1572868
  152.5 5.2 %copy-start.22 = (bf16[1024,256]{1,0:T(8,128)(2,1)S(1)}, bf16[1024,256]{1,0:T(8,128)(2,1)}, u32[]{:S(2)}) copy-start(bf16[1024,256]{1,0:T(8,128)(2,1)} %copy-done.21) | copy-start | bytes 1572868
  157.5 36.7 %collective-permute-start.19 = (bf16[2176,256]{1,0:T(8,128)(2,1)S(1)}, bf16[2176,256]{1,0:T(8,128)(2,1)S(1)}, u32[]{:S(2)}, u32[]{:S(2)}) collective-permute-start(bf16[2176,256]{1,0:T(8,128)(2,1)S(1)} %far_kernel.1), channel_id=1, source_target_pairs={{0,128},{128,0},{1,129},{129,1},{2,130},{130,2},{3,131},{131,3},{4... | collective-permute-start | bytes 3342344 | tf_op jit(solution)/shard_map/ppermute | solution.py:21
  194.2 1.0 copy-start.27
  195.2 2.3 %copy-start.2 = (bf16[2048,1152]{1,0:T(8,128)(2,1)S(1)}, bf16[2048,1152]{1,0:T(8,128)(2,1)}, u32[]{:S(2)}) copy-start(bf16[2048,1152]{1,0:T(8,128)(2,1)} %all-gather.2.cloned.1.call-done) | copy-start | bytes 14155780
  197.5 1.6 copy-start.10
  199.1 1.2 copy-start.28
Sparse Core Ops, SparseCore 0:
  31.9 63.4 all-gather.1

commit v4 on v3

--- a/solution.py
+++ b/solution.py
@@ -283,15 +283,16 @@
     corner_v = flip(across_v, "core", 1)
     gv, *send_v = grad(u, (own_v, beside_v, across_v, corner_v), tokens)
     got_v = [flip(s, "y", bits) for s, bits in zip(send_v, (1, 2, 3))]
-    gk, gv, w, got_v[1], *got_k = hold(gk, gv, w, got_v[1], *got_k)
+    gk, gv, w, *got = hold(gk, gv, w, *got_k, *got_v)
 
     both_cores = shape((2048, 256), F32)
     to_far, to_near = project(beside_kernel, [both_cores] * 2, tokens, w)
     got_far, got_near = flip(to_far, "core", 1), flip(to_near, "core", 1)
-    got_far, got_near, gk, gv, *got = hold(got_far, got_near, gk, gv, *got_k, *got_v)
-    total = spread(sum_over_y(gk, *got[:3], gv, *got[3:]))
+    total = sum_over_y(gk, *got[:3], gv, *got[3:])
     (far,) = project(far_kernel, [shape((2176, 256), BF16)], tokens, w, got_far)
+    total, far, got_near, w = hold(total, far, got_near, w)
     across = flip(far, "xl", 1)
+    total = spread(total)
     d_tokens = back(
         (own_k, beside_k, across_k, corner_k, own_v, beside_v, across_v, corner_v), w
     )

time: 217 us -> 210 us (0.968)
  waiting for transfers between devices: 90.6 us -> 75.8 us
  local copies, waits for them, and re-layouts: 37 us -> 42.2 us
    ppermute x20, waiting for transfers between devices: 90.6 us -> 75.8 us  [flip(): return lax.ppermute(x, axis, [(i, i ^ bits) for i in range(n)])]
    unnamed x86 -> x82, local copies, waits for them, and re-layouts: 25.7 us -> 30.8 us
  transfers between devices with their start and end apart: 22 -> 22, of which waited for: 8 -> 9; matrix products, arithmetic and copies ran while one was open for 2% -> 3% of each run, Pallas kernels for 10% -> 13%
where the time goes in v4:
time: 210 us; the launch traced here: 208 us
  waiting for transfers between devices  75.8 us (36%)
  local copies, waits for them, and re-layouts  42.2 us (20%)
  Pallas kernels  38.4 us (18%)
  starting transfers between devices  37.2 us (18%)
  between operations  14.4 us (7%)
    ppermute x20, waiting for transfers between devices, flip(): return lax.ppermute(x, axis, [(i, i ^ bits) for i in range(n)])  75.8 us
    unnamed x82, local copies, waits for them, and re-layouts  30.8 us
    ppermute x20, starting transfers between devices, flip(): return lax.ppermute(x, axis, [(i, i ^ bits) for i in range(n)])  27.3 us
    pallas_call x3, Pallas kernels, project(): pl.pallas_call(kernel, out_shape=outs, in_specs=[VMEM] * len(args), out_s...  12.6 us
    all_to_all x1, starting transfers between devices, spread(): lax.all_to_all(x.reshape(16, 32, 1280), ('z', 'xh'), 0, 0, tiled=True)  9.78 us
    pallas_call x2, Pallas kernels, grad(): pl.pallas_call(grad_kernel, out_shape=[shape((256, 1152), F32)] + [shape(...  8.67 us
    pallas_call x1, Pallas kernels, back(): pl.pallas_call(back_kernel, out_shape=shape((1024, 1152), BF16), in_specs...  7.8 us
    dynamic_update_slice x6, local copies, waits for them, and re-layouts, put(): return lax.dynamic_update_index_in_dim(x, piece, i, 0)  6.33 us
  transfers between devices with their start and end apart: 22, of which 9 were waited for; matrix products, arithmetic and copies ran while one was open for 3% of the time, Pallas kernels for 13%

profile of v4, /device:TPU:1, one launch (start us, length us, event | category | flops | bytes accessed | tf_op | source)
XLA Modules:
  0.0 208.0 jit_solution(13001630898891136500)
XLA Ops:
  7.2 3.7 %collective-permute-start = (bf16[2,16,1152]{2,1,0:T(8,128)(2,1)}, bf16[2,16,1152]{2,1,0:T(8,128)(2,1)S(1)}, u32[]{:S(2)}, u32[]{:S(2)}) collective-permute-start(bf16[2,16,1152]{2,1,0:T(8,128)(2,1)} %bitcast.55), channel_id=1, source_target_pairs={{0,1},{1,0},{2,3},{3,2},{4,5},{5,4},{6,7},{7,6},{8,9},{9,8},{10,11... | collective-permute-start | bytes 221192 | tf_op jit(solution)/shard_map/ppermute | solution.py:21
  10.9 0.9 bitcast_dynamic-update-slice_fusion.4
  11.8 3.3 %fusion = (bf16[1024,1,256]{2,1,0:T(2,128)(2,1)S(1)}, bf16[1024,1,256]{2,1,0:T(2,128)(2,1)S(1)}) fusion(bf16[1024,2,256]{2,1,0:T(2,128)(2,1)} %param.5), kind=kLoop, calls=%fused_computation.11 | loop fusion | bytes 2097152 | tf_op jit(solution)/shard_map/slice | solution.py:259
  15.3 0.8 fusion.1
  16.5 2.7 %collective-permute-start.4 = (bf16[2,32,1152]{2,1,0:T(8,128)(2,1)S(1)}, bf16[2,32,1152]{2,1,0:T(8,128)(2,1)}, u32[]{:S(2)}, u32[]{:S(2)}) collective-permute-start(bf16[2,32,1152]{2,1,0:T(8,128)(2,1)S(1)} %bitcast.50), channel_id=1, source_target_pairs={{0,48},{16,32},{32,16},{48,0},{1,49},{17,33},{33,17},{49,1},{2,50}... | collective-permute-start | bytes 442376 | tf_op jit(solution)/shard_map/ppermute | solution.py:21
  19.8 5.6 %collective-permute-done.4 = bf16[2,32,1152]{2,1,0:T(8,128)(2,1)} collective-permute-done((bf16[2,32,1152]{2,1,0:T(8,128)(2,1)S(1)}, bf16[2,32,1152]{2,1,0:T(8,128)(2,1)}, u32[]{:S(2)}, u32[]{:S(2)}) %collective-permute-start.4) | collective-permute-done | bytes 147488 | tf_op jit(solution)/shard_map/ppermute | solution.py:21
  25.4 0.9 broadcast_in_dim.29
  26.3 0.7 bitcast_dynamic-update-slice_fusion.3
  27.0 1.6 bitcast_dynamic-update-slice_fusion.2
  28.6 1.6 bitcast_dynamic-update-slice_fusion.1
  30.1 1.6 bitcast_dynamic-update-slice_fusion
  31.8 1.2 collective-permute-start.5
  33.0 3.6 %collective-permute-start.7 = (bf16[1024,256]{1,0:T(8,128)(2,1)S(1)}, bf16[1024,256]{1,0:T(8,128)(2,1)S(1)}, u32[]{:S(2)}, u32[]{:S(2)}) collective-permute-start(bf16[1024,256]{1,0:T(8,128)(2,1)S(1)} %bitcast.40), channel_id=1, source_target_pairs={{0,64},{64,0},{1,65},{65,1},{2,66},{66,2},{3,67},{67,3},{4,68},{68... | collective-permute-start | bytes 1572872 | tf_op jit(solution)/shard_map/ppermute | solution.py:21
  36.6 1.0 constant_dynamic-update-slice_fusion.1
  37.6 4.2 %collective-permute-start.8 = (bf16[1024,256]{1,0:T(8,128)(2,1)S(1)}, bf16[1024,256]{1,0:T(8,128)(2,1)S(1)}, u32[]{:S(2)}, u32[]{:S(2)}) collective-permute-start(bf16[1024,256]{1,0:T(8,128)(2,1)S(1)} %constant_dynamic-update-slice_fusion.p2.refs_2_), channel_id=1, source_target_pairs={{0,64},{64,0},{1,65},{65,1},{2,66},{66,2},{3,67},{67,3},{4,68},{68... | collective-permute-start | bytes 1572872 | tf_op jit(solution)/shard_map/ppermute | solution.py:21
  41.8 1.2 collective-permute-start.6
  43.4 4.3 %grad.2 = (f32[256,1152]{1,0:T(8,128)S(1)}, bf16[272,1152]{1,0:T(8,128)(2,1)S(1)}, bf16[272,1152]{1,0:T(8,128)(2,1)S(1)}, bf16[272,1152]{1,0:T(8,128)(2,1)S(1)}) custom-call(s32[1]{0:T(128)} %bitcast.8.u_ref, bf16[1024,256]{1,0:T(8,128)(2,1)S(1)} %bitcast.41, bf16[1024,256]{1,0:T(8,128)(2,1)S(1)} %collective-permute-done.7.p1.refs_1_, ...), custom_call_target="tpu_custom_call" | custom-call | flops 1 | bytes 1 | tf_op jit(solution)/shard_map/grad/pallas_call | solution.py:81
  47.8 1.0 copy-done.20
  49.1 0.7 collective-permute-start.9
  49.8 5.6 %collective-permute-done.6.p2.refs_6_ = bf16[1024,256]{1,0:T(8,128)(2,1)S(1)} collective-permute-done((bf16[1024,256]{1,0:T(8,128)(2,1)S(1)}, bf16[1024,256]{1,0:T(8,128)(2,1)S(1)}, u32[]{:S(2)}, u32[]{:S(2)}) %collective-permute-start.6) | collective-permute-done | bytes 524320 | tf_op jit(solution)/shard_map/ppermute | solution.py:21
  55.4 0.8 collective-permute-start.10
  56.2 2.0 collective-permute-start.12
  58.2 0.7 collective-permute-start.13
  59.0 4.3 %grad.3 = (f32[256,1152]{1,0:T(8,128)S(1)}, bf16[272,1152]{1,0:T(8,128)(2,1)S(1)}, bf16[272,1152]{1,0:T(8,128)(2,1)S(1)}, bf16[272,1152]{1,0:T(8,128)(2,1)S(1)}) custom-call(s32[1]{0:T(128)} %bitcast.8.u_ref, bf16[1024,256]{1,0:T(8,128)(2,1)S(1)} %bitcast.46, bf16[1024,256]{1,0:T(8,128)(2,1)S(1)} %collective-permute-done.9.p1.refs_5_, ...), custom_call_target="tpu_custom_call" | custom-call | flops 1 | bytes 1 | tf_op jit(solution)/shard_map/grad/pallas_call | solution.py:81
  63.4 1.0 copy-done.22
  64.4 0.5 collective-permute-start.14
  64.9 2.6 %collective-permute-start.15 = (bf16[272,1152]{1,0:T(8,128)(2,1)S(1)}, bf16[272,1152]{1,0:T(8,128)(2,1)S(1)}, u32[]{:S(2)}, u32[]{:S(2)}) collective-permute-start(bf16[272,1152]{1,0:T(8,128)(2,1)S(1)} %get-tuple-element.64), channel_id=1, source_target_pairs={{0,32},{16,48},{32,0},{48,16},{1,33},{17,49},{33,1},{49,17},{2,34}... | collective-permute-start | bytes 1880072 | tf_op jit(solution)/shard_map/ppermute | solution.py:21
  67.5 0.8 copy-done.27
  68.3 0.7 collective-permute-start.16
  69.1 10.9 %collective-permute-done.12.refs_2_ = bf16[272,1152]{1,0:T(8,128)(2,1)S(1)} collective-permute-done((bf16[272,1152]{1,0:T(8,128)(2,1)S(1)}, bf16[272,1152]{1,0:T(8,128)(2,1)S(1)}, u32[]{:S(2)}, u32[]{:S(2)}) %collective-permute-start.12) | collective-permute-done | bytes 626720 | tf_op jit(solution)/shard_map/ppermute | solution.py:21
  80.0 0.8 copy-done.29
  80.8 7.6 %collective-permute-done.13.refs_3_ = bf16[272,1152]{1,0:T(8,128)(2,1)S(1)} collective-permute-done((bf16[272,1152]{1,0:T(8,128)(2,1)S(1)}, bf16[272,1152]{1,0:T(8,128)(2,1)S(1)}, u32[]{:S(2)}, u32[]{:S(2)}) %collective-permute-start.13) | collective-permute-done | bytes 626720 | tf_op jit(solution)/shard_map/ppermute | solution.py:21
  88.4 0.8 copy-done.31
  89.2 1.9 collective-permute-done.14.refs_5_
  91.1 0.9 copy-done.33
  92.0 14.9 %collective-permute-done.15.refs_6_ = bf16[272,1152]{1,0:T(8,128)(2,1)S(1)} collective-permute-done((bf16[272,1152]{1,0:T(8,128)(2,1)S(1)}, bf16[272,1152]{1,0:T(8,128)(2,1)S(1)}, u32[]{:S(2)}, u32[]{:S(2)}) %collective-permute-start.15) | collective-permute-done | bytes 626720 | tf_op jit(solution)/shard_map/ppermute | solution.py:21
  106.9 0.9 copy-done.35
  107.8 7.4 %collective-permute-done.16.refs_7_ = bf16[272,1152]{1,0:T(8,128)(2,1)S(1)} collective-permute-done((bf16[272,1152]{1,0:T(8,128)(2,1)S(1)}, bf16[272,1152]{1,0:T(8,128)(2,1)S(1)}, u32[]{:S(2)}, u32[]{:S(2)}) %collective-permute-start.16) | collective-permute-done | bytes 626720 | tf_op jit(solution)/shard_map/ppermute | solution.py:21
  115.2 0.8 copy-done.37
  116.0 2.3 %copy-done = bf16[2048,1152]{1,0:T(8,128)(2,1)S(1)} copy-done((bf16[2048,1152]{1,0:T(8,128)(2,1)S(1)}, bf16[2048,1152]{1,0:T(8,128)(2,1)}, u32[]{:S(2)}) %copy-start) | copy-done | bytes 4718616
  118.4 4.3 %beside_kernel.1 = (f32[2048,256]{1,0:T(8,128)S(1)}, f32[2048,256]{1,0:T(8,128)S(1)}) custom-call(bf16[1024,1152]{1,0:T(8,128)(2,1)S(1)} %copy-done.4, bf16[8,4,2,32,1152]{4,3,2,1,0:T(8,128)(2,1)S(1)} %bitcast.35), custom_call_target="tpu_custom_call" | custom-call | flops 1 | bytes 1 | tf_op jit(solution)/shard_map/beside_kernel/pallas_call | solution.py:218
  122.7 1.2 collective-permute-start.17
  124.1 5.8 %sum_over_y.1 = bf16[512,1280]{1,0:T(8,128)(2,1)S(1)} custom-call(f32[256,1152]{1,0:T(8,128)S(1)} %copy-done.21, bf16[272,1152]{1,0:T(8,128)(2,1)S(1)} %copy-done.28, bf16[272,1152]{1,0:T(8,128)(2,1)S(1)} %copy-done.30, bf16[272,1152]{1,0:T(8,128)(2,1)S(1)} %copy-done.32, f32[256,1152]{1,0:T(8,128)S(1)} %copy-done.23, bf16[272,1152]{1,0:T(8,128)(2,1)S(1)} %copy-done.34, ...), custom_call_target="tpu_custom_call" | custom-call | flops 1 | bytes 1 | tf_op jit(solution)/shard_map/sum_over_y/pallas_call | solution.py:119
  129.9 1.0 copy-done.5
  131.0 5.0 %far_kernel.1 = bf16[2176,256]{1,0:T(8,128)(2,1)S(1)} custom-call(bf16[1024,1152]{1,0:T(8,128)(2,1)S(1)} %copy-done.4, bf16[8,4,2,32,1152]{4,3,2,1,0:T(8,128)(2,1)S(1)} %bitcast.36, f32[2048,256]{1,0:T(8,128)S(1)} %collective-permute-done.17.got), custom_call_target="tpu_custom_call" | custom-call | flops 1 | bytes 1 | tf_op jit(solution)/shard_map/far_kernel/pallas_call | solution.py:218
  136.0 1.0 copy-done.24
  137.0 1.3 copy-done.8
  138.3 9.8 %all-to-all-start = ((bf16[16,32,1280]{2,1,0:T(8,128)(2,1)}), bf16[16,32,1280]{2,1,0:T(8,128)(2,1)}, u32[]{:S(2)}, u32[]{:S(2)}) async-start(bf16[16,32,1280]{2,1,0:T(8,128)(2,1)} %bitcast.43), calls=%async_computation | async-start | bytes 2621440 | tf_op jit(solution)/shard_map/all_to_all | solution.py:141
  148.2 2.3 %copy-done.2 = bf16[2048,1152]{1,0:T(8,128)(2,1)S(1)} copy-done((bf16[2048,1152]{1,0:T(8,128)(2,1)S(1)}, bf16[2048,1152]{1,0:T(8,128)(2,1)}, u32[]{:S(2)}) %copy-start.2) | copy-done | bytes 4718616
  150.5 1.0 copy-done.7
  151.6 1.0 copy-done.11
  152.6 1.0 copy-done.13
  153.6 1.0 copy-done.15
  154.7 1.0 copy-done.17
  155.7 1.0 copy-done.19
  156.8 7.8 %back.1 = bf16[1024,1152]{1,0:T(8,128)(2,1)} custom-call(bf16[1024,256]{1,0:T(8,128)(2,1)S(1)} %bitcast.42, bf16[1024,256]{1,0:T(8,128)(2,1)S(1)} %copy-done.11, bf16[1024,256]{1,0:T(8,128)(2,1)S(1)} %copy-done.7, bf16[1024,256]{1,0:T(8,128)(2,1)S(1)} %copy-done.13, bf16[1024,256]{1,0:T(8,128)(2,1)S(1)} %bitcast.47, bf16[1024,256]{1,0:T(8,128)(2,1)S(1)} %copy-done.17, ...), custom_call_target="tpu_custom_call" | custom-call | flops 1 | bytes 1 | tf_op jit(solution)/shard_map/back/pallas_call | solution.py:243
  164.6 21.5 %collective-permute-done.19.across = bf16[2176,256]{1,0:T(8,128)(2,1)S(1)} collective-permute-done((bf16[2176,256]{1,0:T(8,128)(2,1)}, bf16[2176,256]{1,0:T(8,128)(2,1)S(1)}, u32[]{:S(2)}, u32[]{:S(2)}) %collective-permute-start.19) | collective-permute-done | bytes 1114144 | tf_op jit(solution)/shard_map/ppermute | solution.py:21
  186.1 1.0 copy-done.25
  187.1 2.3 %copy-done.3 = bf16[2048,1152]{1,0:T(8,128)(2,1)S(1)} copy-done((bf16[2048,1152]{1,0:T(8,128)(2,1)S(1)}, bf16[2048,1152]{1,0:T(8,128)(2,1)}, u32[]{:S(2)}) %copy-start.3) | copy-done | bytes 4718616
  189.4 1.6 copy-done.9
  191.0 1.2 copy-done.26
  192.3 3.3 %near_kernel.1 = (bf16[1024,256]{1,0:T(8,128)(2,1)S(1)}, bf16[1024,256]{1,0:T(8,128)(2,1)S(1)}) custom-call(bf16[1024,1152]{1,0:T(8,128)(2,1)S(1)} %copy-done.4, bf16[8,4,2,32,1152]{4,3,2,1,0:T(8,128)(2,1)S(1)} %bitcast.38, f32[2048,256]{1,0:T(8,128)S(1)} %copy-done.9, bf16[2176,256]{1,0:T(8,128)(2,1)S(1)} %copy-done.26), custom_call_target="tpu_custom_call" | custom-call | flops 1 | bytes 1 | tf_op jit(solution)/shard_map/near_kernel/pallas_call | solution.py:218
  195.7 2.0 copy.12
  197.7 3.5 %sum_over_z.1 = f32[32,1152]{1,0:T(8,128)} custom-call(bf16[512,1280]{1,0:T(8,128)(2,1)} %bitcast.18.x), custom_call_target="tpu_custom_call" | custom-call | flops 1 | bytes 1 | tf_op jit(solution)/shard_map/sum_over_z/pallas_call | solution.py:145
  (83 shorter events, 2.3 us)
Async XLA Ops:
  7.2 108.8 %all-gather.2.cloned.1.call-start = ((), (), s32[]{:S(2)}) async-start(), calls=%async_computation.1 | async-start | bytes 5308416 | tf_op jit(solution)/shard_map/all_gather | solution.py:274
  7.2 8.1 %collective-permute-start = (bf16[2,16,1152]{2,1,0:T(8,128)(2,1)}, bf16[2,16,1152]{2,1,0:T(8,128)(2,1)S(1)}, u32[]{:S(2)}, u32[]{:S(2)}) collective-permute-start(bf16[2,16,1152]{2,1,0:T(8,128)(2,1)} %bitcast.55), channel_id=1, source_target_pairs={{0,1},{1,0},{2,3},{3,2},{4,5},{5,4},{6,7},{7,6},{8,9},{9,8},{10,11... | collective-permute-start | bytes 221192 | tf_op jit(solution)/shard_map/ppermute | solution.py:21
  15.3 28.0 %copy-start.4 = (bf16[1024,1152]{1,0:T(8,128)(2,1)S(1)}, bf16[1024,1152]{1,0:T(8,128)(2,1)}, u32[]{:S(2)}) copy-start(bf16[1024,1152]{1,0:T(8,128)(2,1)} %tok.9) | copy-start | bytes 7077892
  16.2 9.3 %collective-permute-start.1 = (bf16[512,256]{1,0:T(8,128)(2,1)}, bf16[512,256]{1,0:T(8,128)(2,1)}, u32[]{:S(2)}, u32[]{:S(2)}) collective-permute-start(bf16[512,256]{1,0:T(8,128)(2,1)} %get-tuple-element.96), channel_id=1, source_target_pairs={{0,128},{128,0},{1,129},{129,1},{2,130},{130,2},{3,131},{131,3},{4... | collective-permute-start | bytes 786440 | tf_op jit(solution)/shard_map/ppermute | solution.py:21
  16.5 9.0 %collective-permute-start.4 = (bf16[2,32,1152]{2,1,0:T(8,128)(2,1)S(1)}, bf16[2,32,1152]{2,1,0:T(8,128)(2,1)}, u32[]{:S(2)}, u32[]{:S(2)}) collective-permute-start(bf16[2,32,1152]{2,1,0:T(8,128)(2,1)S(1)} %bitcast.50), channel_id=1, source_target_pairs={{0,48},{16,32},{32,16},{48,0},{1,49},{17,33},{33,17},{49,1},{2,50}... | collective-permute-start | bytes 442376 | tf_op jit(solution)/shard_map/ppermute | solution.py:21
  19.2 6.2 %collective-permute-start.3 = (bf16[2,32,1152]{2,1,0:T(8,128)(2,1)S(1)}, bf16[2,32,1152]{2,1,0:T(8,128)(2,1)}, u32[]{:S(2)}, u32[]{:S(2)}) collective-permute-start(bf16[2,32,1152]{2,1,0:T(8,128)(2,1)S(1)} %bitcast.51), channel_id=1, source_target_pairs={{0,32},{16,48},{32,0},{48,16},{1,33},{17,49},{33,1},{49,17},{2,34}... | collective-permute-start | bytes 442376 | tf_op jit(solution)/shard_map/ppermute | solution.py:21
  19.6 5.9 %collective-permute-start.2 = (bf16[2,32,1152]{2,1,0:T(8,128)(2,1)S(1)}, bf16[2,32,1152]{2,1,0:T(8,128)(2,1)}, u32[]{:S(2)}, u32[]{:S(2)}) collective-permute-start(bf16[2,32,1152]{2,1,0:T(8,128)(2,1)S(1)} %bitcast.52), channel_id=1, source_target_pairs={{0,16},{16,0},{32,48},{48,32},{1,17},{17,1},{33,49},{49,33},{2,18}... | collective-permute-start | bytes 442376 | tf_op jit(solution)/shard_map/ppermute | solution.py:21
  31.8 5.8 %collective-permute-start.5 = (bf16[512,256]{1,0:T(8,128)(2,1)}, bf16[512,256]{1,0:T(8,128)(2,1)S(1)}, u32[]{:S(2)}, u32[]{:S(2)}) collective-permute-start(bf16[512,256]{1,0:T(8,128)(2,1)} %get-tuple-element.47), channel_id=1, source_target_pairs={{0,128},{128,0},{1,129},{129,1},{2,130},{130,2},{3,131},{131,3},{4... | collective-permute-start | bytes 786440 | tf_op jit(solution)/shard_map/ppermute | solution.py:21
  33.0 10.0 %collective-permute-start.7 = (bf16[1024,256]{1,0:T(8,128)(2,1)S(1)}, bf16[1024,256]{1,0:T(8,128)(2,1)S(1)}, u32[]{:S(2)}, u32[]{:S(2)}) collective-permute-start(bf16[1024,256]{1,0:T(8,128)(2,1)S(1)} %bitcast.40), channel_id=1, source_target_pairs={{0,64},{64,0},{1,65},{65,1},{2,66},{66,2},{3,67},{67,3},{4,68},{68... | collective-permute-start | bytes 1572872 | tf_op jit(solution)/shard_map/ppermute | solution.py:21
  37.6 10.2 %copy-start.6 = (bf16[1024,256]{1,0:T(8,128)(2,1)}, bf16[1024,256]{1,0:T(8,128)(2,1)S(1)}, u32[]{:S(2)}) copy-start(bf16[1024,256]{1,0:T(8,128)(2,1)S(1)} %constant_dynamic-update-slice_fusion.p2.refs_2_) | copy-start | bytes 1572868
  37.6 5.8 %collective-permute-start.8 = (bf16[1024,256]{1,0:T(8,128)(2,1)S(1)}, bf16[1024,256]{1,0:T(8,128)(2,1)S(1)}, u32[]{:S(2)}, u32[]{:S(2)}) collective-permute-start(bf16[1024,256]{1,0:T(8,128)(2,1)S(1)} %constant_dynamic-update-slice_fusion.p2.refs_2_), channel_id=1, source_target_pairs={{0,64},{64,0},{1,65},{65,1},{2,66},{66,2},{3,67},{67,3},{4,68},{68... | collective-permute-start | bytes 1572872 | tf_op jit(solution)/shard_map/ppermute | solution.py:21
  41.8 13.6 %collective-permute-start.6 = (bf16[1024,256]{1,0:T(8,128)(2,1)S(1)}, bf16[1024,256]{1,0:T(8,128)(2,1)S(1)}, u32[]{:S(2)}, u32[]{:S(2)}) collective-permute-start(bf16[1024,256]{1,0:T(8,128)(2,1)S(1)} %bitcast.44), channel_id=1, source_target_pairs={{0,128},{128,0},{1,129},{129,1},{2,130},{130,2},{3,131},{131,3},{4... | collective-permute-start | bytes 1572872 | tf_op jit(solution)/shard_map/ppermute | solution.py:21
  43.0 4.7 %copy-start.10 = (bf16[1024,256]{1,0:T(8,128)(2,1)}, bf16[1024,256]{1,0:T(8,128)(2,1)S(1)}, u32[]{:S(2)}) copy-start(bf16[1024,256]{1,0:T(8,128)(2,1)S(1)} %collective-permute-done.7.p1.refs_1_) | copy-start | bytes 1572868
  43.4 4.4 %copy-start.12 = (bf16[1024,256]{1,0:T(8,128)(2,1)}, bf16[1024,256]{1,0:T(8,128)(2,1)S(1)}, u32[]{:S(2)}) copy-start(bf16[1024,256]{1,0:T(8,128)(2,1)S(1)} %collective-permute-done.8.p3.refs_3_) | copy-start | bytes 1572868
  47.7 1.0 copy-start.20
  48.8 18.8 %collective-permute-start.11 = (bf16[272,1152]{1,0:T(8,128)(2,1)S(1)}, bf16[272,1152]{1,0:T(8,128)(2,1)S(1)}, u32[]{:S(2)}, u32[]{:S(2)}) collective-permute-start(bf16[272,1152]{1,0:T(8,128)(2,1)S(1)} %get-tuple-element.60), channel_id=1, source_target_pairs={{0,16},{16,0},{32,48},{48,32},{1,17},{17,1},{33,49},{49,33},{2,18}... | collective-permute-start | bytes 1880072 | tf_op jit(solution)/shard_map/ppermute | solution.py:21
  49.1 9.8 %collective-permute-start.9 = (bf16[1024,256]{1,0:T(8,128)(2,1)S(1)}, bf16[1024,256]{1,0:T(8,128)(2,1)S(1)}, u32[]{:S(2)}, u32[]{:S(2)}) collective-permute-start(bf16[1024,256]{1,0:T(8,128)(2,1)S(1)} %bitcast.45), channel_id=1, source_target_pairs={{0,64},{64,0},{1,65},{65,1},{2,66},{66,2},{3,67},{67,3},{4,68},{68... | collective-permute-start | bytes 1572872 | tf_op jit(solution)/shard_map/ppermute | solution.py:21
  55.4 7.9 %copy-start.14 = (bf16[1024,256]{1,0:T(8,128)(2,1)}, bf16[1024,256]{1,0:T(8,128)(2,1)S(1)}, u32[]{:S(2)}) copy-start(bf16[1024,256]{1,0:T(8,128)(2,1)S(1)} %collective-permute-done.6.p2.refs_6_) | copy-start | bytes 1572868
  55.4 3.6 %collective-permute-start.10 = (bf16[1024,256]{1,0:T(8,128)(2,1)S(1)}, bf16[1024,256]{1,0:T(8,128)(2,1)S(1)}, u32[]{:S(2)}, u32[]{:S(2)}) collective-permute-start(bf16[1024,256]{1,0:T(8,128)(2,1)S(1)} %collective-permute-done.6.p2.refs_6_), channel_id=1, source_target_pairs={{0,64},{64,0},{1,65},{65,1},{2,66},{66,2},{3,67},{67,3},{4,68},{68... | collective-permute-start | bytes 1572872 | tf_op jit(solution)/shard_map/ppermute | solution.py:21
  56.2 23.8 %collective-permute-start.12 = (bf16[272,1152]{1,0:T(8,128)(2,1)S(1)}, bf16[272,1152]{1,0:T(8,128)(2,1)S(1)}, u32[]{:S(2)}, u32[]{:S(2)}) collective-permute-start(bf16[272,1152]{1,0:T(8,128)(2,1)S(1)} %get-tuple-element.61), channel_id=1, source_target_pairs={{0,32},{16,48},{32,0},{48,16},{1,33},{17,49},{33,1},{49,17},{2,34}... | collective-permute-start | bytes 1880072 | tf_op jit(solution)/shard_map/ppermute | solution.py:21
  58.2 30.2 %collective-permute-start.13 = (bf16[272,1152]{1,0:T(8,128)(2,1)S(1)}, bf16[272,1152]{1,0:T(8,128)(2,1)S(1)}, u32[]{:S(2)}, u32[]{:S(2)}) collective-permute-start(bf16[272,1152]{1,0:T(8,128)(2,1)S(1)} %get-tuple-element.62), channel_id=1, source_target_pairs={{0,48},{16,32},{32,16},{48,0},{1,49},{17,33},{33,17},{49,1},{2,50}... | collective-permute-start | bytes 1880072 | tf_op jit(solution)/shard_map/ppermute | solution.py:21
  59.0 4.4 %copy-start.16 = (bf16[1024,256]{1,0:T(8,128)(2,1)}, bf16[1024,256]{1,0:T(8,128)(2,1)S(1)}, u32[]{:S(2)}) copy-start(bf16[1024,256]{1,0:T(8,128)(2,1)S(1)} %collective-permute-done.9.p1.refs_5_) | copy-start | bytes 1572868
  59.0 4.4 %copy-start.18 = (bf16[1024,256]{1,0:T(8,128)(2,1)}, bf16[1024,256]{1,0:T(8,128)(2,1)S(1)}, u32[]{:S(2)}) copy-start(bf16[1024,256]{1,0:T(8,128)(2,1)S(1)} %collective-permute-done.10.p3.refs_7_) | copy-start | bytes 1572868
  63.4 1.0 copy-start.22
  64.4 26.7 %collective-permute-start.14 = (bf16[272,1152]{1,0:T(8,128)(2,1)S(1)}, bf16[272,1152]{1,0:T(8,128)(2,1)S(1)}, u32[]{:S(2)}, u32[]{:S(2)}) collective-permute-start(bf16[272,1152]{1,0:T(8,128)(2,1)S(1)} %get-tuple-element.63), channel_id=1, source_target_pairs={{0,16},{16,0},{32,48},{48,32},{1,17},{17,1},{33,49},{49,33},{2,18}... | collective-permute-start | bytes 1880072 | tf_op jit(solution)/shard_map/ppermute | solution.py:21
  64.9 42.0 %collective-permute-start.15 = (bf16[272,1152]{1,0:T(8,128)(2,1)S(1)}, bf16[272,1152]{1,0:T(8,128)(2,1)S(1)}, u32[]{:S(2)}, u32[]{:S(2)}) collective-permute-start(bf16[272,1152]{1,0:T(8,128)(2,1)S(1)} %get-tuple-element.64), channel_id=1, source_target_pairs={{0,32},{16,48},{32,0},{48,16},{1,33},{17,49},{33,1},{49,17},{2,34}... | collective-permute-start | bytes 1880072 | tf_op jit(solution)/shard_map/ppermute | solution.py:21
  67.5 0.8 copy-start.27
  68.3 46.8 %collective-permute-start.16 = (bf16[272,1152]{1,0:T(8,128)(2,1)S(1)}, bf16[272,1152]{1,0:T(8,128)(2,1)S(1)}, u32[]{:S(2)}, u32[]{:S(2)}) collective-permute-start(bf16[272,1152]{1,0:T(8,128)(2,1)S(1)} %get-tuple-element.65), channel_id=1, source_target_pairs={{0,48},{16,32},{32,16},{48,0},{1,49},{17,33},{33,17},{49,1},{2,50}... | collective-permute-start | bytes 1880072 | tf_op jit(solution)/shard_map/ppermute | solution.py:21
  80.0 0.8 copy-start.29
  88.4 0.8 copy-start.31
  91.1 0.9 copy-start.33
  106.9 0.9 copy-start.35
  115.2 0.8 copy-start.37
  116.0 2.3 %copy-start = (bf16[2048,1152]{1,0:T(8,128)(2,1)S(1)}, bf16[2048,1152]{1,0:T(8,128)(2,1)}, u32[]{:S(2)}) copy-start(bf16[2048,1152]{1,0:T(8,128)(2,1)} %all-gather.2.cloned.1.call-done) | copy-start | bytes 14155780
  118.3 5.7 %copy-start.21 = (f32[256,1152]{1,0:T(8,128)S(1)}, f32[256,1152]{1,0:T(8,128)}, u32[]{:S(2)}) copy-start(f32[256,1152]{1,0:T(8,128)} %copy-done.20) | copy-start | bytes 3538948
  118.3 5.7 %copy-start.23 = (f32[256,1152]{1,0:T(8,128)S(1)}, f32[256,1152]{1,0:T(8,128)}, u32[]{:S(2)}) copy-start(f32[256,1152]{1,0:T(8,128)} %copy-done.22) | copy-start | bytes 3538948
  118.3 5.7 %copy-start.28 = (bf16[272,1152]{1,0:T(8,128)(2,1)S(1)}, bf16[272,1152]{1,0:T(8,128)(2,1)}, u32[]{:S(2)}) copy-start(bf16[272,1152]{1,0:T(8,128)(2,1)} %copy-done.27) | copy-start | bytes 1880068
  118.3 5.7 %copy-start.30 = (bf16[272,1152]{1,0:T(8,128)(2,1)S(1)}, bf16[272,1152]{1,0:T(8,128)(2,1)}, u32[]{:S(2)}) copy-start(bf16[272,1152]{1,0:T(8,128)(2,1)} %copy-done.29) | copy-start | bytes 1880068
  118.3 5.7 %copy-start.32 = (bf16[272,1152]{1,0:T(8,128)(2,1)S(1)}, bf16[272,1152]{1,0:T(8,128)(2,1)}, u32[]{:S(2)}) copy-start(bf16[272,1152]{1,0:T(8,128)(2,1)} %copy-done.31) | copy-start | bytes 1880068
  118.4 5.7 %copy-start.34 = (bf16[272,1152]{1,0:T(8,128)(2,1)S(1)}, bf16[272,1152]{1,0:T(8,128)(2,1)}, u32[]{:S(2)}) copy-start(bf16[272,1152]{1,0:T(8,128)(2,1)} %copy-done.33) | copy-start | bytes 1880068
  118.4 5.7 %copy-start.36 = (bf16[272,1152]{1,0:T(8,128)(2,1)S(1)}, bf16[272,1152]{1,0:T(8,128)(2,1)}, u32[]{:S(2)}) copy-start(bf16[272,1152]{1,0:T(8,128)(2,1)} %copy-done.35) | copy-start | bytes 1880068
  118.4 5.7 %copy-start.38 = (bf16[272,1152]{1,0:T(8,128)(2,1)S(1)}, bf16[272,1152]{1,0:T(8,128)(2,1)}, u32[]{:S(2)}) copy-start(bf16[272,1152]{1,0:T(8,128)(2,1)} %copy-done.37) | copy-start | bytes 1880068
  122.7 8.3 %collective-permute-start.17 = (f32[2048,256]{1,0:T(8,128)S(1)}, f32[2048,256]{1,0:T(8,128)S(1)}, u32[]{:S(2)}, u32[]{:S(2)}) collective-permute-start(f32[2048,256]{1,0:T(8,128)S(1)} %get-tuple-element.75), channel_id=1, source_target_pairs={{0,64},{64,0},{1,65},{65,1},{2,66},{66,2},{3,67},{67,3},{4,68},{68... | collective-permute-start | bytes 6291464 | tf_op jit(solution)/shard_map/ppermute | solution.py:21
  123.9 7.1 %copy-start.1 = (bf16[2048,1152]{1,0:T(8,128)(2,1)S(1)}, bf16[2048,1152]{1,0:T(8,128)(2,1)}, u32[]{:S(2)}) copy-start(bf16[2048,1152]{1,0:T(8,128)(2,1)} %all-gather.2.cloned.1.call-done) | copy-start | bytes 14155780
  123.9 13.1 %collective-permute-start.18 = (f32[2048,256]{1,0:T(8,128)S(1)}, f32[2048,256]{1,0:T(8,128)S(1)}, u32[]{:S(2)}, u32[]{:S(2)}) collective-permute-start(f32[2048,256]{1,0:T(8,128)S(1)} %get-tuple-element.76), channel_id=1, source_target_pairs={{0,64},{64,0},{1,65},{65,1},{2,66},{66,2},{3,67},{67,3},{4,68},{68... | collective-permute-start | bytes 6291464 | tf_op jit(solution)/shard_map/ppermute | solution.py:21
  129.9 1.0 copy-start.5
  136.0 1.0 copy-start.24
  137.0 1.3 copy-start.8
  138.3 48.8 %all-to-all-start = ((bf16[16,32,1280]{2,1,0:T(8,128)(2,1)}), bf16[16,32,1280]{2,1,0:T(8,128)(2,1)}, u32[]{:S(2)}, u32[]{:S(2)}) async-start(bf16[16,32,1280]{2,1,0:T(8,128)(2,1)} %bitcast.43), calls=%async_computation | async-start | bytes 2621440 | tf_op jit(solution)/shard_map/all_to_all | solution.py:141
  148.1 38.0 %collective-permute-start.19 = (bf16[2176,256]{1,0:T(8,128)(2,1)}, bf16[2176,256]{1,0:T(8,128)(2,1)S(1)}, u32[]{:S(2)}, u32[]{:S(2)}) collective-permute-start(bf16[2176,256]{1,0:T(8,128)(2,1)} %copy-done.24), channel_id=1, source_target_pairs={{0,128},{128,0},{1,129},{129,1},{2,130},{130,2},{3,131},{131,3},{4... | collective-permute-start | bytes 3342344 | tf_op jit(solution)/shard_map/ppermute | solution.py:21
  148.2 2.3 %copy-start.2 = (bf16[2048,1152]{1,0:T(8,128)(2,1)S(1)}, bf16[2048,1152]{1,0:T(8,128)(2,1)}, u32[]{:S(2)}) copy-start(bf16[2048,1152]{1,0:T(8,128)(2,1)} %all-gather.2.cloned.1.call-done) | copy-start | bytes 14155780
  150.5 1.0 copy-start.7
  151.6 1.0 copy-start.11
  152.6 1.0 copy-start.13
  153.6 1.0 copy-start.15
  154.7 1.0 copy-start.17
  155.7 1.0 copy-start.19
  186.1 1.0 copy-start.25
  187.1 2.3 %copy-start.3 = (bf16[2048,1152]{1,0:T(8,128)(2,1)S(1)}, bf16[2048,1152]{1,0:T(8,128)(2,1)}, u32[]{:S(2)}) copy-start(bf16[2048,1152]{1,0:T(8,128)(2,1)} %all-gather.2.cloned.1.call-done) | copy-start | bytes 14155780
  189.4 1.6 copy-start.9
  191.0 1.2 copy-start.26
Sparse Core Ops, SparseCore 0:
  31.9 63.4 all-gather.1

commit v5 on v3

--- a/solution.py
+++ b/solution.py
@@ -283,19 +283,19 @@
     corner_v = flip(across_v, "core", 1)
     gv, *send_v = grad(u, (own_v, beside_v, across_v, corner_v), tokens)
     got_v = [flip(s, "y", bits) for s, bits in zip(send_v, (1, 2, 3))]
-    gk, gv, w, got_v[1], *got_k = hold(gk, gv, w, got_v[1], *got_k)
+    gk, gv, w, got_v[0], *got_k = hold(gk, gv, w, got_v[0], *got_k)
 
     both_cores = shape((2048, 256), F32)
     to_far, to_near = project(beside_kernel, [both_cores] * 2, tokens, w)
     got_far, got_near = flip(to_far, "core", 1), flip(to_near, "core", 1)
-    got_far, got_near, gk, gv, *got = hold(got_far, got_near, gk, gv, *got_k, *got_v)
-    total = spread(sum_over_y(gk, *got[:3], gv, *got[3:]))
     (far,) = project(far_kernel, [shape((2176, 256), BF16)], tokens, w, got_far)
     across = flip(far, "xl", 1)
+    total = sum_over_y(gk, *got_k, gv, *got_v)
     d_tokens = back(
         (own_k, beside_k, across_k, corner_k, own_v, beside_v, across_v, corner_v), w
     )
     total, across, d_tokens, got_near = hold(total, across, d_tokens, got_near)
+    total = spread(total)
     out_k, out_v = project(
         near_kernel, [shape((1024, 256), BF16)] * 2, tokens, w, got_near, across
     )

time: 217 us -> 214 us (0.986); the launches traced: 216 us -> 210 us
  local copies, waits for them, and re-layouts: 37 us -> 32.8 us
  starting transfers between devices: 35.5 us -> 33.2 us
    all_to_all x1, waiting for transfers between devices: 0.01 us -> 21 us  [spread(): lax.all_to_all(x.reshape(16, 32, 1280), ('z', 'xh'), 0, 0, tiled=True)]
    ppermute x20, waiting for transfers between devices: 90.6 us -> 70.4 us  [flip(): return lax.ppermute(x, axis, [(i, i ^ bits) for i in range(n)])]
    unnamed x86 -> x80, local copies, waits for them, and re-layouts: 25.7 us -> 21.4 us
  transfers between devices with their start and end apart: 22 -> 22, of which waited for: 8 -> 13; matrix products, arithmetic and copies ran while one was open for 2% -> 4% of each run, Pallas kernels for 10% -> 15%
where the time goes in v5:
time: 214 us; the launch traced here: 210 us
  waiting for transfers between devices  91.4 us (43%)
  Pallas kernels  38.5 us (18%)
  starting transfers between devices  33.2 us (16%)
  local copies, waits for them, and re-layouts  32.8 us (15%)
  between operations  14.5 us (7%)
    ppermute x20, waiting for transfers between devices, flip(): return lax.ppermute(x, axis, [(i, i ^ bits) for i in range(n)])  70.4 us
    ppermute x20, starting transfers between devices, flip(): return lax.ppermute(x, axis, [(i, i ^ bits) for i in range(n)])  24.7 us
    unnamed x80, local copies, waits for them, and re-layouts  21.4 us
    all_to_all x1, waiting for transfers between devices, spread(): lax.all_to_all(x.reshape(16, 32, 1280), ('z', 'xh'), 0, 0, tiled=True)  21 us
    pallas_call x3, Pallas kernels, project(): pl.pallas_call(kernel, out_shape=outs, in_specs=[VMEM] * len(args), out_s...  12.6 us
    pallas_call x2, Pallas kernels, grad(): pl.pallas_call(grad_kernel, out_shape=[shape((256, 1152), F32)] + [shape(...  8.67 us
    all_to_all x1, starting transfers between devices, spread(): lax.all_to_all(x.reshape(16, 32, 1280), ('z', 'xh'), 0, 0, tiled=True)  8.52 us
    pallas_call x1, Pallas kernels, back(): pl.pallas_call(back_kernel, out_shape=shape((1024, 1152), BF16), in_specs...  7.92 us
  transfers between devices with their start and end apart: 22, of which 13 were waited for; matrix products, arithmetic and copies ran while one was open for 4% of the time, Pallas kernels for 15%

profile of v5, /device:TPU:1, one launch (start us, length us, event | category | flops | bytes accessed | tf_op | source)
XLA Modules:
  0.0 210.4 jit_solution(6009514016975903767)
XLA Ops:
  7.2 3.7 %collective-permute-start = (bf16[2,16,1152]{2,1,0:T(8,128)(2,1)}, bf16[2,16,1152]{2,1,0:T(8,128)(2,1)S(1)}, u32[]{:S(2)}, u32[]{:S(2)}) collective-permute-start(bf16[2,16,1152]{2,1,0:T(8,128)(2,1)} %bitcast.57), channel_id=1, source_target_pairs={{0,1},{1,0},{2,3},{3,2},{4,5},{5,4},{6,7},{7,6},{8,9},{9,8},{10,11... | collective-permute-start | bytes 221192 | tf_op jit(solution)/shard_map/ppermute | solution.py:21
  10.9 0.9 bitcast_dynamic-update-slice_fusion.4
  11.8 3.3 %fusion = (bf16[1024,1,256]{2,1,0:T(2,128)(2,1)S(1)}, bf16[1024,1,256]{2,1,0:T(2,128)(2,1)S(1)}) fusion(bf16[1024,2,256]{2,1,0:T(2,128)(2,1)} %param.5), kind=kLoop, calls=%fused_computation.11 | loop fusion | bytes 2097152 | tf_op jit(solution)/shard_map/slice | solution.py:259
  15.3 0.8 fusion.1
  16.2 0.3 collective-permute-start.1
  16.5 1.3 collective-permute-start.2
  17.8 2.6 %collective-permute-start.3 = (bf16[2,32,1152]{2,1,0:T(8,128)(2,1)S(1)}, bf16[2,32,1152]{2,1,0:T(8,128)(2,1)}, u32[]{:S(2)}, u32[]{:S(2)}) collective-permute-start(bf16[2,32,1152]{2,1,0:T(8,128)(2,1)S(1)} %bitcast.53), channel_id=1, source_target_pairs={{0,32},{16,48},{32,0},{48,16},{1,33},{17,49},{33,1},{49,17},{2,34}... | collective-permute-start | bytes 442376 | tf_op jit(solution)/shard_map/ppermute | solution.py:21
  20.4 0.2 collective-permute-done.2
  20.6 5.4 %collective-permute-done.3 = bf16[2,32,1152]{2,1,0:T(8,128)(2,1)} collective-permute-done((bf16[2,32,1152]{2,1,0:T(8,128)(2,1)S(1)}, bf16[2,32,1152]{2,1,0:T(8,128)(2,1)}, u32[]{:S(2)}, u32[]{:S(2)}) %collective-permute-start.3) | collective-permute-done | bytes 147488 | tf_op jit(solution)/shard_map/ppermute | solution.py:21
  26.0 2.8 %collective-permute-done.4 = bf16[2,32,1152]{2,1,0:T(8,128)(2,1)} collective-permute-done((bf16[2,32,1152]{2,1,0:T(8,128)(2,1)S(1)}, bf16[2,32,1152]{2,1,0:T(8,128)(2,1)}, u32[]{:S(2)}, u32[]{:S(2)}) %collective-permute-start.4) | collective-permute-done | bytes 147488 | tf_op jit(solution)/shard_map/ppermute | solution.py:21
  28.8 0.9 broadcast_in_dim.29
  29.7 0.7 bitcast_dynamic-update-slice_fusion.3
  30.3 1.6 bitcast_dynamic-update-slice_fusion.2
  31.9 1.6 bitcast_dynamic-update-slice_fusion.1
  33.5 1.6 bitcast_dynamic-update-slice_fusion
  35.1 1.2 collective-permute-start.5
  36.3 2.0 collective-permute-start.7
  38.3 1.0 constant_dynamic-update-slice_fusion.1
  39.3 2.2 %collective-permute-done.5 = bf16[512,256]{1,0:T(8,128)(2,1)S(1)} collective-permute-done((bf16[512,256]{1,0:T(8,128)(2,1)}, bf16[512,256]{1,0:T(8,128)(2,1)S(1)}, u32[]{:S(2)}, u32[]{:S(2)}) %collective-permute-start.5) | collective-permute-done | bytes 262176 | tf_op jit(solution)/shard_map/ppermute | solution.py:21
  41.5 2.7 %collective-permute-start.8 = (bf16[1024,256]{1,0:T(8,128)(2,1)S(1)}, bf16[1024,256]{1,0:T(8,128)(2,1)S(1)}, u32[]{:S(2)}, u32[]{:S(2)}) collective-permute-start(bf16[1024,256]{1,0:T(8,128)(2,1)S(1)} %constant_dynamic-update-slice_fusion.p2.refs_2_), channel_id=1, source_target_pairs={{0,64},{64,0},{1,65},{65,1},{2,66},{66,2},{3,67},{67,3},{4,68},{68... | collective-permute-start | bytes 1572872 | tf_op jit(solution)/shard_map/ppermute | solution.py:21
  44.2 1.2 collective-permute-start.6
  45.4 0.4 collective-permute-start.9
  45.8 4.3 %grad.2 = (f32[256,1152]{1,0:T(8,128)S(1)}, bf16[272,1152]{1,0:T(8,128)(2,1)S(1)}, bf16[272,1152]{1,0:T(8,128)(2,1)S(1)}, bf16[272,1152]{1,0:T(8,128)(2,1)S(1)}) custom-call(s32[1]{0:T(128)} %bitcast.8.u_ref, bf16[1024,256]{1,0:T(8,128)(2,1)S(1)} %bitcast.43, bf16[1024,256]{1,0:T(8,128)(2,1)S(1)} %collective-permute-done.7.p1.refs_1_, ...), custom_call_target="tpu_custom_call" | custom-call | flops 1 | bytes 1 | tf_op jit(solution)/shard_map/grad/pallas_call | solution.py:81
  50.2 1.0 copy-done.18
  51.2 6.6 %collective-permute-done.6.p2.refs_6_ = bf16[1024,256]{1,0:T(8,128)(2,1)S(1)} collective-permute-done((bf16[1024,256]{1,0:T(8,128)(2,1)S(1)}, bf16[1024,256]{1,0:T(8,128)(2,1)S(1)}, u32[]{:S(2)}, u32[]{:S(2)}) %collective-permute-start.6) | collective-permute-done | bytes 524320 | tf_op jit(solution)/shard_map/ppermute | solution.py:21
  57.8 0.8 collective-permute-start.10
  58.6 1.9 collective-permute-start.13
  60.5 1.9 collective-permute-start.14
  62.5 4.3 %grad.3 = (f32[256,1152]{1,0:T(8,128)S(1)}, bf16[272,1152]{1,0:T(8,128)(2,1)S(1)}, bf16[272,1152]{1,0:T(8,128)(2,1)S(1)}, bf16[272,1152]{1,0:T(8,128)(2,1)S(1)}) custom-call(s32[1]{0:T(128)} %bitcast.8.u_ref, bf16[1024,256]{1,0:T(8,128)(2,1)S(1)} %bitcast.48, bf16[1024,256]{1,0:T(8,128)(2,1)S(1)} %collective-permute-done.9.p1.refs_5_, ...), custom_call_target="tpu_custom_call" | custom-call | flops 1 | bytes 1 | tf_op jit(solution)/shard_map/grad/pallas_call | solution.py:81
  66.9 1.1 copy-done.20
  68.0 0.8 copy-done.32
  68.8 0.8 copy-done.34
  69.6 4.8 %collective-permute-done.12.refs_1_ = bf16[272,1152]{1,0:T(8,128)(2,1)S(1)} collective-permute-done((bf16[272,1152]{1,0:T(8,128)(2,1)S(1)}, bf16[272,1152]{1,0:T(8,128)(2,1)S(1)}, u32[]{:S(2)}, u32[]{:S(2)}) %collective-permute-start.12) | collective-permute-done | bytes 626720 | tf_op jit(solution)/shard_map/ppermute | solution.py:21
  74.5 0.8 copy-done.24
  75.3 13.0 %collective-permute-done.13.refs_2_ = bf16[272,1152]{1,0:T(8,128)(2,1)S(1)} collective-permute-done((bf16[272,1152]{1,0:T(8,128)(2,1)S(1)}, bf16[272,1152]{1,0:T(8,128)(2,1)S(1)}, u32[]{:S(2)}, u32[]{:S(2)}) %collective-permute-start.13) | collective-permute-done | bytes 626720 | tf_op jit(solution)/shard_map/ppermute | solution.py:21
  88.3 0.9 copy-done.26
  89.2 1.2 collective-permute-done.14.refs_3_
  90.4 0.9 copy-done.28
  91.2 10.0 %collective-permute-done.11.refs_5_ = bf16[272,1152]{1,0:T(8,128)(2,1)S(1)} collective-permute-done((bf16[272,1152]{1,0:T(8,128)(2,1)S(1)}, bf16[272,1152]{1,0:T(8,128)(2,1)S(1)}, u32[]{:S(2)}, u32[]{:S(2)}) %collective-permute-start.11) | collective-permute-done | bytes 626720 | tf_op jit(solution)/shard_map/ppermute | solution.py:21
  101.3 0.8 copy-done.30
  102.1 2.3 %copy-done = bf16[2048,1152]{1,0:T(8,128)(2,1)S(1)} copy-done((bf16[2048,1152]{1,0:T(8,128)(2,1)S(1)}, bf16[2048,1152]{1,0:T(8,128)(2,1)}, u32[]{:S(2)}) %copy-start) | copy-done | bytes 4718616
  104.4 4.3 %beside_kernel.1 = (f32[2048,256]{1,0:T(8,128)S(1)}, f32[2048,256]{1,0:T(8,128)S(1)}) custom-call(bf16[1024,1152]{1,0:T(8,128)(2,1)S(1)} %copy-done.2, bf16[8,4,2,32,1152]{4,3,2,1,0:T(8,128)(2,1)S(1)} %bitcast.35), custom_call_target="tpu_custom_call" | custom-call | flops 1 | bytes 1 | tf_op jit(solution)/shard_map/beside_kernel/pallas_call | solution.py:218
  108.7 0.9 collective-permute-start.17
  109.7 0.1 collective-permute-start.19
  109.8 3.6 %collective-permute-done.17.got = f32[2048,256]{1,0:T(8,128)S(1)} collective-permute-done((f32[2048,256]{1,0:T(8,128)S(1)}, f32[2048,256]{1,0:T(8,128)S(1)}, u32[]{:S(2)}, u32[]{:S(2)}) %collective-permute-start.17) | collective-permute-done | bytes 2097184 | tf_op jit(solution)/shard_map/ppermute | solution.py:21
  113.4 5.0 %far_kernel.1 = bf16[2176,256]{1,0:T(8,128)(2,1)S(1)} custom-call(bf16[1024,1152]{1,0:T(8,128)(2,1)S(1)} %copy-done.2, bf16[8,4,2,32,1152]{4,3,2,1,0:T(8,128)(2,1)S(1)} %bitcast.36, f32[2048,256]{1,0:T(8,128)S(1)} %collective-permute-done.17.got), custom_call_target="tpu_custom_call" | custom-call | flops 1 | bytes 1 | tf_op jit(solution)/shard_map/far_kernel/pallas_call | solution.py:218
  118.4 1.2 collective-permute-start.18
  119.6 0.2 collective-permute-start.15
  119.8 2.3 %collective-permute-start.16 = (bf16[272,1152]{1,0:T(8,128)(2,1)S(1)}, bf16[272,1152]{1,0:T(8,128)(2,1)S(1)}, u32[]{:S(2)}, u32[]{:S(2)}) collective-permute-start(bf16[272,1152]{1,0:T(8,128)(2,1)S(1)} %copy-done.33), channel_id=1, source_target_pairs={{0,48},{16,32},{32,16},{48,0},{1,49},{17,33},{33,17},{49,1},{2,50}... | collective-permute-start | bytes 1880072 | tf_op jit(solution)/shard_map/ppermute | solution.py:21
  122.2 7.9 %back.1 = bf16[1024,1152]{1,0:T(8,128)(2,1)} custom-call(bf16[1024,256]{1,0:T(8,128)(2,1)S(1)} %bitcast.44, bf16[1024,256]{1,0:T(8,128)(2,1)S(1)} %copy-done.9, bf16[1024,256]{1,0:T(8,128)(2,1)S(1)} %copy-done.5, bf16[1024,256]{1,0:T(8,128)(2,1)S(1)} %copy-done.11, bf16[1024,256]{1,0:T(8,128)(2,1)S(1)} %bitcast.49, bf16[1024,256]{1,0:T(8,128)(2,1)S(1)} %copy-done.15, ...), custom_call_target="tpu_custom_call" | custom-call | flops 1 | bytes 1 | tf_op jit(solution)/shard_map/back/pallas_call | solution.py:243
  130.1 6.0 %collective-permute-done.15.refs_6_ = bf16[272,1152]{1,0:T(8,128)(2,1)S(1)} collective-permute-done((bf16[272,1152]{1,0:T(8,128)(2,1)S(1)}, bf16[272,1152]{1,0:T(8,128)(2,1)S(1)}, u32[]{:S(2)}, u32[]{:S(2)}) %collective-permute-start.15) | collective-permute-done | bytes 626720 | tf_op jit(solution)/shard_map/ppermute | solution.py:21
  136.2 14.4 %collective-permute-done.16.refs_7_ = bf16[272,1152]{1,0:T(8,128)(2,1)S(1)} collective-permute-done((bf16[272,1152]{1,0:T(8,128)(2,1)S(1)}, bf16[272,1152]{1,0:T(8,128)(2,1)S(1)}, u32[]{:S(2)}, u32[]{:S(2)}) %collective-permute-start.16) | collective-permute-done | bytes 626720 | tf_op jit(solution)/shard_map/ppermute | solution.py:21
  150.6 5.9 %sum_over_y.1 = bf16[512,1280]{1,0:T(8,128)(2,1)S(1)} custom-call(f32[256,1152]{1,0:T(8,128)S(1)} %copy-done.19, bf16[272,1152]{1,0:T(8,128)(2,1)S(1)} %copy-done.25, bf16[272,1152]{1,0:T(8,128)(2,1)S(1)} %copy-done.27, bf16[272,1152]{1,0:T(8,128)(2,1)S(1)} %copy-done.29, f32[256,1152]{1,0:T(8,128)S(1)} %copy-done.21, bf16[272,1152]{1,0:T(8,128)(2,1)S(1)} %copy-done.31, ...), custom_call_target="tpu_custom_call" | custom-call | flops 1 | bytes 1 | tf_op jit(solution)/shard_map/sum_over_y/pallas_call | solution.py:119
  156.5 1.1 copy-done.3
  157.6 1.4 copy-done.6
  159.0 1.0 copy-done.22
  160.0 8.5 %all-to-all-start = ((bf16[16,32,1280]{2,1,0:T(8,128)(2,1)}), bf16[16,32,1280]{2,1,0:T(8,128)(2,1)}, u32[]{:S(2)}, u32[]{:S(2)}) async-start(bf16[16,32,1280]{2,1,0:T(8,128)(2,1)} %bitcast.45), calls=%async_computation | async-start | bytes 2621440 | tf_op jit(solution)/shard_map/all_to_all | solution.py:141
  168.5 2.3 %copy-done.1 = bf16[2048,1152]{1,0:T(8,128)(2,1)S(1)} copy-done((bf16[2048,1152]{1,0:T(8,128)(2,1)S(1)}, bf16[2048,1152]{1,0:T(8,128)(2,1)}, u32[]{:S(2)}) %copy-start.1) | copy-done | bytes 4718616
  170.8 1.6 copy-done.7
  172.4 1.2 copy-done.23
  173.7 3.3 %near_kernel.1 = (bf16[1024,256]{1,0:T(8,128)(2,1)S(1)}, bf16[1024,256]{1,0:T(8,128)(2,1)S(1)}) custom-call(bf16[1024,1152]{1,0:T(8,128)(2,1)S(1)} %copy-done.2, bf16[8,4,2,32,1152]{4,3,2,1,0:T(8,128)(2,1)S(1)} %bitcast.40, f32[2048,256]{1,0:T(8,128)S(1)} %copy-done.7, bf16[2176,256]{1,0:T(8,128)(2,1)S(1)} %copy-done.23), custom_call_target="tpu_custom_call" | custom-call | flops 1 | bytes 1 | tf_op jit(solution)/shard_map/near_kernel/pallas_call | solution.py:218
  177.1 2.0 copy.12
  179.1 21.0 %all-to-all-done = bf16[16,32,1280]{2,1,0:T(8,128)(2,1)} async-done(((bf16[16,32,1280]{2,1,0:T(8,128)(2,1)}), bf16[16,32,1280]{2,1,0:T(8,128)(2,1)}, u32[]{:S(2)}, u32[]{:S(2)}) %all-to-all-start) | async-done | bytes 1310752 | tf_op jit(solution)/shard_map/all_to_all | solution.py:141
  200.1 3.5 %sum_over_z.1 = f32[32,1152]{1,0:T(8,128)} custom-call(bf16[512,1280]{1,0:T(8,128)(2,1)} %bitcast.18.x), custom_call_target="tpu_custom_call" | custom-call | flops 1 | bytes 1 | tf_op jit(solution)/shard_map/sum_over_z/pallas_call | solution.py:145
  (82 shorter events, 0.5 us)
Async XLA Ops:
  7.2 94.9 %all-gather.2.cloned.1.call-start = ((), (), s32[]{:S(2)}) async-start(), calls=%async_computation.1 | async-start | bytes 5308416 | tf_op jit(solution)/shard_map/all_gather | solution.py:274
  7.2 8.1 %collective-permute-start = (bf16[2,16,1152]{2,1,0:T(8,128)(2,1)}, bf16[2,16,1152]{2,1,0:T(8,128)(2,1)S(1)}, u32[]{:S(2)}, u32[]{:S(2)}) collective-permute-start(bf16[2,16,1152]{2,1,0:T(8,128)(2,1)} %bitcast.57), channel_id=1, source_target_pairs={{0,1},{1,0},{2,3},{3,2},{4,5},{5,4},{6,7},{7,6},{8,9},{9,8},{10,11... | collective-permute-start | bytes 221192 | tf_op jit(solution)/shard_map/ppermute | solution.py:21
  15.3 30.5 %copy-start.2 = (bf16[1024,1152]{1,0:T(8,128)(2,1)S(1)}, bf16[1024,1152]{1,0:T(8,128)(2,1)}, u32[]{:S(2)}) copy-start(bf16[1024,1152]{1,0:T(8,128)(2,1)} %tok.9) | copy-start | bytes 7077892
  16.2 12.6 %collective-permute-start.1 = (bf16[512,256]{1,0:T(8,128)(2,1)}, bf16[512,256]{1,0:T(8,128)(2,1)}, u32[]{:S(2)}, u32[]{:S(2)}) collective-permute-start(bf16[512,256]{1,0:T(8,128)(2,1)} %get-tuple-element.84), channel_id=1, source_target_pairs={{0,128},{128,0},{1,129},{129,1},{2,130},{130,2},{3,131},{131,3},{4... | collective-permute-start | bytes 786440 | tf_op jit(solution)/shard_map/ppermute | solution.py:21
  16.5 4.1 %collective-permute-start.2 = (bf16[2,32,1152]{2,1,0:T(8,128)(2,1)S(1)}, bf16[2,32,1152]{2,1,0:T(8,128)(2,1)}, u32[]{:S(2)}, u32[]{:S(2)}) collective-permute-start(bf16[2,32,1152]{2,1,0:T(8,128)(2,1)S(1)} %bitcast.52), channel_id=1, source_target_pairs={{0,16},{16,0},{32,48},{48,32},{1,17},{17,1},{33,49},{49,33},{2,18}... | collective-permute-start | bytes 442376 | tf_op jit(solution)/shard_map/ppermute | solution.py:21
  17.8 8.2 %collective-permute-start.3 = (bf16[2,32,1152]{2,1,0:T(8,128)(2,1)S(1)}, bf16[2,32,1152]{2,1,0:T(8,128)(2,1)}, u32[]{:S(2)}, u32[]{:S(2)}) collective-permute-start(bf16[2,32,1152]{2,1,0:T(8,128)(2,1)S(1)} %bitcast.53), channel_id=1, source_target_pairs={{0,32},{16,48},{32,0},{48,16},{1,33},{17,49},{33,1},{49,17},{2,34}... | collective-permute-start | bytes 442376 | tf_op jit(solution)/shard_map/ppermute | solution.py:21
  20.4 8.4 %collective-permute-start.4 = (bf16[2,32,1152]{2,1,0:T(8,128)(2,1)S(1)}, bf16[2,32,1152]{2,1,0:T(8,128)(2,1)}, u32[]{:S(2)}, u32[]{:S(2)}) collective-permute-start(bf16[2,32,1152]{2,1,0:T(8,128)(2,1)S(1)} %bitcast.54), channel_id=1, source_target_pairs={{0,48},{16,32},{32,16},{48,0},{1,49},{17,33},{33,17},{49,1},{2,50}... | collective-permute-start | bytes 442376 | tf_op jit(solution)/shard_map/ppermute | solution.py:21
  35.1 6.4 %collective-permute-start.5 = (bf16[512,256]{1,0:T(8,128)(2,1)}, bf16[512,256]{1,0:T(8,128)(2,1)S(1)}, u32[]{:S(2)}, u32[]{:S(2)}) collective-permute-start(bf16[512,256]{1,0:T(8,128)(2,1)} %get-tuple-element.41), channel_id=1, source_target_pairs={{0,128},{128,0},{1,129},{129,1},{2,130},{130,2},{3,131},{131,3},{4... | collective-permute-start | bytes 786440 | tf_op jit(solution)/shard_map/ppermute | solution.py:21
  36.3 9.4 %collective-permute-start.7 = (bf16[1024,256]{1,0:T(8,128)(2,1)S(1)}, bf16[1024,256]{1,0:T(8,128)(2,1)S(1)}, u32[]{:S(2)}, u32[]{:S(2)}) collective-permute-start(bf16[1024,256]{1,0:T(8,128)(2,1)S(1)} %bitcast.42), channel_id=1, source_target_pairs={{0,64},{64,0},{1,65},{65,1},{2,66},{66,2},{3,67},{67,3},{4,68},{68... | collective-permute-start | bytes 1572872 | tf_op jit(solution)/shard_map/ppermute | solution.py:21
  41.5 8.6 %copy-start.4 = (bf16[1024,256]{1,0:T(8,128)(2,1)}, bf16[1024,256]{1,0:T(8,128)(2,1)S(1)}, u32[]{:S(2)}) copy-start(bf16[1024,256]{1,0:T(8,128)(2,1)S(1)} %constant_dynamic-update-slice_fusion.p2.refs_2_) | copy-start | bytes 1572868
  41.5 4.2 %collective-permute-start.8 = (bf16[1024,256]{1,0:T(8,128)(2,1)S(1)}, bf16[1024,256]{1,0:T(8,128)(2,1)S(1)}, u32[]{:S(2)}, u32[]{:S(2)}) collective-permute-start(bf16[1024,256]{1,0:T(8,128)(2,1)S(1)} %constant_dynamic-update-slice_fusion.p2.refs_2_), channel_id=1, source_target_pairs={{0,64},{64,0},{1,65},{65,1},{2,66},{66,2},{3,67},{67,3},{4,68},{68... | collective-permute-start | bytes 1572872 | tf_op jit(solution)/shard_map/ppermute | solution.py:21
  44.2 13.6 %collective-permute-start.6 = (bf16[1024,256]{1,0:T(8,128)(2,1)S(1)}, bf16[1024,256]{1,0:T(8,128)(2,1)S(1)}, u32[]{:S(2)}, u32[]{:S(2)}) collective-permute-start(bf16[1024,256]{1,0:T(8,128)(2,1)S(1)} %bitcast.46), channel_id=1, source_target_pairs={{0,128},{128,0},{1,129},{129,1},{2,130},{130,2},{3,131},{131,3},{4... | collective-permute-start | bytes 1572872 | tf_op jit(solution)/shard_map/ppermute | solution.py:21
  45.4 17.1 %collective-permute-start.9 = (bf16[1024,256]{1,0:T(8,128)(2,1)S(1)}, bf16[1024,256]{1,0:T(8,128)(2,1)S(1)}, u32[]{:S(2)}, u32[]{:S(2)}) collective-permute-start(bf16[1024,256]{1,0:T(8,128)(2,1)S(1)} %bitcast.47), channel_id=1, source_target_pairs={{0,64},{64,0},{1,65},{65,1},{2,66},{66,2},{3,67},{67,3},{4,68},{68... | collective-permute-start | bytes 1572872 | tf_op jit(solution)/shard_map/ppermute | solution.py:21
  45.8 4.4 %copy-start.8 = (bf16[1024,256]{1,0:T(8,128)(2,1)}, bf16[1024,256]{1,0:T(8,128)(2,1)S(1)}, u32[]{:S(2)}) copy-start(bf16[1024,256]{1,0:T(8,128)(2,1)S(1)} %collective-permute-done.7.p1.refs_1_) | copy-start | bytes 1572868
  45.8 4.4 %copy-start.10 = (bf16[1024,256]{1,0:T(8,128)(2,1)}, bf16[1024,256]{1,0:T(8,128)(2,1)S(1)}, u32[]{:S(2)}) copy-start(bf16[1024,256]{1,0:T(8,128)(2,1)S(1)} %collective-permute-done.8.p3.refs_3_) | copy-start | bytes 1572868
  50.2 1.0 copy-start.18
  57.8 9.0 %copy-start.12 = (bf16[1024,256]{1,0:T(8,128)(2,1)}, bf16[1024,256]{1,0:T(8,128)(2,1)S(1)}, u32[]{:S(2)}) copy-start(bf16[1024,256]{1,0:T(8,128)(2,1)S(1)} %collective-permute-done.6.p2.refs_6_) | copy-start | bytes 1572868
  57.8 4.6 %collective-permute-start.10 = (bf16[1024,256]{1,0:T(8,128)(2,1)S(1)}, bf16[1024,256]{1,0:T(8,128)(2,1)S(1)}, u32[]{:S(2)}, u32[]{:S(2)}) collective-permute-start(bf16[1024,256]{1,0:T(8,128)(2,1)S(1)} %collective-permute-done.6.p2.refs_6_), channel_id=1, source_target_pairs={{0,64},{64,0},{1,65},{65,1},{2,66},{66,2},{3,67},{67,3},{4,68},{68... | collective-permute-start | bytes 1572872 | tf_op jit(solution)/shard_map/ppermute | solution.py:21
  58.6 15.9 %collective-permute-start.12 = (bf16[272,1152]{1,0:T(8,128)(2,1)S(1)}, bf16[272,1152]{1,0:T(8,128)(2,1)S(1)}, u32[]{:S(2)}, u32[]{:S(2)}) collective-permute-start(bf16[272,1152]{1,0:T(8,128)(2,1)S(1)} %get-tuple-element.55), channel_id=1, source_target_pairs={{0,16},{16,0},{32,48},{48,32},{1,17},{17,1},{33,49},{49,33},{2,18}... | collective-permute-start | bytes 1880072 | tf_op jit(solution)/shard_map/ppermute | solution.py:21
  58.6 29.7 %collective-permute-start.13 = (bf16[272,1152]{1,0:T(8,128)(2,1)S(1)}, bf16[272,1152]{1,0:T(8,128)(2,1)S(1)}, u32[]{:S(2)}, u32[]{:S(2)}) collective-permute-start(bf16[272,1152]{1,0:T(8,128)(2,1)S(1)} %get-tuple-element.56), channel_id=1, source_target_pairs={{0,32},{16,48},{32,0},{48,16},{1,33},{17,49},{33,1},{49,17},{2,34}... | collective-permute-start | bytes 1880072 | tf_op jit(solution)/shard_map/ppermute | solution.py:21
  60.5 29.9 %collective-permute-start.14 = (bf16[272,1152]{1,0:T(8,128)(2,1)S(1)}, bf16[272,1152]{1,0:T(8,128)(2,1)S(1)}, u32[]{:S(2)}, u32[]{:S(2)}) collective-permute-start(bf16[272,1152]{1,0:T(8,128)(2,1)S(1)} %get-tuple-element.57), channel_id=1, source_target_pairs={{0,48},{16,32},{32,16},{48,0},{1,49},{17,33},{33,17},{49,1},{2,50}... | collective-permute-start | bytes 1880072 | tf_op jit(solution)/shard_map/ppermute | solution.py:21
  62.5 4.4 %copy-start.14 = (bf16[1024,256]{1,0:T(8,128)(2,1)}, bf16[1024,256]{1,0:T(8,128)(2,1)S(1)}, u32[]{:S(2)}) copy-start(bf16[1024,256]{1,0:T(8,128)(2,1)S(1)} %collective-permute-done.9.p1.refs_5_) | copy-start | bytes 1572868
  62.5 4.4 %copy-start.16 = (bf16[1024,256]{1,0:T(8,128)(2,1)}, bf16[1024,256]{1,0:T(8,128)(2,1)S(1)}, u32[]{:S(2)}) copy-start(bf16[1024,256]{1,0:T(8,128)(2,1)S(1)} %collective-permute-done.10.p3.refs_7_) | copy-start | bytes 1572868
  66.8 1.1 copy-start.20
  68.0 0.8 copy-start.32
  68.8 0.8 copy-start.34
  69.6 31.6 %collective-permute-start.11 = (bf16[272,1152]{1,0:T(8,128)(2,1)S(1)}, bf16[272,1152]{1,0:T(8,128)(2,1)S(1)}, u32[]{:S(2)}, u32[]{:S(2)}) collective-permute-start(bf16[272,1152]{1,0:T(8,128)(2,1)S(1)} %get-tuple-element.54), channel_id=1, source_target_pairs={{0,16},{16,0},{32,48},{48,32},{1,17},{17,1},{33,49},{49,33},{2,18}... | collective-permute-start | bytes 1880072 | tf_op jit(solution)/shard_map/ppermute | solution.py:21
  74.5 0.8 copy-start.24
  88.3 0.9 copy-start.26
  90.4 0.9 copy-start.28
  101.2 0.8 copy-start.30
  102.1 2.3 %copy-start = (bf16[2048,1152]{1,0:T(8,128)(2,1)S(1)}, bf16[2048,1152]{1,0:T(8,128)(2,1)}, u32[]{:S(2)}) copy-start(bf16[2048,1152]{1,0:T(8,128)(2,1)} %all-gather.2.cloned.1.call-done) | copy-start | bytes 14155780
  108.7 4.6 %collective-permute-start.17 = (f32[2048,256]{1,0:T(8,128)S(1)}, f32[2048,256]{1,0:T(8,128)S(1)}, u32[]{:S(2)}, u32[]{:S(2)}) collective-permute-start(f32[2048,256]{1,0:T(8,128)S(1)} %get-tuple-element.67), channel_id=1, source_target_pairs={{0,64},{64,0},{1,65},{65,1},{2,66},{66,2},{3,67},{67,3},{4,68},{68... | collective-permute-start | bytes 6291464 | tf_op jit(solution)/shard_map/ppermute | solution.py:21
  109.6 12.5 %slice-start = ((s8[4718592]{0:T(1024)(128)(4,1)}), s8[4194304]{0:T(1024)(128)(4,1)S(1)}, s32[]{:S(2)}) async-start(s8[4718592]{0:T(1024)(128)(4,1)} %bitcast.37), calls=%async_computation.2 | async-start | bytes 8388608
  109.6 10.0 %copy-start.35 = (bf16[272,1152]{1,0:T(8,128)(2,1)S(1)}, bf16[272,1152]{1,0:T(8,128)(2,1)}, u32[]{:S(2)}) copy-start(bf16[272,1152]{1,0:T(8,128)(2,1)} %copy-done.34) | copy-start | bytes 1880068
  109.6 10.2 %copy-start.33 = (bf16[272,1152]{1,0:T(8,128)(2,1)S(1)}, bf16[272,1152]{1,0:T(8,128)(2,1)}, u32[]{:S(2)}) copy-start(bf16[272,1152]{1,0:T(8,128)(2,1)} %copy-done.32) | copy-start | bytes 1880068
  109.6 12.5 %slice-start.1 = ((s8[4718592]{0:T(1024)(128)(4,1)}), s8[524288]{0:T(1024)(128)(4,1)S(1)}, s32[]{:S(2)}) async-start(s8[4718592]{0:T(1024)(128)(4,1)} %bitcast.37), calls=%async_computation.3 | async-start | bytes 1048576
  109.6 12.5 %copy-start.5 = (bf16[1024,256]{1,0:T(8,128)(2,1)S(1)}, bf16[1024,256]{1,0:T(8,128)(2,1)}, u32[]{:S(2)}) copy-start(bf16[1024,256]{1,0:T(8,128)(2,1)} %copy-done.4) | copy-start | bytes 1572868
  109.6 12.5 %copy-start.9 = (bf16[1024,256]{1,0:T(8,128)(2,1)S(1)}, bf16[1024,256]{1,0:T(8,128)(2,1)}, u32[]{:S(2)}) copy-start(bf16[1024,256]{1,0:T(8,128)(2,1)} %copy-done.8) | copy-start | bytes 1572868
  109.6 12.5 %copy-start.11 = (bf16[1024,256]{1,0:T(8,128)(2,1)S(1)}, bf16[1024,256]{1,0:T(8,128)(2,1)}, u32[]{:S(2)}) copy-start(bf16[1024,256]{1,0:T(8,128)(2,1)} %copy-done.10) | copy-start | bytes 1572868
  109.6 12.5 %copy-start.13 = (bf16[1024,256]{1,0:T(8,128)(2,1)S(1)}, bf16[1024,256]{1,0:T(8,128)(2,1)}, u32[]{:S(2)}) copy-start(bf16[1024,256]{1,0:T(8,128)(2,1)} %copy-done.12) | copy-start | bytes 1572868
  109.6 12.5 %copy-start.15 = (bf16[1024,256]{1,0:T(8,128)(2,1)S(1)}, bf16[1024,256]{1,0:T(8,128)(2,1)}, u32[]{:S(2)}) copy-start(bf16[1024,256]{1,0:T(8,128)(2,1)} %copy-done.14) | copy-start | bytes 1572868
  109.7 12.5 %copy-start.17 = (bf16[1024,256]{1,0:T(8,128)(2,1)S(1)}, bf16[1024,256]{1,0:T(8,128)(2,1)}, u32[]{:S(2)}) copy-start(bf16[1024,256]{1,0:T(8,128)(2,1)} %copy-done.16) | copy-start | bytes 1572868
  109.7 47.9 %collective-permute-start.19 = (f32[2048,256]{1,0:T(8,128)S(1)}, f32[2048,256]{1,0:T(8,128)S(1)}, u32[]{:S(2)}, u32[]{:S(2)}) collective-permute-start(f32[2048,256]{1,0:T(8,128)S(1)} %get-tuple-element.68), channel_id=1, source_target_pairs={{0,64},{64,0},{1,65},{65,1},{2,66},{66,2},{3,67},{67,3},{4,68},{68... | collective-permute-start | bytes 6291464 | tf_op jit(solution)/shard_map/ppermute | solution.py:21
  118.4 40.6 %collective-permute-start.18 = (bf16[2176,256]{1,0:T(8,128)(2,1)S(1)}, bf16[2176,256]{1,0:T(8,128)(2,1)S(1)}, u32[]{:S(2)}, u32[]{:S(2)}) collective-permute-start(bf16[2176,256]{1,0:T(8,128)(2,1)S(1)} %far_kernel.1), channel_id=1, source_target_pairs={{0,128},{128,0},{1,129},{129,1},{2,130},{130,2},{3,131},{131,3},{4... | collective-permute-start | bytes 3342344 | tf_op jit(solution)/shard_map/ppermute | solution.py:21
  119.6 16.6 %collective-permute-start.15 = (bf16[272,1152]{1,0:T(8,128)(2,1)S(1)}, bf16[272,1152]{1,0:T(8,128)(2,1)S(1)}, u32[]{:S(2)}, u32[]{:S(2)}) collective-permute-start(bf16[272,1152]{1,0:T(8,128)(2,1)S(1)} %copy-done.35), channel_id=1, source_target_pairs={{0,32},{16,48},{32,0},{48,16},{1,33},{17,49},{33,1},{49,17},{2,34}... | collective-permute-start | bytes 1880072 | tf_op jit(solution)/shard_map/ppermute | solution.py:21
  119.8 30.8 %copy-start.19 = (f32[256,1152]{1,0:T(8,128)S(1)}, f32[256,1152]{1,0:T(8,128)}, u32[]{:S(2)}) copy-start(f32[256,1152]{1,0:T(8,128)} %copy-done.18) | copy-start | bytes 3538948
  119.8 30.8 %copy-start.21 = (f32[256,1152]{1,0:T(8,128)S(1)}, f32[256,1152]{1,0:T(8,128)}, u32[]{:S(2)}) copy-start(f32[256,1152]{1,0:T(8,128)} %copy-done.20) | copy-start | bytes 3538948
  119.8 30.8 %copy-start.25 = (bf16[272,1152]{1,0:T(8,128)(2,1)S(1)}, bf16[272,1152]{1,0:T(8,128)(2,1)}, u32[]{:S(2)}) copy-start(bf16[272,1152]{1,0:T(8,128)(2,1)} %copy-done.24) | copy-start | bytes 1880068
  119.8 30.8 %copy-start.27 = (bf16[272,1152]{1,0:T(8,128)(2,1)S(1)}, bf16[272,1152]{1,0:T(8,128)(2,1)}, u32[]{:S(2)}) copy-start(bf16[272,1152]{1,0:T(8,128)(2,1)} %copy-done.26) | copy-start | bytes 1880068
  119.8 30.8 %copy-start.29 = (bf16[272,1152]{1,0:T(8,128)(2,1)S(1)}, bf16[272,1152]{1,0:T(8,128)(2,1)}, u32[]{:S(2)}) copy-start(bf16[272,1152]{1,0:T(8,128)(2,1)} %copy-done.28) | copy-start | bytes 1880068
  119.8 30.8 %copy-start.31 = (bf16[272,1152]{1,0:T(8,128)(2,1)S(1)}, bf16[272,1152]{1,0:T(8,128)(2,1)}, u32[]{:S(2)}) copy-start(bf16[272,1152]{1,0:T(8,128)(2,1)} %copy-done.30) | copy-start | bytes 1880068
  119.8 30.7 %collective-permute-start.16 = (bf16[272,1152]{1,0:T(8,128)(2,1)S(1)}, bf16[272,1152]{1,0:T(8,128)(2,1)S(1)}, u32[]{:S(2)}, u32[]{:S(2)}) collective-permute-start(bf16[272,1152]{1,0:T(8,128)(2,1)S(1)} %copy-done.33), channel_id=1, source_target_pairs={{0,48},{16,32},{32,16},{48,0},{1,49},{17,33},{33,17},{49,1},{2,50}... | collective-permute-start | bytes 1880072 | tf_op jit(solution)/shard_map/ppermute | solution.py:21
  156.5 1.1 copy-start.3
  157.6 1.4 copy-start.6
  159.0 1.0 copy-start.22
  160.0 40.2 %all-to-all-start = ((bf16[16,32,1280]{2,1,0:T(8,128)(2,1)}), bf16[16,32,1280]{2,1,0:T(8,128)(2,1)}, u32[]{:S(2)}, u32[]{:S(2)}) async-start(bf16[16,32,1280]{2,1,0:T(8,128)(2,1)} %bitcast.45), calls=%async_computation | async-start | bytes 2621440 | tf_op jit(solution)/shard_map/all_to_all | solution.py:141
  168.5 2.3 %copy-start.1 = (bf16[2048,1152]{1,0:T(8,128)(2,1)S(1)}, bf16[2048,1152]{1,0:T(8,128)(2,1)}, u32[]{:S(2)}) copy-start(bf16[2048,1152]{1,0:T(8,128)(2,1)} %all-gather.2.cloned.1.call-done) | copy-start | bytes 14155780
  170.8 1.6 copy-start.7
  172.4 1.2 copy-start.23
Sparse Core Ops, SparseCore 0:
  35.2 60.1 all-gather.1
